TPU v7x, 512 devices: a whole 4x8x8 slice. The times are simulated.
512 devices in a mesh: ctx: 32 (over y, z_hi), head: 16 (over x, z_lo, core).
Axes of the slice: x: 4, y: 8, z: 8 (z_hi: 4, z_lo: 2; z = z_hi * 2 + z_lo), core: 2. Of those that a mesh axis runs over, the one named last changes fastest.
Arguments:
- x_in: bfloat16 [8192, 4096], P(('ctx', 'head')), may hold values from -6 to 6
- b_in: bfloat16 [8192, 1024], P(('ctx', 'head')), may hold values from -6 to 6
- c_in: bfloat16 [8192, 1024], P(('ctx', 'head')), may hold values from -6 to 6
- dt_in: bfloat16 [8192, 64], P(('ctx', 'head')), may hold values from -2.5 to 2.5
- gate_in: bfloat16 [8192, 4096], P(('ctx', 'head')), may hold values from -6 to 6
- out_grad: bfloat16 [8192, 4096], P(('ctx', 'head')), may hold values from -6 to 6
- conv_x: float32 [4, 4096], P(None, 'head'), may hold values from -3 to 3
- conv_b: float32 [4, 1024], replicated, may hold values from -3 to 3
- conv_c: float32 [4, 1024], replicated, may hold values from -3 to 3
- a_log: float32 [64], P('head'), may hold values from -12 to -3
- dt_bias: float32 [64], P('head'), may hold values from -0.5 to 0.5
- d_skip: float32 [64], P('head'), may hold values from 0.5 to 1.5
- norm_gain: float32 [4096], replicated, may hold values from 0.5 to 1.5
Outputs:
- x_grad: bfloat16 [8192, 4096], P(('ctx', 'head'))
- b_grad: bfloat16 [8192, 1024], P(('ctx', 'head'))
- c_grad: bfloat16 [8192, 1024], P(('ctx', 'head'))
- dt_grad: bfloat16 [8192, 64], P(('ctx', 'head'))
- gate_grad: bfloat16 [8192, 4096], P(('ctx', 'head'))
- conv_x_grad: float32 [4, 4096], P(None, 'head')
- conv_b_grad: float32 [4, 1024], replicated
- conv_c_grad: float32 [4, 1024], replicated
- a_log_grad: float32 [64], P('head')
- dt_bias_grad: float32 [64], P('head')
- d_skip_grad: float32 [64], P('head')
- gain_grad: float32 [4096], replicated
All inputs are finite; a program needn't handle non-finite values.
Results may differ from a plain program's by a relative error of at most 0.015.
The roundings to bfloat16 on the way count: a program that leaves them out, or rounds other values in their place, can miss the bound.
Values may be sent and summed in bfloat16 or wider, within the bound.
No kernel may reach another device: no remote copies, remote signals or barrier semaphores. Data moves between devices by JAX's collectives and lax.ppermute only.
A program may use at most 64 MiB of HBM per device.

v0:
```python
import jax
import jax.numpy as jnp
import numpy as np
from jax import lax
from jax.sharding import PartitionSpec as P

N = 128
G = 8
CH = 256


PRECISE = lax.Precision.HIGHEST


def shifted(value, axis, steps):
    count = lax.axis_size(axis)
    leading, last = (max(0, -steps), min(count, count - steps))
    return lax.ppermute(value, axis, [(source, source + steps) for source in range(leading, last)])


def entering(value, axis, join, neutral, backward):
    count, mine = (lax.axis_size(axis), lax.axis_index(axis))
    pieces = jax.tree.map(lambda part: lax.all_gather(part, axis), value)
    if backward:
        pieces = jax.tree.map(lambda part: part[::-1], pieces)
        mine = count - 1 - mine
    running = jax.tree.map(
        lambda part, zero: jnp.full_like(part, 0) + jnp.asarray(zero, part.dtype), value, neutral
    )

    def step(position, running):
        longer = join(running, jax.tree.map(lambda part: part[position], pieces))
        return jax.tree.map(lambda new, old: jnp.where(position < mine, new, old), longer, running)

    return lax.fori_loop(0, count - 1, step, running)


def causal_taps(padded, weight):
    row_count = padded.shape[0] - weight.shape[0] + 1
    summed = weight[0] * padded[0:row_count]
    for tap_index in range(1, weight.shape[0]):
        summed = summed + weight[tap_index] * padded[tap_index : tap_index + row_count]
    return summed


def stored(array_in):
    return lax.optimization_barrier(array_in.astype(jnp.bfloat16)).astype(jnp.float32)


def rates_of(dt_raw, dt_bias, a_log):
    stepsize = jax.nn.softplus(dt_raw + dt_bias)
    return (stepsize, -jnp.exp(a_log) * stepsize)


def span_math(carried, pieces):
    x_rows, b_rows, c_rows, log_rows, step_rows = pieces
    cumlog = jnp.cumsum(log_rows, axis=0)
    block_len = log_rows.shape[0]
    causal = (jnp.arange(block_len)[:, None] >= jnp.arange(block_len)[None, :])[None]
    log_gap = cumlog.T[:, :, None] - cumlog.T[:, None, :]
    decays = jnp.where(causal, jnp.exp(jnp.where(causal, log_gap, 0.0)), 0.0)
    scores = jnp.einsum("ten,sen->ets", c_rows, b_rows, precision=PRECISE)
    weights = scores * decays * step_rows.T[:, None, :]
    inside = jnp.einsum("ets,sep->tep", weights, x_rows, precision=PRECISE)
    from_state = (
        jnp.einsum("ten,epn->tep", c_rows, carried, precision=PRECISE) * jnp.exp(cumlog)[:, :, None]
    )
    final_log = cumlog[-1]
    to_end = jnp.exp(final_log[None, :] - cumlog) * step_rows
    fresh_state = jnp.einsum("sep,sen->epn", x_rows * to_end[:, :, None], b_rows, precision=PRECISE)
    carried = jnp.exp(final_log)[:, None, None] * carried + fresh_state
    return (carried, inside + from_state)


def combine_states(earlier, latter):
    return (earlier[0] * latter[0], latter[0][:, None, None] * earlier[1] + latter[1])


def gated_norm(mixed_in, gate_vec, gain_vec):
    gated = mixed_in * jax.nn.silu(gate_vec)
    grouped = gated.reshape(gated.shape[0], G, -1)
    inv_rms = lax.rsqrt(jnp.mean(grouped * grouped, axis=-1, keepdims=True) + 1e-05)
    return (grouped * inv_rms).reshape(gated.shape) * gain_vec


def per_device(
    x_in,
    b_in,
    c_in,
    dt_in,
    gate_in,
    out_grad,
    conv_x,
    conv_b,
    conv_c,
    a_log,
    dt_bias,
    d_skip,
    norm_gain,
):
    head_ways = lax.axis_size("head")
    head_at = lax.axis_index("head")
    heads_dev = a_log.shape[0]
    heads_all = heads_dev * head_ways
    head_width = conv_x.shape[1] // heads_dev
    per_group = heads_all // G
    groups_dev = max(1, heads_dev * G // heads_all)
    tok_rows = x_in.shape[0]
    tap_count = conv_x.shape[0]
    rim_len = tap_count - 1
    first_group = head_at * heads_dev // per_group
    head_pick = np.arange(heads_dev) // per_group
    group_pick = np.array(
        [
            block_at * heads_dev // per_group + inner_at
            for block_at in range(head_ways)
            for inner_at in range(groups_dev)
        ],
        dtype=np.int32,
    )
    x_rows, dt_rows = (
        lax.all_to_all(x_in, "head", split_axis=1, concat_axis=0, tiled=True),
        lax.all_to_all(dt_in, "head", split_axis=1, concat_axis=0, tiled=True),
    )
    own_rows = x_rows.shape[0]
    n_spans = own_rows // CH
    b_every, c_every = (
        lax.all_gather(b_in, "head", axis=0, tiled=True),
        lax.all_gather(c_in, "head", axis=0, tiled=True),
    )
    b_rows = lax.dynamic_slice_in_dim(b_every, first_group * N, groups_dev * N, 1)
    c_rows = lax.dynamic_slice_in_dim(c_every, first_group * N, groups_dev * N, 1)
    w_b = lax.dynamic_slice_in_dim(conv_b, first_group * N, groups_dev * N, 1)
    w_c = lax.dynamic_slice_in_dim(conv_c, first_group * N, groups_dev * N, 1)
    rim_rows = shifted(
        (x_rows[own_rows - rim_len :], b_rows[own_rows - rim_len :], c_rows[own_rows - rim_len :]),
        "ctx",
        1,
    )

    def extend(rim_part, own_part):
        return jnp.concatenate([rim_part, own_part], axis=0).astype(jnp.float32)

    def conv_part(x_ext, b_ext, c_ext, w_x, w_bb, w_cc):
        return (
            jax.nn.silu(causal_taps(x_ext, w_x)),
            jax.nn.silu(causal_taps(b_ext, w_bb)),
            jax.nn.silu(causal_taps(c_ext, w_cc)),
        )

    (x_conv, b_conv, c_conv), conv_back = jax.vjp(
        conv_part,
        extend(rim_rows[0], x_rows),
        extend(rim_rows[1], b_rows),
        extend(rim_rows[2], c_rows),
        conv_x,
        w_b,
        w_c,
    )
    x_heads = stored(x_conv).reshape(own_rows, heads_dev, head_width)
    b_blocks = stored(b_conv).reshape(own_rows, groups_dev, N)
    c_blocks = stored(c_conv).reshape(own_rows, groups_dev, N)
    dt_raw = dt_rows.astype(jnp.float32)

    def split_rows(array_in):
        return array_in.reshape((n_spans, CH) + array_in.shape[1:])

    def state_part(x_heads, b_blocks, dt_raw, dt_bias, a_log):
        stepsize, logdecay = rates_of(dt_raw, dt_bias, a_log)

        def state_advance(carried, pieces):
            x_part, b_blk, log_rows, step_rows = pieces
            cumlog = jnp.cumsum(log_rows, axis=0)
            final_log = cumlog[-1]
            to_end = jnp.exp(final_log[None, :] - cumlog) * step_rows
            fresh_state = jnp.einsum(
                "sep,sen->epn",
                x_part * to_end[:, :, None],
                b_blk[:, head_pick, :],
                precision=PRECISE,
            )
            return (jnp.exp(final_log)[:, None, None] * carried + fresh_state, None)

        zero_state = jnp.zeros((heads_dev, head_width, N), jnp.float32)
        final_state, _ = lax.scan(
            state_advance,
            zero_state,
            (split_rows(x_heads), split_rows(b_blocks), split_rows(logdecay), split_rows(stepsize)),
        )
        return (jnp.exp(jnp.sum(logdecay, axis=0)), final_state)

    def mixer_part(x_heads, b_blocks, c_blocks, dt_raw, dt_bias, a_log, d_skip, state_in):
        stepsize, logdecay = rates_of(dt_raw, dt_bias, a_log)

        def mixer_advance(carried, pieces):
            x_part, b_blk, c_blk, log_rows, step_rows = pieces
            return span_math(
                carried,
                (x_part, b_blk[:, head_pick, :], c_blk[:, head_pick, :], log_rows, step_rows),
            )

        _, outputs = lax.scan(
            mixer_advance,
            state_in,
            (
                split_rows(x_heads),
                split_rows(b_blocks),
                split_rows(c_blocks),
                split_rows(logdecay),
                split_rows(stepsize),
            ),
        )
        return outputs.reshape(x_heads.shape) + d_skip[:, None] * x_heads

    (decay_all, state_local), state_back = jax.vjp(
        state_part, x_heads, b_blocks, dt_raw, dt_bias, a_log
    )
    identity = (jnp.ones_like(decay_all), jnp.zeros_like(state_local))
    _, state_in = entering((decay_all, state_local), "ctx", combine_states, identity, False)
    mixed_out, mixer_back = jax.vjp(
        mixer_part, x_heads, b_blocks, c_blocks, dt_raw, dt_bias, a_log, d_skip, state_in
    )
    mixed_tok = lax.all_to_all(
        mixed_out.reshape(own_rows, heads_dev * head_width).astype(jnp.bfloat16),
        "head",
        split_axis=0,
        concat_axis=1,
        tiled=True,
    )
    _, norm_back = jax.vjp(
        gated_norm, mixed_tok.astype(jnp.float32), gate_in.astype(jnp.float32), norm_gain
    )
    y_grad, gate_grad, gain_grad = norm_back(out_grad.astype(jnp.float32))
    y_rows = lax.all_to_all(
        y_grad.astype(jnp.bfloat16), "head", split_axis=1, concat_axis=0, tiled=True
    )
    dx_first, db_first, dc_heads, dt_first, bias_first, alog_first, skip_grad, state_grad = (
        mixer_back(y_rows.astype(jnp.float32).reshape(own_rows, heads_dev, head_width))
    )
    _, later_grad = entering((decay_all, state_grad), "ctx", combine_states, identity, True)
    decay_grad = jnp.sum(later_grad * state_in, axis=(1, 2))
    dx_second, db_second, dt_second, bias_second, alog_second = state_back((decay_grad, later_grad))
    dx_ext, db_ext, dc_ext, grad_wx, grad_wb, grad_wc = conv_back(
        (
            (dx_first + dx_second).reshape(own_rows, -1),
            (db_first + db_second).reshape(own_rows, -1),
            dc_heads.reshape(own_rows, -1),
        )
    )
    returned = shifted((dx_ext[:rim_len], db_ext[:rim_len], dc_ext[:rim_len]), "ctx", -1)

    def settle(ext_grad, rim_grad):
        return ext_grad[rim_len:].at[own_rows - rim_len :].add(rim_grad)

    dx_rows = settle(dx_ext, returned[0])
    db_rows = settle(db_ext, returned[1])
    dc_rows = settle(dc_ext, returned[2])
    x_grad, dt_grad = (
        lax.all_to_all(
            dx_rows.astype(jnp.bfloat16), "head", split_axis=0, concat_axis=1, tiled=True
        ),
        lax.all_to_all(
            (dt_first + dt_second).astype(jnp.bfloat16),
            "head",
            split_axis=0,
            concat_axis=1,
            tiled=True,
        ),
    )
    b_back, c_back = (
        lax.all_to_all(
            db_rows.astype(jnp.bfloat16), "head", split_axis=0, concat_axis=1, tiled=True
        ),
        lax.all_to_all(
            dc_rows.astype(jnp.bfloat16), "head", split_axis=0, concat_axis=1, tiled=True
        ),
    )
    group_table = (group_pick[:, None] == np.arange(G)[None, :]).astype(np.float32)

    def regroup(received):
        merged = jnp.einsum(
            "rkn,kg->rgn",
            received.reshape(tok_rows, -1, N).astype(jnp.float32),
            group_table,
            precision=PRECISE,
        )
        return merged.reshape(tok_rows, G * N).astype(jnp.bfloat16)

    b_grad = regroup(b_back)
    c_grad = regroup(c_back)
    wide_b = lax.dynamic_update_slice_in_dim(jnp.zeros_like(conv_b), grad_wb, first_group * N, 1)
    wide_c = lax.dynamic_update_slice_in_dim(jnp.zeros_like(conv_c), grad_wc, first_group * N, 1)
    head_terms = jnp.stack([alog_first + alog_second, bias_first + bias_second, skip_grad])
    conv_x_grad, head_sums = lax.psum((grad_wx, head_terms), "ctx")
    gain_sum, conv_b_grad, conv_c_grad = lax.psum((gain_grad, wide_b, wide_c), ("ctx", "head"))
    return (
        x_grad,
        b_grad,
        c_grad,
        dt_grad,
        gate_grad.astype(jnp.bfloat16),
        conv_x_grad,
        conv_b_grad,
        conv_c_grad,
        head_sums[0],
        head_sums[1],
        head_sums[2],
        gain_sum,
    )


def solution(mesh):
    return jax.shard_map(
        per_device,
        mesh=mesh,
        in_specs=(
            P(("ctx", "head"), None),
            P(("ctx", "head"), None),
            P(("ctx", "head"), None),
            P(("ctx", "head"), None),
            P(("ctx", "head"), None),
            P(("ctx", "head"), None),
            P(None, "head"),
            P(),
            P(),
            P("head"),
            P("head"),
            P("head"),
            P(),
        ),
        out_specs=(
            P(("ctx", "head"), None),
            P(("ctx", "head"), None),
            P(("ctx", "head"), None),
            P(("ctx", "head"), None),
            P(("ctx", "head"), None),
            P(None, "head"),
            P(),
            P(),
            P("head"),
            P("head"),
            P("head"),
            P(),
        ),
        check_vma=False,
    )
```

profile of v0, /device:TPU:1, one launch (start us, length us, event | category | flops | bytes accessed | tf_op | source)
XLA Modules:
  0.0 641.9 jit_solution(11450315560916808205)
XLA Ops:
  7.2 26.0 %all_gather.25 = bf16[256,1024]{1,0:T(8,128)(2,1)S(1)} all-gather(bf16[16,1024]{1,0:T(8,128)(2,1)} %param.31), channel_id=1, replica_groups=mesh['ctx'=32,'head'=16] {'head'}, dimensions={0}, use_global_device_ids=true | all-gather | bytes 557056 | tf_op jit(solution)/shard_map/all_gather | solution.py:128
  33.3 4.2 collective-permute-start.1
  38.8 3.7 all-to-all-start
  42.6 22.5 %all_gather.24 = bf16[256,1024]{1,0:T(8,128)(2,1)S(1)} all-gather(bf16[16,1024]{1,0:T(8,128)(2,1)} %param.32), channel_id=1, replica_groups=mesh['ctx'=32,'head'=16] {'head'}, dimensions={0}, use_global_device_ids=true | all-gather | bytes 557056 | tf_op jit(solution)/shard_map/all_gather | solution.py:129
  79.4 6.1 collective-permute-start.2
  88.3 4.5 collective-permute-start
  96.9 67.9 %all-reduce.26 = f32[128]{0:T(128)S(1)} all-reduce(f32[128]{0:T(128)S(1)} %exponential_dynamic-update-slice_fusion), channel_id=2, replica_groups=mesh['ctx'=32,'head'=16] {'ctx'}, use_global_device_ids=true, to_apply=%add.26 | all-reduce | flops 128 | bytes 1024
  165.0 25.7 %all-gather.6.cloned.1.call-done = f32[128,64,128]{2,1,0:T(8,128)} async-done(((f32[4,64,128]{2,1,0:T(8,128)}), f32[128,64,128]{2,1,0:T(8,128)}) %all-gather.6.cloned.1.call-update) | async-done | bytes 4194320 | tf_op jit(solution)/shard_map/all_gather | solution.py:23
  190.7 32.0 %while.24 = (s32[]{:T(128)}, f32[4,64,128]{2,1,0:T(8,128)S(1)}, s32[]{:T(128)}, f32[32,4]{1,0:T(8,128)S(1)}, f32[32,4,64,128]{3,2,1,0:T(8,128)}, /*index=5*/s32[]{:T(128)}, s32[]{:T(128)}) while((s32[]{:T(128)}, f32[4,64,128]{2,1,0:T(8,128)S(1)}, s32[]{:T(128)}, f32[32,4]{1,0:T(8,128)S(1)}, f32[32,4,64,128]{3,2,1,0:T(8,128)}, ...), condition=%wide.region_4.6_spmd.clone, body=%wide.region_3.5_spmd.clone.sunk | while | flops 131076 | bytes 393369 | solution.py:35
  225.7 13.4 %all_to_all.129 = bf16[16,16,256]{2,1,0:T(8,128)(2,1)S(1)} all-to-all(bf16[16,16,256]{2,1,0:T(8,128)(2,1)S(1)} %bitcast.342), channel_id=1, replica_groups=mesh['ctx'=32,'head'=16] {'head'}, dimensions={0} | all-to-all | bytes 262144 | tf_op jit(solution)/shard_map/all_to_all | solution.py:223
  243.5 9.4 %all_to_all.128 = bf16[16,16,256]{2,0,1:T(8,128)(2,1)S(1)} all-to-all(bf16[16,16,256]{2,0,1:T(8,128)(2,1)S(1)} %bitcast.341), channel_id=1, replica_groups=mesh['ctx'=32,'head'=16] {'head'}, dimensions={1} | all-to-all | bytes 262144 | tf_op jit(solution)/shard_map/all_to_all | solution.py:234
  281.9 4.0 all-to-all-start.6
  286.0 5.8 all-to-all-done.6
  292.6 57.9 %all-gather.8.cloned.1.call-done = f32[128,64,128]{2,1,0:T(8,128)} async-done(((f32[4,64,128]{2,1,0:T(8,128)}), f32[128,64,128]{2,1,0:T(8,128)}) %all-gather.8.cloned.1.call-update) | async-done | bytes 4194320 | tf_op jit(solution)/shard_map/all_gather | solution.py:23
  350.5 4.8 rev.7
  355.4 52.9 %while.25 = (s32[]{:T(128)}, f32[4,64,128]{2,1,0:T(8,128)S(1)}, s32[]{:T(128)}, f32[32,4]{1,0:T(8,128)}, f32[32,4,64,128]{3,2,1,0:T(8,128)}, /*index=5*/s32[]{:T(128)}, s32[]{:T(128)}) while((s32[]{:T(128)}, f32[4,64,128]{2,1,0:T(8,128)S(1)}, s32[]{:T(128)}, f32[32,4]{1,0:T(8,128)}, f32[32,4,64,128]{3,2,1,0:T(8,128)}, ...), condition=%wide.region_8.10_spmd.clone, body=%wide.region_7.9_spmd.clone.sunk | while | flops 131076 | bytes 393369 | solution.py:35
  411.9 5.0 reduce-window.42
  417.3 5.0 reduce-window.44
  423.7 67.7 %all-reduce.28 = (f32[4,256]{1,0:T(4,128)}, f32[3,4]{1,0:T(4,128)S(1)}) all-reduce(f32[4,256]{1,0:T(4,128)S(1)} %pad_add_fusion.4, f32[3,4]{1,0:T(4,128)S(1)} %pad_maximum_fusion), channel_id=1, replica_groups=mesh['ctx'=32,'head'=16] {'ctx'}, use_global_device_ids=true, to_apply=%region_31.33 | all-reduce | flops 1036 | bytes 8288 | tf_op jit(solution)/shard_map/psum | solution.py:294
  494.2 20.3 %all-to-all-start.7 = ((bf16[16,16,4]{1,2,0:T(4,128)(2,1)}), bf16[16,16,4]{1,2,0:T(4,128)(2,1)S(1)}, u32[]{:S(2)}, u32[]{:S(2)}) async-start(bf16[16,16,4]{1,2,0:T(4,128)(2,1)} %copy.205), calls=%async_computation.7 | async-start | bytes 32768 | tf_op jit(solution)/shard_map/all_to_all | solution.py:262
  520.3 3.8 all-to-all-start.5
  525.4 4.5 all-to-all-done.5
  529.9 3.7 all-to-all-start.4
  533.7 99.3 %all-reduce.27 = (f32[4,1024]{1,0:T(4,128)}, f32[4,1024]{1,0:T(4,128)}, f32[4096]{0:T(1024)}) all-reduce(f32[4,1024]{1,0:T(4,128)S(1)} %add_dynamic-update-slice_fusion.1, f32[4,1024]{1,0:T(4,128)S(1)} %add_dynamic-update-slice_fusion, f32[4096]{0:T(1024)S(1)} %copy-done.16), channel_id=1, replica_groups=mesh['ctx'=32,'head'=16] {'ctx','head'}, use_global_device_ids=true, to_apply=%region_36.38 | all-reduce | flops 12288 | bytes 98304 | tf_op jit(solution)/shard_map/psum | solution.py:295
  (424 shorter events, 159.1 us)
Async XLA Ops:
  7.2 85.9 %copy-start.60 = (f32[4]{0:T(128)S(1)}, f32[4]{0:T(128)}, u32[]{:S(2)}) copy-start(f32[4]{0:T(128)} %param.41) | copy-start | bytes 52
  33.3 35.7 %collective-permute-start.1 = (bf16[3,128]{1,0:T(4,128)(2,1)S(1)}, bf16[3,128]{1,0:T(4,128)(2,1)S(1)}, u32[]{:S(2)}, u32[]{:S(2)}) collective-permute-start(bf16[3,128]{1,0:T(4,128)(2,1)S(1)} %dynamic-slice.33), channel_id=1, source_target_pairs={{0,16},{16,32},{32,48},{48,64},{64,80},{80,96},{96,112},{112,128},... | collective-permute-start | bytes 2312 | tf_op jit(solution)/shard_map/ppermute | solution.py:18
  38.8 30.9 %all-to-all-start = ((bf16[16,16,4]{0,2,1:T(4,128)(2,1)}), bf16[16,16,4]{0,2,1:T(4,128)(2,1)S(1)}, u32[]{:S(2)}, u32[]{:S(2)}) async-start(bf16[16,16,4]{0,2,1:T(4,128)(2,1)} %bitcast.9), calls=%async_computation | async-start | bytes 32768 | tf_op jit(solution)/shard_map/all_to_all | solution.py:123
  69.7 9.7 %all-to-all-start.1 = ((bf16[16,16,256]{2,0,1:T(8,128)(2,1)}), bf16[16,16,256]{2,0,1:T(8,128)(2,1)S(1)}, u32[]{:S(2)}, u32[]{:S(2)}) async-start(bf16[16,16,256]{2,0,1:T(8,128)(2,1)} %bitcast.307), calls=%async_computation.1 | async-start | bytes 262144 | tf_op jit(solution)/shard_map/all_to_all | solution.py:122
  73.2 117.6 %all-gather.6.cloned.1.call-start = ((), (), s32[]{:S(2)}) async-start(), calls=%async_computation.8 | async-start | bytes 4325376 | tf_op jit(solution)/shard_map/all_gather | solution.py:23
  74.1 150.7 %copy-start.13 = (f32[256,4]{0,1:T(4,128)}, f32[256,4]{0,1:T(4,128)S(1)}, u32[]{:S(2)}) copy-start(f32[256,4]{0,1:T(4,128)S(1)} %get-tuple-element.824) | copy-start | bytes 12292
  75.7 149.1 %copy-start.25 = (f32[1,4,2,128]{3,1,2,0:T(4,128)}, f32[1,4,2,128]{3,1,2,0:T(4,128)S(1)}, u32[]{:S(2)}) copy-start(f32[1,4,2,128]{3,1,2,0:T(4,128)S(1)} %copy.272) | copy-start | bytes 12292
  76.1 146.7 %copy-start.61 = (f32[4]{0:T(128)}, f32[4]{0:T(128)S(1)}, u32[]{:S(2)}) copy-start(f32[4]{0:T(128)S(1)} %get-tuple-element.862) | copy-start | bytes 52
  76.1 148.7 %copy-start.20 = (f32[256,4]{0,1:T(4,128)}, f32[256,4]{0,1:T(4,128)S(1)}, u32[]{:S(2)}) copy-start(f32[256,4]{0,1:T(4,128)S(1)} %get-tuple-element.860) | copy-start | bytes 12292
  79.4 6.8 %collective-permute-start.2 = (bf16[3,256]{1,0:T(4,128)(2,1)S(1)}, bf16[3,256]{1,0:T(4,128)(2,1)S(1)}, u32[]{:S(2)}, u32[]{:S(2)}) collective-permute-start(bf16[3,256]{1,0:T(4,128)(2,1)S(1)} %slice.260), channel_id=1, source_target_pairs={{0,16},{16,32},{32,48},{48,64},{64,80},{80,96},{96,112},{112,128},... | collective-permute-start | bytes 4616 | tf_op jit(solution)/shard_map/ppermute | solution.py:18
  88.2 262.3 %all-gather.8.cloned.1.call-start = ((), (), s32[]{:S(2)}) async-start(), calls=%async_computation.9 | async-start | bytes 4325376 | tf_op jit(solution)/shard_map/all_gather | solution.py:23
  88.3 7.3 %collective-permute-start = (bf16[3,128]{1,0:T(4,128)(2,1)S(1)}, bf16[3,128]{1,0:T(4,128)(2,1)S(1)}, u32[]{:S(2)}, u32[]{:S(2)}) collective-permute-start(bf16[3,128]{1,0:T(4,128)(2,1)S(1)} %dynamic-slice.32), channel_id=1, source_target_pairs={{0,16},{16,32},{32,48},{48,64},{64,80},{80,96},{96,112},{112,128},... | collective-permute-start | bytes 2312 | tf_op jit(solution)/shard_map/ppermute | solution.py:18
  93.0 131.9 %copy-start.17 = (pred[256,256]{1,0:T(8,128)(4,1)}, pred[256,256]{1,0:T(8,128)(4,1)S(1)}, u32[]{:S(2)}) copy-start(pred[256,256]{1,0:T(8,128)(4,1)S(1)} %iota_compare_fusion) | copy-start | bytes 196612
  96.5 142.6 %copy-start.5 = (bf16[16,4096]{1,0:T(8,128)(2,1)S(1)}, bf16[16,4096]{1,0:T(8,128)(2,1)}, u32[]{:S(2)}) copy-start(bf16[16,4096]{1,0:T(8,128)(2,1)} %param.34) | copy-start | bytes 393220
  96.5 142.7 %copy-start.6 = (bf16[16,4096]{1,0:T(8,128)(2,1)S(1)}, bf16[16,4096]{1,0:T(8,128)(2,1)}, u32[]{:S(2)}) copy-start(bf16[16,4096]{1,0:T(8,128)(2,1)} %param.35) | copy-start | bytes 393220
  268.1 11.9 %collective-permute-start.5 = (f32[3,128]{1,0:T(4,128)}, f32[3,128]{1,0:T(4,128)}, u32[]{:S(2)}, u32[]{:S(2)}) collective-permute-start(f32[3,128]{1,0:T(4,128)} %pad_add_fusion.5), channel_id=1, source_target_pairs={{16,0},{32,16},{48,32},{64,48},{80,64},{96,80},{112,96},{128,112},... | collective-permute-start | bytes 4616 | tf_op jit(solution)/shard_map/ppermute | solution.py:18
  281.9 9.9 %all-to-all-start.6 = ((bf16[16,16,128]{2,1,0:T(8,128)(2,1)}), bf16[16,16,128]{2,1,0:T(8,128)(2,1)S(1)}, u32[]{:S(2)}, u32[]{:S(2)}) async-start(bf16[16,16,128]{2,1,0:T(8,128)(2,1)} %bitcast.50), calls=%async_computation.6 | async-start | bytes 131072 | tf_op jit(solution)/shard_map/all_to_all | solution.py:274
  422.9 110.8 %copy-start.16 = (f32[4096]{0:T(1024)S(1)}, f32[4096]{0:T(1024)}, u32[]{:S(2)}) copy-start(f32[4096]{0:T(1024)} %get-tuple-element.833) | copy-start | bytes 49156
  422.9 210.8 %copy-start.24 = (f32[16,8,1]{0,1,2:T(8,128)S(1)}, f32[16,8,1]{0,1,2:T(8,128)}, u32[]{:S(2)}) copy-start(f32[16,8,1]{0,1,2:T(8,128)} %constant.408) | copy-start | bytes 1540
  491.9 25.2 %collective-permute-start.4 = (f32[3,128]{1,0:T(4,128)S(1)}, f32[3,128]{1,0:T(4,128)S(1)}, u32[]{:S(2)}, u32[]{:S(2)}) collective-permute-start(f32[3,128]{1,0:T(4,128)S(1)} %pad_add_fusion.6), channel_id=1, source_target_pairs={{16,0},{32,16},{48,32},{64,48},{80,64},{96,80},{112,96},{128,112},... | collective-permute-start | bytes 4616 | tf_op jit(solution)/shard_map/ppermute | solution.py:18
  494.2 26.1 %all-to-all-start.7 = ((bf16[16,16,4]{1,2,0:T(4,128)(2,1)}), bf16[16,16,4]{1,2,0:T(4,128)(2,1)S(1)}, u32[]{:S(2)}, u32[]{:S(2)}) async-start(bf16[16,16,4]{1,2,0:T(4,128)(2,1)} %copy.205), calls=%async_computation.7 | async-start | bytes 32768 | tf_op jit(solution)/shard_map/all_to_all | solution.py:262
  515.1 9.0 %collective-permute-start.3 = (f32[3,256]{1,0:T(4,128)S(1)}, f32[3,256]{1,0:T(4,128)S(1)}, u32[]{:S(2)}, u32[]{:S(2)}) collective-permute-start(f32[3,256]{1,0:T(4,128)S(1)} %pad_add_fusion.3), channel_id=1, source_target_pairs={{16,0},{32,16},{48,32},{64,48},{80,64},{96,80},{112,96},{128,112},... | collective-permute-start | bytes 9224 | tf_op jit(solution)/shard_map/ppermute | solution.py:18
  520.3 9.6 %all-to-all-start.5 = ((bf16[16,16,128]{2,1,0:T(8,128)(2,1)}), bf16[16,16,128]{2,1,0:T(8,128)(2,1)S(1)}, u32[]{:S(2)}, u32[]{:S(2)}) async-start(bf16[16,16,128]{2,1,0:T(8,128)(2,1)} %bitcast.45), calls=%async_computation.5 | async-start | bytes 131072 | tf_op jit(solution)/shard_map/all_to_all | solution.py:271
  529.9 104.5 %all-to-all-start.4 = ((bf16[16,16,256]{2,1,0:T(8,128)(2,1)}), bf16[16,16,256]{2,1,0:T(8,128)(2,1)S(1)}, u32[]{:S(2)}, u32[]{:S(2)}) async-start(bf16[16,16,256]{2,1,0:T(8,128)(2,1)} %bitcast.39), calls=%async_computation.4 | async-start | bytes 262144 | tf_op jit(solution)/shard_map/all_to_all | solution.py:259
  (56 other events, 1845.6 us)
Sparse Core Ops, SparseCore 0:
  88.3 102.3 all-gather.5
  255.0 95.4 all-gather.7
where the time goes:
time: 646 us; the launch traced here: 642 us
  blocking collectives  306 us (47%)
  waiting for transfers between devices  99.9 us (15%)
  other arithmetic  89.6 us (14%)
  starting transfers between devices  57.9 us (9%)
  local copies, waits for them, and re-layouts  51.5 us (8%)
  matrix products  19.4 us (3%)
  between operations  16 us (2%)
    psum x1, blocking collectives, per_device(): lax.psum((gain_grad, wide_b, wide_c), ('ctx', 'head'))  99.3 us
    all_gather x2, waiting for transfers between devices, entering(): pieces = jax.tree.map(lambda part: lax.all_gather(part, axis), value)  83.6 us
    unnamed x1, blocking collectives  67.9 us
    psum x1, blocking collectives, per_device(): conv_x_grad, head_sums = lax.psum((grad_wx, head_terms), 'ctx')  67.7 us
    select_n x62, other arithmetic, step(): jnp.where(position < mine, new, old)  61.4 us
    all_gather x1, blocking collectives, per_device(): lax.all_gather(b_in, 'head', axis=0, tiled=True)  26 us
    all_gather x1, blocking collectives, per_device(): lax.all_gather(c_in, 'head', axis=0, tiled=True)  22.5 us
    mul x62, local copies, waits for them, and re-layouts, combine_states(): latter[0][:, None, None] * earlier[1] + latter[1]  21.9 us
  transfers between devices with their start and end apart: 14, of which 7 were waited for; matrix products, arithmetic and copies ran while one was open for 7% of the time, Pallas kernels for 0%

commit v1 on v0

v1 whole, which is shorter than its diff:
```python
import functools

import jax
import jax.numpy as jnp
from jax import lax
from jax.experimental import pallas as pl
from jax.experimental.pallas import tpu as pltpu
from jax.sharding import PartitionSpec as P

BF, F32 = jnp.bfloat16, jnp.float32
GROUPS = 8
N = 128
PS = 64
HD = 4
CW = 256
T = 256
KT = 4
ROWS = 16
IN_W = 1152
OUT_W = 896
VMEM_LIMIT = 48 * 1024 * 1024


def dot(a, b, ca, cb):
    return lax.dot_general(
        a, b, (((ca,), (cb,)), ((), ())), preferred_element_type=F32
    )


def pieces(a, count):
    out = []
    for _ in range(count - 1):
        head = a.astype(BF)
        out.append(head)
        a = a - head.astype(F32)
    return out + [a.astype(BF)]


def dot_parts(a, b, ca, cb, count):
    total = None
    for piece in pieces(a, count):
        term = dot(piece, b, ca, cb)
        total = term if total is None else total + term
    return total


def dot_right(a, b, ca, cb):
    high, low = pieces(b, 2)
    return dot(a, high, ca, cb) + dot(a, low, ca, cb)


def dot_both(a, b, ca, cb):
    a_high, a_low = pieces(a, 2)
    b_high, b_low = pieces(b, 2)
    return dot(a_high, b_high, ca, cb) + (dot(a_high, b_low, ca, cb) + dot(a_low, b_high, ca, cb))


def iota(shape, axis):
    return lax.broadcasted_iota(jnp.int32, shape, axis)


def spread(cols):
    low = iota((cols.shape[0], 128), 1) < PS
    halves = []
    for pair in range(HD // 2):
        first = jnp.broadcast_to(cols[:, 2 * pair : 2 * pair + 1], (cols.shape[0], 128))
        second = jnp.broadcast_to(cols[:, 2 * pair + 1 : 2 * pair + 2], (cols.shape[0], 128))
        halves.append(jnp.where(low, first, second))
    return jnp.concatenate(halves, axis=1)


def head_sums(wide):
    pick = (iota((CW, 128), 0) // PS == iota((CW, 128), 1)).astype(BF)
    return dot_parts(wide, pick, 1, 0, 3)


def scalar_row(ref, width, per):
    lane = iota((1, width), 1) // per
    row = jnp.zeros((1, width), F32)
    for e in range(HD):
        row = jnp.where(lane == e, ref[e], row)
    return row


def softplus(v):
    return jnp.maximum(v, 0.0) + jnp.log1p(jnp.exp(-jnp.abs(v)))


def rates(dt_cols, bias_row, alog_row):
    live = iota((T, 128), 1) < HD
    shifted = dt_cols + bias_row
    step = jnp.where(live, softplus(shifted), 0.0)
    logd = -jnp.exp(alog_row) * step
    tril = (iota((T, T), 0) >= iota((T, T), 1)).astype(BF)
    cum = sum(dot(tril, piece, 1, 0) for piece in pieces(logd, 3))
    return shifted, step, logd, cum


def taps(ext_ref, weight, lo, hi):
    total = None
    for k in range(KT):
        term = weight[k : k + 1, :] * ext_ref[ROWS - KT + 1 + k : ROWS - KT + 1 + k + T, lo:hi]
        total = term if total is None else total + term
    return total


def gap_decay(cum, cum_t, e):
    causal = iota((T, T), 0) >= iota((T, T), 1)
    gap = jnp.where(causal, cum[:, e : e + 1] - cum_t[e : e + 1, :], 0.0)
    return jnp.where(causal, jnp.exp(gap), 0.0)


def silu_slope(pre):
    gate = jax.nn.sigmoid(pre)
    return pre * gate, gate * (1.0 + pre * (1.0 - gate))


def three_rows(row, count):
    at = iota((count, row.shape[1]), 0)
    high, middle, low = pieces(row, 3)
    return jnp.where(
        at == 0,
        high.astype(F32),
        jnp.where(at == 1, middle.astype(F32), jnp.where(at == 2, low.astype(F32), 0.0)),
    ).astype(BF)


def enter_math(ext, dt_cols, wx, wb, wc, bias_row, alog_row):
    def act(weight, lo, hi):
        pre = taps(ext, weight, lo, hi)
        return (pre * jax.nn.sigmoid(pre)).astype(BF)

    x_act, b_act, c_act = act(wx, 0, 256), act(wb, 256, 384), act(wc, 384, 512)
    shifted, step, logd, cum = rates(dt_cols, bias_row, alog_row)
    final = cum[T - 1 : T, :]
    to_end = jnp.exp(final - cum) * step
    weighted = x_act.astype(F32) * spread(to_end)
    fresh = dot_parts(weighted, b_act, 0, 0, 2)
    return x_act, b_act, c_act, step, cum, fresh, final


def within_math(x_act, b_act, c_act, step, cum, cum_t):
    scores = dot(c_act, b_act, 1, 1)
    stepped = x_act.astype(F32) * spread(step)
    outs, kept = [], []
    for e in range(HD):
        mix = (scores * gap_decay(cum, cum_t, e)).astype(BF)
        kept.append(mix)
        part = stepped[:, e * PS : (e + 1) * PS]
        high, low = pieces(part, 2)
        both = dot(mix, jnp.concatenate([high, low], axis=1), 1, 0)
        outs.append(both[:, :PS] + both[:, PS:])
    return jnp.concatenate(outs, axis=1), kept


def mix_math(x_act, c_act, inside, carried, cum, skip_row, gate, out_grad, gain):
    grown = spread(jnp.exp(cum))
    y = inside + grown * dot_right(c_act, carried, 1, 1)
    mixed = (y + skip_row * x_act.astype(F32)).astype(BF)
    gate_act = gate * jax.nn.sigmoid(gate)
    v = mixed.astype(F32) * gate_act
    squares = jnp.sum(v * v, axis=1, keepdims=True)
    along = jnp.sum(out_grad * gain * v, axis=1, keepdims=True)
    return y, mixed, squares, along


def norm_math(mixed, gate, out_grad, gain, squares, along, c_act, cum):
    gate_act, gate_slope = silu_slope(gate)
    mixed = mixed.astype(F32)
    v = mixed * gate_act
    inv = lax.rsqrt(squares * (1.0 / (2 * CW)) + 1e-05)
    normed = v * inv
    v_grad = inv * (out_grad * gain - normed * (along * inv * (1.0 / (2 * CW))))
    y_grad = (v_grad * gate_act).astype(BF)
    gate_grad = (v_grad * mixed * gate_slope).astype(BF)
    gain_grad = jnp.sum(out_grad * normed, axis=0, keepdims=True)
    grown = spread(jnp.exp(cum))
    lifted = y_grad.astype(F32) * grown
    start_grad = dot_parts(lifted, c_act, 0, 0, 2)
    return y_grad, gate_grad, gain_grad, lifted, start_grad


def within_back_math(x_act, b_act, c_act, step, cum, cum_t, kept, y, y_grad, lifted, carried):
    score_grad = jnp.zeros((T, T), F32)
    x_parts = []
    step_t = step.T
    for e in range(HD):
        cut = slice(e * PS, (e + 1) * PS)
        x_parts.append(dot(kept[e], y_grad[:, cut], 0, 0))
        mix_grad = dot(y_grad[:, cut], x_act[:, cut], 1, 1)
        score_grad = score_grad + mix_grad * (gap_decay(cum, cum_t, e) * step_t[e : e + 1, :])
    x_in = jnp.concatenate(x_parts, axis=1)
    score_grad = score_grad.astype(BF)
    c_grad = dot(score_grad, b_act, 1, 0) + dot_both(lifted, carried, 1, 0)
    b_in = dot(score_grad, c_act, 0, 0)
    dy = y_grad.astype(F32)
    x32 = x_act.astype(F32)
    out_dots = head_sums(dy * y)
    in_dots = head_sums(x32 * x_in)
    skip_grad = jnp.sum(dy * x32, axis=0, keepdims=True)
    return x_in, b_in, c_grad, out_dots, in_dots, skip_grad


def leave_math(x_act, b_act, step, cum, shifted, logd, alog_row, skip_row, y_grad, x_in, b_in, out_dots, in_dots, carried, end_grad):
    final = cum[T - 1 : T, :]
    tail = jnp.exp(final - cum)
    x32 = x_act.astype(F32)
    end_b = end_grad.astype(BF)
    x_state = spread(tail) * dot(b_act, end_b, 1, 1)
    state_dots = head_sums(x32 * x_state)
    wide_step = spread(step)
    x_grad = wide_step * (x_in + x_state) + skip_row * y_grad.astype(F32)
    weighted = (x32 * spread(tail * step)).astype(BF)
    b_grad = b_in + dot(weighted, end_b, 1, 0)
    pull = step * state_dots
    cum_grad = out_dots - step * in_dots - pull
    kept_dots = jnp.sum(carried * end_grad, axis=1, keepdims=True)
    lane = iota((1, 128), 1)
    over = jnp.zeros((1, 128), F32)
    for e in range(HD):
        over = jnp.where(lane == e, jnp.sum(kept_dots[e * PS : (e + 1) * PS, :], axis=0, keepdims=True), over)
    final_grad = jnp.sum(pull, axis=0, keepdims=True) + jnp.exp(final) * over
    triu = (iota((T, T), 0) <= iota((T, T), 1)).astype(BF)
    log_grad = sum(dot(triu, piece, 1, 0) for piece in pieces(cum_grad, 3)) + final_grad
    step_grad = in_dots + state_dots - jnp.exp(alog_row) * log_grad
    alog_grad = jnp.sum(log_grad * logd, axis=0, keepdims=True)
    live = iota((T, 128), 1) < HD
    dt_grad = jnp.where(live, step_grad * jax.nn.sigmoid(shifted), 0.0)
    bias_grad = jnp.sum(dt_grad, axis=0, keepdims=True)
    return x_grad, b_grad, dt_grad, alog_grad, bias_grad


def conv_slopes(ext, wx, wb, wc):
    def slope(weight, lo, hi):
        return silu_slope(taps(ext, weight, lo, hi))[1]

    return jnp.concatenate([slope(wx, 0, 256), slope(wb, 256, 384), slope(wc, 384, 512)], axis=1)


def weight_grads(ext, pre_grad):
    return [
        jnp.sum(pre_grad * ext[ROWS - KT + 1 + k : ROWS - KT + 1 + k + T], axis=0, keepdims=True)
        for k in range(KT)
    ]


def conv_back(pre_ext, weight, lo, hi):
    total = None
    for k in range(KT):
        term = weight[k : k + 1, :] * pre_ext[KT - 1 - k : KT - 1 - k + T, lo:hi]
        total = term if total is None else total + term
    return total


ZW = 4
PACK = T + 8


def call(kernel, out_shape, in_specs, out_specs=None, scratch=(), flops=0, bytes_accessed=0):
    vmem = pl.BlockSpec(memory_space=pltpu.VMEM)
    smem = pl.BlockSpec(memory_space=pltpu.SMEM)
    place = {"v": vmem, "s": smem}
    return pl.pallas_call(
        kernel,
        out_shape=out_shape,
        in_specs=[place[c] for c in in_specs],
        out_specs=[place[c] for c in (out_specs or "v" * len(out_shape))],
        scratch_shapes=list(scratch),
        compiler_params=pltpu.CompilerParams(vmem_limit_bytes=VMEM_LIMIT),
        cost_estimate=pl.CostEstimate(
            flops=flops, bytes_accessed=bytes_accessed, transcendentals=0
        ),
    )


def sds(shape, dtype):
    return jax.ShapeDtypeStruct(shape, dtype)


def pack_kernel(x, b, c, dt, gate, out_grad, out):
    ways = out.shape[0]
    per = GROUPS * N // ways
    wide_dt = jnp.concatenate(
        [dt[...].astype(F32), jnp.zeros((ROWS, 128 - dt.shape[1]), F32)], axis=1
    )
    lane = iota((ROWS, 128), 1)
    for j in range(ways):
        g = (j * per) // N
        own = slice(j * CW, (j + 1) * CW)
        shared = slice(g * N, (g + 1) * N)
        out[j, :, 0:256] = x[:, own]
        out[j, :, 256:384] = b[:, shared]
        out[j, :, 384:512] = c[:, shared]
        out[j, :, 512:768] = gate[:, own]
        out[j, :, 768:1024] = out_grad[:, own]
        turned = pltpu.roll(wide_dt, (128 - HD * j) % 128, 1)
        out[j, :, 1024:1152] = jnp.where(lane < HD, turned, 0.0).astype(BF)


def group_lanes(ref, where):
    return ref[:, pl.ds(pl.multiple_of(where[1] * N, N), N)]


def final_rows(final):
    return jnp.broadcast_to(final, (8, 128))


def enter_kernel(rows, halo, wx, wb, wc, alog, bias, where, xbc, step_out, cum_out, send, ext):
    ext[0:ROWS] = halo[...].astype(F32)
    ext[ROWS : ROWS + T] = rows[:, 0:512].astype(F32)
    x_act, b_act, c_act, step, cum, fresh, final = enter_math(
        ext,
        rows[:, 1024:1152].astype(F32),
        wx[...],
        group_lanes(wb, where),
        group_lanes(wc, where),
        scalar_row(bias, 128, 1),
        scalar_row(alog, 128, 1),
    )
    xbc[:, 0:256] = x_act
    xbc[:, 256:384] = b_act
    xbc[:, 384:512] = c_act
    step_out[...] = step
    cum_out[...] = cum
    tail = final_rows(final)
    for i in range(send.shape[0]):
        send[i, 0:T] = fresh
        send[i, T:PACK] = tail


def within_kernel(xbc, step, cum, inside, kept):
    step, cum = step[...], cum[...]
    out, mixes = within_math(xbc[:, 0:256], xbc[:, 256:384], xbc[:, 384:512], step, cum, cum.T)
    inside[...] = out
    for e in range(HD):
        kept[e] = mixes[e]


def head_column(row):
    return jnp.concatenate(
        [jnp.broadcast_to(row[:, e : e + 1], (PS, 1)) for e in range(HD)], axis=0
    )


def chain(received, count, backward, mine):
    state = jnp.zeros((T, 128), F32)
    total = jnp.zeros((1, 128), F32)
    kept_state, kept_total = state, total
    for i in range(count):
        at = count - 1 - i if backward else i
        here = mine == at
        kept_state = jnp.where(here, state, kept_state)
        kept_total = jnp.where(here, total, kept_total)
        log = received[at, T : T + 1, :]
        state = head_column(jnp.exp(log)) * state + received[at, 0:T, :]
        total = total + log
    return kept_state, kept_total, state, total


def near_kernel(backward, received, where, send, near):
    kept_state, kept_total, state, total = chain(received, received.shape[0], backward, where[2])
    near[0:T] = kept_state
    near[T:PACK] = final_rows(kept_total)
    tail = final_rows(total)
    for i in range(send.shape[0]):
        send[i, 0:T] = state
        send[i, T:PACK] = tail


def far_state(backward, received, near, mine):
    count = received.shape[0]
    state = jnp.zeros((T, 128), F32)
    for i in range(count):
        at = count - 1 - i if backward else i
        log = received[at, T : T + 1, :]
        longer = head_column(jnp.exp(log)) * state + received[at, 0:T, :]
        use = (at > mine) if backward else (at < mine)
        state = jnp.where(use, longer, state)
    return head_column(jnp.exp(near[T : T + 1, :])) * state + near[0:T, :]


def pair_rows(squares, along):
    lane = iota((T, 128), 1)
    both = jnp.where(lane == 0, squares, jnp.where(lane == 1, along, 0.0))
    return both.T[0:8, :]


def gain_lanes(ref, where):
    return ref[:, pl.ds(pl.multiple_of(where[0] * CW, CW), CW)]


def mix_kernel(received, near, xbc, inside, cum, rows, gain, skip, where, y_out, mixed_out, carried_out, message):
    carried = far_state(False, received, near, where[3])
    y, mixed, squares, along = mix_math(
        xbc[:, 0:256],
        xbc[:, 384:512],
        inside[...],
        carried,
        cum[...],
        scalar_row(skip, CW, PS),
        rows[:, 512:768].astype(F32),
        rows[:, 768:1024].astype(F32),
        gain_lanes(gain, where),
    )
    y_out[...] = y
    mixed_out[...] = mixed
    carried_out[...] = carried
    message[...] = pair_rows(squares, along)


def norm_kernel(message, mixed, rows, gain, xbc, cum, where, y_grad_out, gate_out, gain_out, lifted_out, send):
    cum = cum[...]
    sums = jnp.concatenate([message[...], jnp.zeros((120, T), F32)], axis=0).T
    y_grad, gate_grad, gain_grad, lifted, start_grad = norm_math(
        mixed[...],
        rows[:, 512:768].astype(F32),
        rows[:, 768:1024].astype(F32),
        gain_lanes(gain, where),
        sums[:, 0:1],
        sums[:, 1:2],
        xbc[:, 384:512],
        cum,
    )
    y_grad_out[...] = y_grad
    gate_out[...] = gate_grad
    gain_out[...] = jnp.broadcast_to(gain_grad, (8, CW))
    lifted_out[...] = lifted
    tail = final_rows(cum[T - 1 : T, :])
    for i in range(send.shape[0]):
        send[i, 0:T] = start_grad
        send[i, T:PACK] = tail


def back_kernel(
    rows, halo, wx, wb, wc, where, xbc, step, cum, kept, y, y_grad, lifted, carried,
    x_in_out, b_in_out, c_grad_out, out_dots_out, in_dots_out, skip_out, slopes_out, ext,
):
    ext[0:ROWS] = halo[...].astype(F32)
    ext[ROWS : ROWS + T] = rows[:, 0:512].astype(F32)
    slopes_out[...] = conv_slopes(
        ext, wx[...], group_lanes(wb, where), group_lanes(wc, where)
    )
    cum = cum[...]
    x_in, b_in, c_grad, out_dots, in_dots, skip_grad = within_back_math(
        xbc[:, 0:256],
        xbc[:, 256:384],
        xbc[:, 384:512],
        step[...],
        cum,
        cum.T,
        [kept[e] for e in range(HD)],
        y[...],
        y_grad[...],
        lifted[...],
        carried[...],
    )
    x_in_out[...] = x_in
    b_in_out[...] = b_in
    c_grad_out[...] = c_grad
    out_dots_out[...] = out_dots
    in_dots_out[...] = in_dots
    skip_out[...] = jnp.broadcast_to(skip_grad, (8, CW))


def leave_kernel(
    received, near, rows, halo, where, alog, bias, skip, xbc, step, cum, y_grad, x_in, b_in,
    c_grad, out_dots, in_dots, carried, gain_grad, skip_grad, slopes,
    pre_out, dt_out, send, ext,
):
    ext[0:ROWS] = halo[...].astype(F32)
    ext[ROWS : ROWS + T] = rows[:, 0:512].astype(F32)
    end_grad = far_state(True, received, near, where[3])
    alog_row = scalar_row(alog, 128, 1)
    step = step[...]
    x_grad, b_grad, dt_grad, alog_grad, bias_grad = leave_math(
        xbc[:, 0:256],
        xbc[:, 256:384],
        step,
        cum[...],
        rows[:, 1024:1152].astype(F32) + scalar_row(bias, 128, 1),
        -jnp.exp(alog_row) * step,
        alog_row,
        scalar_row(skip, CW, PS),
        y_grad[...],
        x_in[...],
        b_in[...],
        out_dots[...],
        in_dots[...],
        carried[...],
        end_grad,
    )
    dt_out[...] = dt_grad
    pre = jnp.concatenate([x_grad, b_grad, c_grad[...]], axis=1) * slopes[...]
    pre_out[...] = pre
    weights = weight_grads(ext, pre)
    block = jnp.concatenate(
        weights
        + [
            jnp.concatenate([gain_grad[0:1, :], skip_grad[0:1, :]], axis=1),
            jnp.concatenate([alog_grad, bias_grad, jnp.zeros((1, 256), F32)], axis=1),
            jnp.zeros((2, 512), F32),
            pre[0:8, :],
        ],
        axis=0,
    )
    for i in range(send.shape[0]):
        send[i] = block


def near_sum_kernel(received, where, send, halo):
    ways = received.shape[0]
    mine = where[2]
    total = received[0, 0:8, :]
    for i in range(1, ways):
        total = total + received[i, 0:8, :]
    following = jnp.zeros((8, 512), F32)
    for i in range(1, ways):
        following = jnp.where(mine == i - 1, received[i, 8:16, :], following)
    halo[...] = following
    first = received[0, 8:16, :]
    for i in range(send.shape[0]):
        send[i, 0:8] = total
        send[i, 8:16] = first


def finish_kernel(received, near_halo, where, wx, wb, wc, pre, dt_grad, gate_grad, send, conv_x_out, alog_out, bias_out, skip_out, ext):
    ways = received.shape[0]
    total = received[0, 0:8, :]
    for i in range(1, ways):
        total = total + received[i, 0:8, :]
    following = jnp.zeros((8, 512), F32)
    for i in range(1, ways):
        following = jnp.where(where[3] == i - 1, received[i, 8:16, :], following)
    following = jnp.where(where[2] == ZW - 1, following, near_halo[...])
    ext[0:T] = pre[...]
    ext[T : T + 8] = following
    x_grad = conv_back(ext, wx[...], 0, 256).astype(BF)
    b_grad = conv_back(ext, group_lanes(wb, where), 256, 384).astype(BF)
    c_grad = conv_back(ext, group_lanes(wc, where), 384, 512).astype(BF)
    conv_x_out[...] = total[0:KT, 0:CW]
    for e in range(HD):
        alog_out[e] = jnp.sum(total[5:6, e : e + 1])
        bias_out[e] = jnp.sum(total[5:6, 128 + e : 129 + e])
        skip_out[e] = jnp.sum(total[4:5, CW + e * PS : CW + (e + 1) * PS])
    shared = jnp.concatenate([total[0:5, 256:512], jnp.zeros((11, 256), F32)], axis=0)
    shared = jnp.where(iota((16, 256), 0) == 4, jnp.broadcast_to(total[4:5, 0:256], (16, 256)), shared)
    high, middle, low = pieces(shared, 3)
    dt_low = dt_grad[...].astype(BF)
    for j in range(send.shape[0]):
        cut = slice(j * ROWS, (j + 1) * ROWS)
        send[j, :, 0:256] = x_grad[cut]
        send[j, :, 256:384] = b_grad[cut]
        send[j, :, 384:512] = c_grad[cut]
        send[j, :, 512:768] = gate_grad[cut, :]
        send[j, :, 768:896] = dt_low[cut]
        send[j, :, 896:1152] = high
        send[j, :, 1152:1408] = middle
        send[j, :, 1408:1664] = low


def unpack_kernel(received, x_out, b_out, c_out, dt_out, gate_out, conv_b_out, conv_c_out, gain_out):
    ways = received.shape[0]
    lane = iota((ROWS, 128), 1)
    dt = jnp.zeros((ROWS, 128), F32)
    shared = []
    for j in range(ways):
        own = slice(j * CW, (j + 1) * CW)
        x_out[:, own] = received[j, :, 0:256]
        gate_out[:, own] = received[j, :, 512:768]
        turned = pltpu.roll(received[j, :, 768:896].astype(F32), HD * j, 1)
        dt = jnp.where(lane // HD == j, turned, dt)
        shared.append(
            received[j, :, 896:1152].astype(F32)
            + received[j, :, 1152:1408].astype(F32)
            + received[j, :, 1408:1664].astype(F32)
        )
        gain_out[:, own] = shared[j][4:5, :]
    dt_out[...] = dt[:, 0 : dt_out.shape[1]].astype(BF)
    per = ways // GROUPS
    for g in range(GROUPS):
        cut = slice(g * N, (g + 1) * N)
        b_sum, c_sum, w_sum = 0.0, 0.0, 0.0
        for j in range(g * per, (g + 1) * per):
            b_sum = b_sum + received[j, :, 256:384].astype(F32)
            c_sum = c_sum + received[j, :, 384:512].astype(F32)
            w_sum = w_sum + shared[j]
        b_out[:, cut] = b_sum.astype(BF)
        c_out[:, cut] = c_sum.astype(BF)
        conv_b_out[:, cut] = w_sum[0:KT, 0:128]
        conv_c_out[:, cut] = w_sum[0:KT, 128:256]


def per_device(
    x_in, b_in, c_in, dt_in, gate_in, out_grad, conv_x, conv_b, conv_c, a_log, dt_bias, d_skip, norm_gain
):
    ways = lax.axis_size("head")
    blocks = lax.axis_size("ctx")
    far = blocks // ZW
    near_groups = [[y * ZW + z for z in range(ZW)] for y in range(far)]
    far_groups = [[y * ZW + z for y in range(far)] for z in range(ZW)]
    head_at, ctx_at = lax.axis_index("head"), lax.axis_index("ctx")
    where = jnp.stack(
        [head_at, head_at * GROUPS // ways, ctx_at % ZW, ctx_at // ZW]
    ).astype(jnp.int32)
    gain = norm_gain.reshape(1, -1)

    def near_swap(value):
        return lax.all_to_all(value, "ctx", 0, 0, axis_index_groups=near_groups)

    def far_swap(value):
        return lax.all_to_all(value, "ctx", 0, 0, axis_index_groups=far_groups)

    def head_swap(value):
        return lax.all_to_all(value, "head", 0, 0, tiled=True)

    sent = call(pack_kernel, [sds((ways, ROWS, IN_W), BF)], "vvvvvv")(
        x_in, b_in, c_in, dt_in, gate_in, out_grad
    )[0]
    arrived = head_swap(sent)
    rows = arrived.reshape(T, IN_W)
    halo = lax.ppermute(
        arrived[ways - 1, :, 0:512], "ctx", [(i, i + 1) for i in range(blocks - 1)]
    )
    wide = sds((T, CW), F32)
    slim = sds((T, 128), F32)
    message = sds((ZW, PACK, 128), F32)
    far_message = sds((far, PACK, 128), F32)
    near_part = sds((PACK, 128), F32)
    ext = pltpu.VMEM((ROWS + T, 512), F32)

    xbc, step, cum, send = call(
        enter_kernel, [sds((T, 512), BF), slim, slim, message], "vvvvvsss", scratch=[ext]
    )(rows, halo, conv_x, conv_b, conv_c, a_log, dt_bias, where)
    received = near_swap(send)
    inside, kept = call(
        within_kernel, [wide, sds((HD, T, T), BF)], "vvv", flops=10**8, bytes_accessed=2 * 10**6
    )(xbc, step, cum)
    send, near = call(functools.partial(near_kernel, False), [far_message, near_part], "vs")(
        received, where
    )
    received = far_swap(send)
    y, mixed, carried, sums = call(
        mix_kernel,
        [wide, sds((T, CW), BF), slim, sds((8, T), F32)],
        "vvvvvvvss",
    )(received, near, xbc, inside, cum, rows, gain, d_skip, where)
    per = ways // GROUPS
    sums = lax.psum(
        sums, "head", axis_index_groups=[[g * per + i for i in range(per)] for g in range(GROUPS)]
    )
    y_grad, gate_grad, gain_grad, lifted, send = call(
        norm_kernel,
        [sds((T, CW), BF), sds((T, CW), BF), sds((8, CW), F32), wide, message],
        "vvvvvvs",
    )(sums, mixed, rows, gain, xbc, cum, where)
    received = near_swap(send)
    x_part, b_part, c_grad, out_dots, in_dots, skip_grad, slopes = call(
        back_kernel,
        [wide, slim, slim, slim, slim, sds((8, CW), F32), sds((T, 512), F32)],
        "vvvvvsvvvvvvvv",
        scratch=[ext],
        flops=3 * 10**8,
        bytes_accessed=4 * 10**6,
    )(rows, halo, conv_x, conv_b, conv_c, where, xbc, step, cum, kept, y, y_grad, lifted, carried)
    send, near = call(functools.partial(near_kernel, True), [far_message, near_part], "vs")(
        received, where
    )
    received = far_swap(send)
    pre, dt_grad, send = call(
        leave_kernel,
        [sds((T, 512), F32), slim, sds((ZW, 16, 512), F32)],
        "vvvvssss" + "v" * 13,
        scratch=[ext],
    )(
        received, near, rows, halo, where, a_log, dt_bias, d_skip, xbc, step, cum, y_grad, x_part,
        b_part, c_grad, out_dots, in_dots, carried, gain_grad, skip_grad, slopes,
    )
    received = near_swap(send)
    send, near_halo = call(
        near_sum_kernel, [sds((far, 16, 512), F32), sds((8, 512), F32)], "vs"
    )(received, where)
    received = far_swap(send)
    four = sds((HD,), F32)
    send, conv_x_grad, alog_grad, bias_grad, skip_sum = call(
        finish_kernel,
        [sds((ways, ROWS, 1664), BF), sds((KT, CW), F32), four, four, four],
        "vvsvvvvvv",
        "vvsss",
        scratch=[pltpu.VMEM((T + 8, 512), F32)],
    )(received, near_halo, where, conv_x, conv_b, conv_c, pre, dt_grad, gate_grad)
    received = head_swap(send)
    heads = dt_in.shape[1]
    x_grad, b_grad, c_grad, dt_out, gate_out, conv_b_grad, conv_c_grad, gain_sum = call(
        unpack_kernel,
        [
            sds(x_in.shape, BF),
            sds(b_in.shape, BF),
            sds(c_in.shape, BF),
            sds((ROWS, heads), BF),
            sds(gate_in.shape, BF),
            sds(conv_b.shape, F32),
            sds(conv_c.shape, F32),
            sds((1, norm_gain.shape[0]), F32),
        ],
        "v",
    )(received)
    return (
        x_grad,
        b_grad,
        c_grad,
        dt_out,
        gate_out,
        conv_x_grad,
        conv_b_grad,
        conv_c_grad,
        alog_grad,
        bias_grad,
        skip_sum,
        gain_sum.reshape(-1),
    )


def solution(mesh):
    tokens = P(("ctx", "head"), None)
    return jax.shard_map(
        per_device,
        mesh=mesh,
        in_specs=(tokens,) * 6 + (P(None, "head"), P(), P(), P("head"), P("head"), P("head"), P()),
        out_specs=(tokens,) * 5
        + (P(None, "head"), P(), P(), P("head"), P("head"), P("head"), P()),
        check_vma=False,
    )
```

time: 646 us -> 217 us (0.34)
  blocking collectives: 306 us -> 97.3 us
  other arithmetic: 89.6 us -> 0.08 us
  waiting for transfers between devices: 99.9 us -> 50.9 us
  starting transfers between devices: 57.9 us -> 23.8 us
  local copies, waits for them, and re-layouts: 51.5 us -> 26.5 us
  matrix products: 19.4 us -> 0 us
  Pallas kernels: 0 us -> 16.9 us
  between operations: 16 us -> 0.82 us
    psum x2 -> x1, blocking collectives: 167 us -> 8.07 us  [per_device(): lax.psum(sums, 'head', axis_index_groups=[[g * per + i for i in range(per...]
    all_gather x2 -> x0, waiting for transfers between devices: 83.6 us -> none  [entering(): pieces = jax.tree.map(lambda part: lax.all_gather(part, axis), value)]
    unnamed x1 -> x0, blocking collectives: 67.9 us -> none
    all_to_all x2 -> x5, blocking collectives: 22.8 us -> 89.2 us  [the longest x3 54 us: near_swap(): return lax.all_to_all(value, 'ctx', 0, 0, axis_index_groups=near_groups)]
    select_n x62 -> x0, other arithmetic: 61.4 us -> none  [step(): jnp.where(position < mine, new, old)]
    all_gather x2 -> x0, blocking collectives: 48.5 us -> none  [the longest x1 26 us: per_device(): lax.all_gather(b_in, 'head', axis=0, tiled=True)]
    all_to_all x6 -> x3, waiting for transfers between devices: 15.5 us -> 50.1 us  [the longest x2 39.5 us: far_swap(): return lax.all_to_all(value, 'ctx', 0, 0, axis_index_groups=far_groups)]
    mul x67 -> x0, local copies, waits for them, and re-layouts: 22.7 us -> none  [the longest x62 21.9 us: combine_states(): latter[0][:, None, None] * earlier[1] + latter[1]]
  transfers between devices with their start and end apart: 14 -> 4, of which waited for: 7 -> 4; matrix products, arithmetic and copies ran while one was open for 7% -> 0% of each run, Pallas kernels for 0% -> 2%
where the time goes in v1:
time: 217 us; the launch traced here: 216 us
  blocking collectives  97.3 us (45%)
  waiting for transfers between devices  50.9 us (23%)
  local copies, waits for them, and re-layouts  26.5 us (12%)
  starting transfers between devices  23.8 us (11%)
  Pallas kernels  16.9 us (8%)
    all_to_all x3, blocking collectives, near_swap(): return lax.all_to_all(value, 'ctx', 0, 0, axis_index_groups=near_groups)  54 us
    all_to_all x2, waiting for transfers between devices, far_swap(): return lax.all_to_all(value, 'ctx', 0, 0, axis_index_groups=far_groups)  39.5 us
    unnamed x90, local copies, waits for them, and re-layouts  26.5 us
    all_to_all x1, blocking collectives, head_swap(): return lax.all_to_all(value, 'head', 0, 0, tiled=True)  23.4 us
    all_to_all x1, blocking collectives, far_swap(): return lax.all_to_all(value, 'ctx', 0, 0, axis_index_groups=far_groups)  11.8 us
    all_to_all x1, waiting for transfers between devices, head_swap(): return lax.all_to_all(value, 'head', 0, 0, tiled=True)  10.6 us
    all_to_all x2, starting transfers between devices, far_swap(): return lax.all_to_all(value, 'ctx', 0, 0, axis_index_groups=far_groups)  10.5 us
    all_to_all x1, starting transfers between devices, head_swap(): return lax.all_to_all(value, 'head', 0, 0, tiled=True)  10.2 us
  transfers between devices with their start and end apart: 4, of which 4 were waited for; matrix products, arithmetic and copies ran while one was open for 0% of the time, Pallas kernels for 2%

profile of v1, /device:TPU:1, one launch (start us, length us, event | category | flops | bytes accessed | tf_op | source)
XLA Modules:
  0.0 216.3 jit_solution(3694727749115509862)
XLA Ops:
  6.5 10.2 %all-to-all-start = ((bf16[16,16,1152]{2,1,0:T(8,128)(2,1)}), bf16[16,16,1152]{2,1,0:T(8,128)(2,1)S(1)}, u32[]{:S(2)}, u32[]{:S(2)}) async-start(bf16[16,16,1152]{2,1,0:T(8,128)(2,1)} %shard_map.220), calls=%async_computation | async-start | bytes 1179648 | tf_op jit(solution)/shard_map/all_to_all | solution.py:614
  16.8 10.6 %all-to-all-done = bf16[16,16,1152]{2,1,0:T(8,128)(2,1)S(1)} async-done(((bf16[16,16,1152]{2,1,0:T(8,128)(2,1)}), bf16[16,16,1152]{2,1,0:T(8,128)(2,1)S(1)}, u32[]{:S(2)}, u32[]{:S(2)}) %all-to-all-start) | async-done | bytes 589856 | tf_op jit(solution)/shard_map/all_to_all | solution.py:614
  27.4 3.1 %collective-permute-start = (bf16[16,512]{1,0:T(8,128)(2,1)S(1)}, bf16[16,512]{1,0:T(8,128)(2,1)S(1)}, u32[]{:S(2)}, u32[]{:S(2)}) collective-permute-start(bf16[16,512]{1,0:T(8,128)(2,1)S(1)} %slice_bitcast_fusion), channel_id=1, source_target_pairs={{0,16},{16,32},{32,48},{48,64},{64,80},{80,96},{96,112},{112,128},... | collective-permute-start | bytes 49160 | tf_op jit(solution)/shard_map/ppermute | solution.py:621
  31.4 1.8 shard_map.221
  33.1 20.5 %all_to_all.40.received = f32[4,264,128]{2,1,0:T(8,128)S(1)} all-to-all(f32[4,264,128]{2,1,0:T(8,128)S(1)} %get-tuple-element.56), channel_id=1, replica_groups={{0,16,32,48},{64,80,96,112},{128,144,160,176},{192,208,224,240},{256,27..., dimensions={0} | all-to-all | bytes 1081344 | tf_op jit(solution)/shard_map/all_to_all | solution.py:608
  53.6 1.8 shard_map.222
  55.4 6.9 %all-to-all-start.2 = ((f32[8,264,128]{2,1,0:T(8,128)}), f32[8,264,128]{2,1,0:T(8,128)S(1)}, u32[]{:S(2)}, u32[]{:S(2)}) async-start(f32[8,264,128]{2,1,0:T(8,128)} %get-tuple-element.57), calls=%async_computation.2 | async-start | bytes 2162688 | tf_op jit(solution)/shard_map/all_to_all | solution.py:611
  62.3 1.2 shard_map.223
  63.6 23.2 %all-to-all-done.2.received = f32[8,264,128]{2,1,0:T(8,128)S(1)} async-done(((f32[8,264,128]{2,1,0:T(8,128)}), f32[8,264,128]{2,1,0:T(8,128)S(1)}, u32[]{:S(2)}, u32[]{:S(2)}) %all-to-all-start.2) | async-done | bytes 1081376 | tf_op jit(solution)/shard_map/all_to_all | solution.py:611
  86.8 1.2 shard_map.224
  89.4 8.1 %psum.7.message = f32[8,256]{1,0:T(8,128)S(1)} all-reduce(f32[8,256]{1,0:T(8,128)S(1)} %get-tuple-element.63), channel_id=1, replica_groups={{0,1},{2,3},{4,5},{6,7},{8,9},{10,11},{12,13},{14,15},{16,17},{18,19},{..., use_global_device_ids=true, to_apply=%region_0.1 | all-reduce | flops 2048 | bytes 16384 | tf_op jit(solution)/shard_map/psum | solution.py:648
  98.3 1.4 shard_map.225
  101.7 17.8 %all_to_all.41.received = f32[4,264,128]{2,1,0:T(8,128)S(1)} all-to-all(f32[4,264,128]{2,1,0:T(8,128)S(1)} %get-tuple-element.65), channel_id=1, replica_groups={{0,16,32,48},{64,80,96,112},{128,144,160,176},{192,208,224,240},{256,27..., dimensions={0} | all-to-all | bytes 1081344 | tf_op jit(solution)/shard_map/all_to_all | solution.py:608
  119.5 1.8 shard_map.226
  122.0 3.6 %all-to-all-start.4 = ((f32[8,264,128]{2,1,0:T(8,128)}), f32[8,264,128]{2,1,0:T(8,128)S(1)}, u32[]{:S(2)}, u32[]{:S(2)}) async-start(f32[8,264,128]{2,1,0:T(8,128)} %get-tuple-element.66), calls=%async_computation.4 | async-start | bytes 2162688 | tf_op jit(solution)/shard_map/all_to_all | solution.py:611
  126.5 0.9 copy-done.5
  128.8 2.2 %shard_map.227 = (f32[256,256]{1,0:T(8,128)S(1)}, f32[256,128]{1,0:T(8,128)S(1)}, f32[256,128]{1,0:T(8,128)S(1)}, f32[256,128]{1,0:T(8,128)S(1)}, f32[256,128]{1...) custom-call(bf16[256,1152]{1,0:T(8,128)(2,1)S(1)} %bitcast.12, ...), custom_call_target="tpu_custom_call" | custom-call | flops 300000000 | bytes 4000000 | tf_op jit(solution)/shard_map/pallas_call | solution.py:657
  134.9 16.3 %all-to-all-done.4.received = f32[8,264,128]{2,1,0:T(8,128)S(1)} async-done(((f32[8,264,128]{2,1,0:T(8,128)}), f32[8,264,128]{2,1,0:T(8,128)S(1)}, u32[]{:S(2)}, u32[]{:S(2)}) %all-to-all-start.4) | async-done | bytes 1081376 | tf_op jit(solution)/shard_map/all_to_all | solution.py:611
  151.2 0.9 copy-done.1
  160.7 1.8 shard_map.228
  162.4 15.7 %all_to_all.42.received = f32[4,16,512]{2,1,0:T(8,128)S(1)} all-to-all(f32[4,16,512]{2,1,0:T(8,128)S(1)} %get-tuple-element.81), channel_id=1, replica_groups={{0,16,32,48},{64,80,96,112},{128,144,160,176},{192,208,224,240},{256,27..., dimensions={0} | all-to-all | bytes 262144 | tf_op jit(solution)/shard_map/all_to_all | solution.py:608
  178.8 11.8 %all_to_all.43.received = f32[8,16,512]{2,1,0:T(8,128)S(1)} all-to-all(f32[8,16,512]{2,1,0:T(8,128)S(1)} %get-tuple-element.82), channel_id=1, replica_groups={{0,64,128,192,256,320,384,448},{16,80,144,208,272,336,400,464},{32,96,1..., dimensions={0} | all-to-all | bytes 524288 | tf_op jit(solution)/shard_map/all_to_all | solution.py:611
  190.6 1.6 shard_map.230
  192.2 23.4 %all_to_all.44.received = bf16[16,16,1664]{2,1,0:T(8,128)(2,1)S(1)} all-to-all(bf16[16,16,1664]{2,1,0:T(8,128)(2,1)S(1)} %get-tuple-element.87), channel_id=1, replica_groups=mesh['ctx'=32,'head'=16] {'head'}, dimensions={0} | all-to-all | bytes 1703936 | tf_op jit(solution)/shard_map/all_to_all | solution.py:614
  (94 shorter events, 27.7 us)
Async XLA Ops:
  0.6 30.7 %copy-start.6 = (f32[4,1024]{1,0:T(4,128)S(1)}, f32[4,1024]{1,0:T(4,128)}, u32[]{:S(2)}) copy-start(f32[4,1024]{1,0:T(4,128)} %wb.5) | copy-start | bytes 49156
  0.7 30.7 %copy-start.7 = (f32[4,1024]{1,0:T(4,128)S(1)}, f32[4,1024]{1,0:T(4,128)}, u32[]{:S(2)}) copy-start(f32[4,1024]{1,0:T(4,128)} %wc.5) | copy-start | bytes 49156
  0.7 0.9 copy-start.18
  1.6 0.9 copy-start.19
  2.5 0.9 copy-start.20
  5.6 25.8 %copy-start.29 = (f32[4,256]{1,0:T(4,128)S(1)}, f32[4,256]{1,0:T(4,128)}, u32[]{:S(2)}) copy-start(f32[4,256]{1,0:T(4,128)} %wx.5) | copy-start | bytes 12292
  5.6 25.8 %copy-start.41 = (f32[4]{0:T(128)S(1)}, f32[4]{0:T(128)}, u32[]{:S(2)}) copy-start(f32[4]{0:T(128)} %alog.3) | copy-start | bytes 52
  5.6 25.8 %copy-start.43 = (f32[4]{0:T(128)S(1)}, f32[4]{0:T(128)}, u32[]{:S(2)}) copy-start(f32[4]{0:T(128)} %bias.3) | copy-start | bytes 52
  6.5 20.9 %all-to-all-start = ((bf16[16,16,1152]{2,1,0:T(8,128)(2,1)}), bf16[16,16,1152]{2,1,0:T(8,128)(2,1)S(1)}, u32[]{:S(2)}, u32[]{:S(2)}) async-start(bf16[16,16,1152]{2,1,0:T(8,128)(2,1)} %shard_map.220), calls=%async_computation | async-start | bytes 1179648 | tf_op jit(solution)/shard_map/all_to_all | solution.py:614
  27.4 3.9 %collective-permute-start = (bf16[16,512]{1,0:T(8,128)(2,1)S(1)}, bf16[16,512]{1,0:T(8,128)(2,1)S(1)}, u32[]{:S(2)}, u32[]{:S(2)}) collective-permute-start(bf16[16,512]{1,0:T(8,128)(2,1)S(1)} %slice_bitcast_fusion), channel_id=1, source_target_pairs={{0,16},{16,32},{32,48},{48,64},{64,80},{80,96},{96,112},{112,128},... | collective-permute-start | bytes 49160 | tf_op jit(solution)/shard_map/ppermute | solution.py:621
  30.6 88.9 %copy-start.26 = (s32[4]{0:T(128)}, s32[4]{0:T(128)S(1)}, u32[]{:S(2)}) copy-start(s32[4]{0:T(128)S(1)} %pad_add_fusion.where) | copy-start | bytes 52
  55.4 31.4 %copy-start.25 = (f32[4096]{0:T(1024)S(1)}, f32[4096]{0:T(1024)}, u32[]{:S(2)}) copy-start(f32[4096]{0:T(1024)} %param.25) | copy-start | bytes 49156
  55.4 31.4 %copy-start.39 = (f32[4]{0:T(128)S(1)}, f32[4]{0:T(128)}, u32[]{:S(2)}) copy-start(f32[4]{0:T(128)} %skip.3) | copy-start | bytes 52
  55.4 31.4 %all-to-all-start.2 = ((f32[8,264,128]{2,1,0:T(8,128)}), f32[8,264,128]{2,1,0:T(8,128)S(1)}, u32[]{:S(2)}, u32[]{:S(2)}) async-start(f32[8,264,128]{2,1,0:T(8,128)} %get-tuple-element.57), calls=%async_computation.2 | async-start | bytes 2162688 | tf_op jit(solution)/shard_map/all_to_all | solution.py:611
  97.4 0.9 copy-start.24
  122.0 29.2 %all-to-all-start.4 = ((f32[8,264,128]{2,1,0:T(8,128)}), f32[8,264,128]{2,1,0:T(8,128)S(1)}, u32[]{:S(2)}, u32[]{:S(2)}) async-start(f32[8,264,128]{2,1,0:T(8,128)} %get-tuple-element.66), calls=%async_computation.4 | async-start | bytes 2162688 | tf_op jit(solution)/shard_map/all_to_all | solution.py:611
  125.5 1.0 copy-start.3
  126.5 0.9 copy-start.5
  151.2 1.0 copy-start.1
  152.1 0.9 copy-start.9
  154.8 0.9 copy-start.15
  155.7 0.9 copy-start.17
  160.7 29.9 %copy-start.22 = (bf16[256,256]{1,0:T(8,128)(2,1)S(1)}, bf16[256,256]{1,0:T(8,128)(2,1)}, u32[]{:S(2)}) copy-start(bf16[256,256]{1,0:T(8,128)(2,1)} %copy-done.21) | copy-start | bytes 393220
  160.7 29.9 %copy-start.31 = (f32[4,256]{1,0:T(4,128)S(1)}, f32[4,256]{1,0:T(4,128)}, u32[]{:S(2)}) copy-start(f32[4,256]{1,0:T(4,128)} %wx.5) | copy-start | bytes 12292
  (25 other events, 17.3 us)

commit v2 on v1

--- a/solution.py
+++ b/solution.py
@@ -17,8 +17,8 @@
 KT = 4
 ROWS = 16
 IN_W = 1152
-OUT_W = 896
-VMEM_LIMIT = 48 * 1024 * 1024
+OUT_W = 1152
+VMEM_LIMIT = 16 * 1024 * 1024
 
 
 def dot(a, b, ca, cb):
@@ -74,11 +74,11 @@
     return dot_parts(wide, pick, 1, 0, 3)
 
 
-def scalar_row(ref, width, per):
+def scalar_row(ref, first, width, per):
     lane = iota((1, width), 1) // per
     row = jnp.zeros((1, width), F32)
     for e in range(HD):
-        row = jnp.where(lane == e, ref[e], row)
+        row = jnp.where(lane == e, ref[first + e], row)
     return row
 
 
@@ -252,14 +252,12 @@
     return total
 
 
-ZW = 4
-PACK = T + 8
-
-
 def call(kernel, out_shape, in_specs, out_specs=None, scratch=(), flops=0, bytes_accessed=0):
-    vmem = pl.BlockSpec(memory_space=pltpu.VMEM)
-    smem = pl.BlockSpec(memory_space=pltpu.SMEM)
-    place = {"v": vmem, "s": smem}
+    place = {
+        "v": pl.BlockSpec(memory_space=pltpu.VMEM),
+        "s": pl.BlockSpec(memory_space=pltpu.SMEM),
+        "h": pl.BlockSpec(memory_space=pltpu.HBM),
+    }
     return pl.pallas_call(
         kernel,
         out_shape=out_shape,
@@ -277,7 +275,17 @@
     return jax.ShapeDtypeStruct(shape, dtype)
 
 
-def pack_kernel(x, b, c, dt, gate, out_grad, out):
+def pack_kernel(x_at, b_at, c_at, dt_at, gate_at, grad_at, out, x, b, c, dt, gate, out_grad, sems):
+    moves = [
+        pltpu.make_async_copy(source, target, sems.at[i])
+        for i, (source, target) in enumerate(
+            [(x_at, x), (b_at, b), (c_at, c), (dt_at, dt), (gate_at, gate), (grad_at, out_grad)]
+        )
+    ]
+    for move in moves:
+        move.start()
+    for move in moves:
+        move.wait()
     ways = out.shape[0]
     per = GROUPS * N // ways
     wide_dt = jnp.concatenate(
@@ -301,11 +309,17 @@
     return ref[:, pl.ds(pl.multiple_of(where[1] * N, N), N)]
 
 
-def final_rows(final):
-    return jnp.broadcast_to(final, (8, 128))
-
-
-def enter_kernel(rows, halo, wx, wb, wc, alog, bias, where, xbc, step_out, cum_out, send, ext):
+def gain_lanes(ref, where):
+    return ref[:, pl.ds(pl.multiple_of(where[0] * CW, CW), CW)]
+
+
+def head_column(row):
+    return jnp.concatenate(
+        [jnp.broadcast_to(row[:, e : e + 1], (PS, 128)) for e in range(HD)], axis=0
+    )
+
+
+def enter_kernel(rows, halo, wx, wb, wc, head, where, xbc, step_out, cum_out, send, ext):
     ext[0:ROWS] = halo[...].astype(F32)
     ext[ROWS : ROWS + T] = rows[:, 0:512].astype(F32)
     x_act, b_act, c_act, step, cum, fresh, final = enter_math(
@@ -314,18 +328,17 @@
         wx[...],
         group_lanes(wb, where),
         group_lanes(wc, where),
-        scalar_row(bias, 128, 1),
-        scalar_row(alog, 128, 1),
+        scalar_row(head, HD, 128, 1),
+        scalar_row(head, 0, 128, 1),
     )
     xbc[:, 0:256] = x_act
     xbc[:, 256:384] = b_act
     xbc[:, 384:512] = c_act
     step_out[...] = step
     cum_out[...] = cum
-    tail = final_rows(final)
-    for i in range(send.shape[0]):
-        send[i, 0:T] = fresh
-        send[i, T:PACK] = tail
+    pieces_of = send.shape[0]
+    send[:, 0:8] = fresh.reshape(pieces_of, 8, 128)
+    send[:, 8:16] = head_column(final).reshape(pieces_of, 8, 128)
 
 
 def within_kernel(xbc, step, cum, inside, kept):
@@ -336,47 +349,20 @@
         kept[e] = mixes[e]
 
 
-def head_column(row):
-    return jnp.concatenate(
-        [jnp.broadcast_to(row[:, e : e + 1], (PS, 1)) for e in range(HD)], axis=0
-    )
-
-
-def chain(received, count, backward, mine):
-    state = jnp.zeros((T, 128), F32)
-    total = jnp.zeros((1, 128), F32)
-    kept_state, kept_total = state, total
-    for i in range(count):
-        at = count - 1 - i if backward else i
-        here = mine == at
-        kept_state = jnp.where(here, state, kept_state)
-        kept_total = jnp.where(here, total, kept_total)
-        log = received[at, T : T + 1, :]
-        state = head_column(jnp.exp(log)) * state + received[at, 0:T, :]
-        total = total + log
-    return kept_state, kept_total, state, total
-
-
-def near_kernel(backward, received, where, send, near):
-    kept_state, kept_total, state, total = chain(received, received.shape[0], backward, where[2])
-    near[0:T] = kept_state
-    near[T:PACK] = final_rows(kept_total)
-    tail = final_rows(total)
-    for i in range(send.shape[0]):
-        send[i, 0:T] = state
-        send[i, T:PACK] = tail
-
-
-def far_state(backward, received, near, mine):
-    count = received.shape[0]
-    state = jnp.zeros((T, 128), F32)
-    for i in range(count):
-        at = count - 1 - i if backward else i
-        log = received[at, T : T + 1, :]
-        longer = head_column(jnp.exp(log)) * state + received[at, 0:T, :]
-        use = (at > mine) if backward else (at < mine)
-        state = jnp.where(use, longer, state)
-    return head_column(jnp.exp(near[T : T + 1, :])) * state + near[0:T, :]
+def scan_kernel(received, send, decays):
+    state = jnp.zeros((8, 128), F32)
+    for i in range(received.shape[0]):
+        send[i] = state
+        decay = jnp.exp(received[i, 8:16])
+        decays[i] = decay
+        state = decay * state + received[i, 0:8]
+
+
+def scan_back_kernel(received, decays, send):
+    state = jnp.zeros((8, 128), F32)
+    for i in reversed(range(received.shape[0])):
+        send[i] = state
+        state = decays[i] * state + received[i]
 
 
 def pair_rows(squares, along):
@@ -385,31 +371,24 @@
     return both.T[0:8, :]
 
 
-def gain_lanes(ref, where):
-    return ref[:, pl.ds(pl.multiple_of(where[0] * CW, CW), CW)]
-
-
-def mix_kernel(received, near, xbc, inside, cum, rows, gain, skip, where, y_out, mixed_out, carried_out, message):
-    carried = far_state(False, received, near, where[3])
+def mix_kernel(carried, xbc, inside, cum, rows, gain, head, where, y_out, mixed_out, message):
     y, mixed, squares, along = mix_math(
         xbc[:, 0:256],
         xbc[:, 384:512],
         inside[...],
-        carried,
+        carried[...],
         cum[...],
-        scalar_row(skip, CW, PS),
+        scalar_row(head, 2 * HD, CW, PS),
         rows[:, 512:768].astype(F32),
         rows[:, 768:1024].astype(F32),
         gain_lanes(gain, where),
     )
     y_out[...] = y
     mixed_out[...] = mixed
-    carried_out[...] = carried
     message[...] = pair_rows(squares, along)
 
 
 def norm_kernel(message, mixed, rows, gain, xbc, cum, where, y_grad_out, gate_out, gain_out, lifted_out, send):
-    cum = cum[...]
     sums = jnp.concatenate([message[...], jnp.zeros((120, T), F32)], axis=0).T
     y_grad, gate_grad, gain_grad, lifted, start_grad = norm_math(
         mixed[...],
@@ -419,16 +398,13 @@
         sums[:, 0:1],
         sums[:, 1:2],
         xbc[:, 384:512],
-        cum,
+        cum[...],
     )
     y_grad_out[...] = y_grad
     gate_out[...] = gate_grad
     gain_out[...] = jnp.broadcast_to(gain_grad, (8, CW))
     lifted_out[...] = lifted
-    tail = final_rows(cum[T - 1 : T, :])
-    for i in range(send.shape[0]):
-        send[i, 0:T] = start_grad
-        send[i, T:PACK] = tail
+    send[...] = start_grad.reshape(send.shape)
 
 
 def back_kernel(
@@ -463,88 +439,73 @@
 
 
 def leave_kernel(
-    received, near, rows, halo, where, alog, bias, skip, xbc, step, cum, y_grad, x_in, b_in,
-    c_grad, out_dots, in_dots, carried, gain_grad, skip_grad, slopes,
-    pre_out, dt_out, send, ext,
+    end_grad, rows, halo, head, xbc, step, cum, y_grad, x_in, b_in, c_grad, out_dots, in_dots,
+    carried, gain_grad, skip_grad, slopes, pre_out, dt_out, rim, send, ext,
 ):
     ext[0:ROWS] = halo[...].astype(F32)
     ext[ROWS : ROWS + T] = rows[:, 0:512].astype(F32)
-    end_grad = far_state(True, received, near, where[3])
-    alog_row = scalar_row(alog, 128, 1)
+    alog_row = scalar_row(head, 0, 128, 1)
     step = step[...]
     x_grad, b_grad, dt_grad, alog_grad, bias_grad = leave_math(
         xbc[:, 0:256],
         xbc[:, 256:384],
         step,
         cum[...],
-        rows[:, 1024:1152].astype(F32) + scalar_row(bias, 128, 1),
+        rows[:, 1024:1152].astype(F32) + scalar_row(head, HD, 128, 1),
         -jnp.exp(alog_row) * step,
         alog_row,
-        scalar_row(skip, CW, PS),
+        scalar_row(head, 2 * HD, CW, PS),
         y_grad[...],
         x_in[...],
         b_in[...],
         out_dots[...],
         in_dots[...],
         carried[...],
-        end_grad,
+        end_grad[...],
     )
     dt_out[...] = dt_grad
     pre = jnp.concatenate([x_grad, b_grad, c_grad[...]], axis=1) * slopes[...]
     pre_out[...] = pre
-    weights = weight_grads(ext, pre)
+    rim[...] = pre[0:8]
+    weights = jnp.concatenate(weight_grads(ext, pre), axis=0)
     block = jnp.concatenate(
-        weights
-        + [
-            jnp.concatenate([gain_grad[0:1, :], skip_grad[0:1, :]], axis=1),
-            jnp.concatenate([alog_grad, bias_grad, jnp.zeros((1, 256), F32)], axis=1),
-            jnp.zeros((2, 512), F32),
-            pre[0:8, :],
-        ],
+        [weights[:, i * 128 : (i + 1) * 128] for i in range(4)]
+        + [gain_grad[0:1, 0:128], gain_grad[0:1, 128:256]]
+        + [skip_grad[0:1, 0:128], skip_grad[0:1, 128:256]]
+        + [alog_grad, bias_grad, jnp.zeros((2, 128), F32)],
         axis=0,
     )
     for i in range(send.shape[0]):
         send[i] = block
 
 
-def near_sum_kernel(received, where, send, halo):
-    ways = received.shape[0]
-    mine = where[2]
-    total = received[0, 0:8, :]
-    for i in range(1, ways):
-        total = total + received[i, 0:8, :]
-    following = jnp.zeros((8, 512), F32)
-    for i in range(1, ways):
-        following = jnp.where(mine == i - 1, received[i, 8:16, :], following)
-    halo[...] = following
-    first = received[0, 8:16, :]
-    for i in range(send.shape[0]):
-        send[i, 0:8] = total
-        send[i, 8:16] = first
-
-
-def finish_kernel(received, near_halo, where, wx, wb, wc, pre, dt_grad, gate_grad, send, conv_x_out, alog_out, bias_out, skip_out, ext):
-    ways = received.shape[0]
-    total = received[0, 0:8, :]
-    for i in range(1, ways):
-        total = total + received[i, 0:8, :]
-    following = jnp.zeros((8, 512), F32)
-    for i in range(1, ways):
-        following = jnp.where(where[3] == i - 1, received[i, 8:16, :], following)
-    following = jnp.where(where[2] == ZW - 1, following, near_halo[...])
+def finish_kernel(received, following, where, wx, wb, wc, pre, dt_grad, gate_grad, send, conv_x_out, alog_out, bias_out, skip_out, ext):
+    total = received[0]
+    for i in range(1, received.shape[0]):
+        total = total + received[i]
     ext[0:T] = pre[...]
-    ext[T : T + 8] = following
+    ext[T : T + 8] = following[...]
     x_grad = conv_back(ext, wx[...], 0, 256).astype(BF)
     b_grad = conv_back(ext, group_lanes(wb, where), 256, 384).astype(BF)
     c_grad = conv_back(ext, group_lanes(wc, where), 384, 512).astype(BF)
-    conv_x_out[...] = total[0:KT, 0:CW]
+    conv_x_out[...] = jnp.concatenate([total[0:4], total[4:8]], axis=1)
     for e in range(HD):
-        alog_out[e] = jnp.sum(total[5:6, e : e + 1])
-        bias_out[e] = jnp.sum(total[5:6, 128 + e : 129 + e])
-        skip_out[e] = jnp.sum(total[4:5, CW + e * PS : CW + (e + 1) * PS])
-    shared = jnp.concatenate([total[0:5, 256:512], jnp.zeros((11, 256), F32)], axis=0)
-    shared = jnp.where(iota((16, 256), 0) == 4, jnp.broadcast_to(total[4:5, 0:256], (16, 256)), shared)
-    high, middle, low = pieces(shared, 3)
+        at = 18 + e // 2
+        cut = slice((e % 2) * PS, (e % 2 + 1) * PS)
+        alog_out[e] = jnp.sum(total[20:21, e : e + 1])
+        bias_out[e] = jnp.sum(total[21:22, e : e + 1])
+        skip_out[e] = jnp.sum(total[at : at + 1, cut])
+    shared = jnp.concatenate(
+        [
+            jnp.concatenate([total[8:12], total[12:16]], axis=1),
+            jnp.concatenate([total[16:17], total[17:18]], axis=1),
+        ],
+        axis=0,
+    )
+    high = shared.astype(BF).astype(F32)
+    middle = (shared - high).astype(BF).astype(F32)
+    low = shared - high - middle
+    shared = jnp.concatenate([high, middle, low, jnp.zeros((1, 256), F32)], axis=0).astype(BF)
     dt_low = dt_grad[...].astype(BF)
     for j in range(send.shape[0]):
         cut = slice(j * ROWS, (j + 1) * ROWS)
@@ -553,9 +514,7 @@
         send[j, :, 384:512] = c_grad[cut]
         send[j, :, 512:768] = gate_grad[cut, :]
         send[j, :, 768:896] = dt_low[cut]
-        send[j, :, 896:1152] = high
-        send[j, :, 1152:1408] = middle
-        send[j, :, 1408:1664] = low
+        send[j, :, 896:1152] = shared
 
 
 def unpack_kernel(received, x_out, b_out, c_out, dt_out, gate_out, conv_b_out, conv_c_out, gain_out):
@@ -569,11 +528,8 @@
         gate_out[:, own] = received[j, :, 512:768]
         turned = pltpu.roll(received[j, :, 768:896].astype(F32), HD * j, 1)
         dt = jnp.where(lane // HD == j, turned, dt)
-        shared.append(
-            received[j, :, 896:1152].astype(F32)
-            + received[j, :, 1152:1408].astype(F32)
-            + received[j, :, 1408:1664].astype(F32)
-        )
+        three = received[j, :, 896:1152].astype(F32)
+        shared.append(three[0:5] + three[5:10] + three[10:15])
         gain_out[:, own] = shared[j][4:5, :]
     dt_out[...] = dt[:, 0 : dt_out.shape[1]].astype(BF)
     per = ways // GROUPS
@@ -595,27 +551,24 @@
 ):
     ways = lax.axis_size("head")
     blocks = lax.axis_size("ctx")
-    far = blocks // ZW
-    near_groups = [[y * ZW + z for z in range(ZW)] for y in range(far)]
-    far_groups = [[y * ZW + z for y in range(far)] for z in range(ZW)]
-    head_at, ctx_at = lax.axis_index("head"), lax.axis_index("ctx")
-    where = jnp.stack(
-        [head_at, head_at * GROUPS // ways, ctx_at % ZW, ctx_at // ZW]
-    ).astype(jnp.int32)
+    head_at = lax.axis_index("head")
+    where = jnp.stack([head_at, (head_at * GROUPS) // ways]).astype(jnp.int32)
+    head = jnp.concatenate([a_log, dt_bias, d_skip])
     gain = norm_gain.reshape(1, -1)
 
-    def near_swap(value):
-        return lax.all_to_all(value, "ctx", 0, 0, axis_index_groups=near_groups)
-
-    def far_swap(value):
-        return lax.all_to_all(value, "ctx", 0, 0, axis_index_groups=far_groups)
+    def ctx_swap(value):
+        return lax.all_to_all(value, "ctx", 0, 0, tiled=True)
 
     def head_swap(value):
         return lax.all_to_all(value, "head", 0, 0, tiled=True)
 
-    sent = call(pack_kernel, [sds((ways, ROWS, IN_W), BF)], "vvvvvv")(
-        x_in, b_in, c_in, dt_in, gate_in, out_grad
-    )[0]
+    inputs = (x_in, b_in, c_in, dt_in, gate_in, out_grad)
+    sent = call(
+        pack_kernel,
+        [sds((ways, ROWS, IN_W), BF)],
+        "hhhhhh",
+        scratch=[pltpu.VMEM(a.shape, a.dtype) for a in inputs] + [pltpu.SemaphoreType.DMA((6,))],
+    )(*inputs)[0]
     arrived = head_swap(sent)
     rows = arrived.reshape(T, IN_W)
     halo = lax.ppermute(
@@ -623,37 +576,34 @@
     )
     wide = sds((T, CW), F32)
     slim = sds((T, 128), F32)
-    message = sds((ZW, PACK, 128), F32)
-    far_message = sds((far, PACK, 128), F32)
-    near_part = sds((PACK, 128), F32)
+    chunk = sds((blocks, T // blocks, 128), F32)
     ext = pltpu.VMEM((ROWS + T, 512), F32)
 
     xbc, step, cum, send = call(
-        enter_kernel, [sds((T, 512), BF), slim, slim, message], "vvvvvsss", scratch=[ext]
-    )(rows, halo, conv_x, conv_b, conv_c, a_log, dt_bias, where)
-    received = near_swap(send)
+        enter_kernel,
+        [sds((T, 512), BF), slim, slim, sds((blocks, 2 * T // blocks, 128), F32)],
+        "vvvvvss",
+        scratch=[ext],
+    )(rows, halo, conv_x, conv_b, conv_c, head, where)
+    received = ctx_swap(send)
     inside, kept = call(
         within_kernel, [wide, sds((HD, T, T), BF)], "vvv", flops=10**8, bytes_accessed=2 * 10**6
     )(xbc, step, cum)
-    send, near = call(functools.partial(near_kernel, False), [far_message, near_part], "vs")(
-        received, where
-    )
-    received = far_swap(send)
-    y, mixed, carried, sums = call(
-        mix_kernel,
-        [wide, sds((T, CW), BF), slim, sds((8, T), F32)],
-        "vvvvvvvss",
-    )(received, near, xbc, inside, cum, rows, gain, d_skip, where)
+    send, decays = call(scan_kernel, [chunk, chunk], "v")(received)
+    carried = ctx_swap(send).reshape(T, 128)
+    y, mixed, sums = call(
+        mix_kernel, [wide, sds((T, CW), BF), sds((8, T), F32)], "vvvvvvss"
+    )(carried, xbc, inside, cum, rows, gain, head, where)
     per = ways // GROUPS
     sums = lax.psum(
         sums, "head", axis_index_groups=[[g * per + i for i in range(per)] for g in range(GROUPS)]
     )
     y_grad, gate_grad, gain_grad, lifted, send = call(
         norm_kernel,
-        [sds((T, CW), BF), sds((T, CW), BF), sds((8, CW), F32), wide, message],
+        [sds((T, CW), BF), sds((T, CW), BF), sds((8, CW), F32), wide, chunk],
         "vvvvvvs",
     )(sums, mixed, rows, gain, xbc, cum, where)
-    received = near_swap(send)
+    received = ctx_swap(send)
     x_part, b_part, c_grad, out_dots, in_dots, skip_grad, slopes = call(
         back_kernel,
         [wide, slim, slim, slim, slim, sds((8, CW), F32), sds((T, 512), F32)],
@@ -662,41 +612,35 @@
         flops=3 * 10**8,
         bytes_accessed=4 * 10**6,
     )(rows, halo, conv_x, conv_b, conv_c, where, xbc, step, cum, kept, y, y_grad, lifted, carried)
-    send, near = call(functools.partial(near_kernel, True), [far_message, near_part], "vs")(
-        received, where
-    )
-    received = far_swap(send)
-    pre, dt_grad, send = call(
+    send = call(scan_back_kernel, [chunk], "vv")(received, decays)[0]
+    end_grad = ctx_swap(send).reshape(T, 128)
+    pre, dt_grad, rim, send = call(
         leave_kernel,
-        [sds((T, 512), F32), slim, sds((ZW, 16, 512), F32)],
-        "vvvvssss" + "v" * 13,
+        [sds((T, 512), F32), slim, sds((8, 512), F32), sds((blocks, 24, 128), F32)],
+        "vvvs" + "v" * 13,
         scratch=[ext],
     )(
-        received, near, rows, halo, where, a_log, dt_bias, d_skip, xbc, step, cum, y_grad, x_part,
-        b_part, c_grad, out_dots, in_dots, carried, gain_grad, skip_grad, slopes,
-    )
-    received = near_swap(send)
-    send, near_halo = call(
-        near_sum_kernel, [sds((far, 16, 512), F32), sds((8, 512), F32)], "vs"
-    )(received, where)
-    received = far_swap(send)
+        end_grad, rows, halo, head, xbc, step, cum, y_grad, x_part, b_part, c_grad, out_dots,
+        in_dots, carried, gain_grad, skip_grad, slopes,
+    )
+    following = lax.ppermute(rim, "ctx", [(i + 1, i) for i in range(blocks - 1)])
+    received = ctx_swap(send)
     four = sds((HD,), F32)
     send, conv_x_grad, alog_grad, bias_grad, skip_sum = call(
         finish_kernel,
-        [sds((ways, ROWS, 1664), BF), sds((KT, CW), F32), four, four, four],
+        [sds((ways, ROWS, OUT_W), BF), sds((KT, CW), F32), four, four, four],
         "vvsvvvvvv",
         "vvsss",
         scratch=[pltpu.VMEM((T + 8, 512), F32)],
-    )(received, near_halo, where, conv_x, conv_b, conv_c, pre, dt_grad, gate_grad)
+    )(received, following, where, conv_x, conv_b, conv_c, pre, dt_grad, gate_grad)
     received = head_swap(send)
-    heads = dt_in.shape[1]
     x_grad, b_grad, c_grad, dt_out, gate_out, conv_b_grad, conv_c_grad, gain_sum = call(
         unpack_kernel,
         [
             sds(x_in.shape, BF),
             sds(b_in.shape, BF),
             sds(c_in.shape, BF),
-            sds((ROWS, heads), BF),
+            sds(dt_in.shape, BF),
             sds(gate_in.shape, BF),
             sds(conv_b.shape, F32),
             sds(conv_c.shape, F32),

time: 217 us -> 162 us (0.75)
  blocking collectives: 97.3 us -> 65.1 us
  local copies, waits for them, and re-layouts: 26.5 us -> 11.1 us
  waiting for transfers between devices: 50.9 us -> 40 us
  starting transfers between devices: 23.8 us -> 28.5 us
    all_to_all x4 -> x2, blocking collectives: 65.9 us -> 40.5 us  [ctx_swap(): return lax.all_to_all(value, 'ctx', 0, 0, tiled=True)]
    unnamed x90 -> x42, local copies, waits for them, and re-layouts: 26.5 us -> 11.1 us
    all_to_all x2 -> x3, waiting for transfers between devices: 39.5 us -> 24.4 us  [ctx_swap(): return lax.all_to_all(value, 'ctx', 0, 0, tiled=True)]
    all_to_all x1, blocking collectives: 23.4 us -> 17.7 us  [head_swap(): return lax.all_to_all(value, 'head', 0, 0, tiled=True)]
    ppermute x0 -> x1, waiting for transfers between devices: none -> 4.35 us  [per_device(): lax.ppermute(rim, 'ctx', [(i + 1, i) for i in range(blocks - 1)])]
    all_to_all x2 -> x3, starting transfers between devices: 10.5 us -> 13.9 us  [ctx_swap(): return lax.all_to_all(value, 'ctx', 0, 0, tiled=True)]
    pallas_call x8 -> x7, Pallas kernels: 11.4 us -> 9.57 us  [the longest x1 2.28 us: per_device(): call(leave_kernel, [sds((T, 512), F32), slim, sds((8, 512), F32), sds((bl...]
  transfers between devices with their start and end apart: 4 -> 6, of which waited for: 4 -> 6; matrix products, arithmetic and copies ran while one was open for 0% -> 0% of each run, Pallas kernels for 2% -> 2%
where the time goes in v2:
time: 162 us; the launch traced here: 161 us
  blocking collectives  65.1 us (40%)
  waiting for transfers between devices  40 us (25%)
  starting transfers between devices  28.5 us (18%)
  Pallas kernels  15.1 us (9%)
  local copies, waits for them, and re-layouts  11.1 us (7%)
    all_to_all x2, blocking collectives, ctx_swap(): return lax.all_to_all(value, 'ctx', 0, 0, tiled=True)  40.5 us
    all_to_all x3, waiting for transfers between devices, ctx_swap(): return lax.all_to_all(value, 'ctx', 0, 0, tiled=True)  24.4 us
    all_to_all x1, blocking collectives, head_swap(): return lax.all_to_all(value, 'head', 0, 0, tiled=True)  17.7 us
    all_to_all x3, starting transfers between devices, ctx_swap(): return lax.all_to_all(value, 'ctx', 0, 0, tiled=True)  13.9 us
    unnamed x42, local copies, waits for them, and re-layouts  11.1 us
    all_to_all x1, waiting for transfers between devices, head_swap(): return lax.all_to_all(value, 'head', 0, 0, tiled=True)  10.5 us
    all_to_all x1, starting transfers between devices, head_swap(): return lax.all_to_all(value, 'head', 0, 0, tiled=True)  10.3 us
    psum x1, blocking collectives, per_device(): lax.psum(sums, 'head', axis_index_groups=[[g * per + i for i in range(per...  6.88 us
  transfers between devices with their start and end apart: 6, of which 6 were waited for; matrix products, arithmetic and copies ran while one was open for 0% of the time, Pallas kernels for 2%

profile of v2, /device:TPU:1, one launch (start us, length us, event | category | flops | bytes accessed | tf_op | source)
XLA Modules:
  0.0 160.9 jit_solution(10303391491550013792)
XLA Ops:
  5.6 1.5 shard_map.220
  7.1 10.3 %all-to-all-start = ((bf16[16,16,1152]{2,1,0:T(8,128)(2,1)}), bf16[16,16,1152]{2,1,0:T(8,128)(2,1)S(1)}, u32[]{:S(2)}, u32[]{:S(2)}) async-start(bf16[16,16,1152]{2,1,0:T(8,128)(2,1)} %shard_map.220), calls=%async_computation | async-start | bytes 1179648 | tf_op jit(solution)/shard_map/all_to_all | solution.py:563
  17.5 10.5 %all-to-all-done = bf16[16,16,1152]{2,1,0:T(8,128)(2,1)S(1)} async-done(((bf16[16,16,1152]{2,1,0:T(8,128)(2,1)}), bf16[16,16,1152]{2,1,0:T(8,128)(2,1)S(1)}, u32[]{:S(2)}, u32[]{:S(2)}) %all-to-all-start) | async-done | bytes 589856 | tf_op jit(solution)/shard_map/all_to_all | solution.py:563
  28.0 3.1 %collective-permute-start = (bf16[16,512]{1,0:T(8,128)(2,1)S(1)}, bf16[16,512]{1,0:T(8,128)(2,1)S(1)}, u32[]{:S(2)}, u32[]{:S(2)}) collective-permute-start(bf16[16,512]{1,0:T(8,128)(2,1)S(1)} %slice_bitcast_fusion), channel_id=1, source_target_pairs={{0,16},{16,32},{32,48},{48,64},{64,80},{80,96},{96,112},{112,128},... | collective-permute-start | bytes 49160 | tf_op jit(solution)/shard_map/ppermute | solution.py:574
  31.9 1.7 %shard_map.221 = (bf16[256,512]{1,0:T(8,128)(2,1)S(1)}, f32[256,128]{1,0:T(8,128)S(1)}, f32[256,128]{1,0:T(8,128)S(1)}, f32[32,16,128]{2,1,0:T(8,128)S(1)}) custom-call(bf16[256,1152]{1,0:T(8,128)(2,1)S(1)} %bitcast.9, bf16[16,512]{1,0:T(8,128)(2,1)S(1)} %collective-permute-done.halo, f32[4,256]{1,0:T(4,128)S(1)} %copy-done.14, f32[4,1024]{1,0:T(4,128)S(1)} %copy-done, ...), custom_call_target="tpu_custom_call" | custom-call | tf_op jit(solution)/shard_map/pallas_call | solution.py:582
  33.7 26.2 %all_to_all.35.received = f32[32,16,128]{2,1,0:T(8,128)S(1)} all-to-all(f32[32,16,128]{2,1,0:T(8,128)S(1)} %get-tuple-element.52), channel_id=1, replica_groups=mesh['ctx'=32,'head'=16] {'ctx'}, dimensions={0} | all-to-all | bytes 524288 | tf_op jit(solution)/shard_map/all_to_all | solution.py:560
  60.6 4.5 %all-to-all-start.2 = ((f32[32,8,128]{2,1,0:T(8,128)}), f32[32,8,128]{2,1,0:T(8,128)S(1)}, u32[]{:S(2)}, u32[]{:S(2)}) async-start(f32[32,8,128]{2,1,0:T(8,128)} %get-tuple-element.53), calls=%async_computation.2 | async-start | bytes 262144 | tf_op jit(solution)/shard_map/all_to_all | solution.py:560
  65.2 1.2 shard_map.223
  66.4 10.1 %all-to-all-done.2 = f32[32,8,128]{2,1,0:T(8,128)S(1)} async-done(((f32[32,8,128]{2,1,0:T(8,128)}), f32[32,8,128]{2,1,0:T(8,128)S(1)}, u32[]{:S(2)}, u32[]{:S(2)}) %all-to-all-start.2) | async-done | bytes 131104 | tf_op jit(solution)/shard_map/all_to_all | solution.py:560
  76.4 1.0 shard_map.224
  77.4 6.9 %psum.7.message = f32[8,256]{1,0:T(8,128)S(1)} all-reduce(f32[8,256]{1,0:T(8,128)S(1)} %get-tuple-element.58), channel_id=1, replica_groups={{0,1},{2,3},{4,5},{6,7},{8,9},{10,11},{12,13},{14,15},{16,17},{18,19},{..., use_global_device_ids=true, to_apply=%region_0.1 | all-reduce | flops 2048 | bytes 16384 | tf_op jit(solution)/shard_map/psum | solution.py:598
  84.3 1.4 shard_map.225
  85.7 14.3 %all_to_all.36.received = f32[32,8,128]{2,1,0:T(8,128)S(1)} all-to-all(f32[32,8,128]{2,1,0:T(8,128)S(1)} %get-tuple-element.60), channel_id=1, replica_groups=mesh['ctx'=32,'head'=16] {'ctx'}, dimensions={0} | all-to-all | bytes 262144 | tf_op jit(solution)/shard_map/all_to_all | solution.py:560
  100.7 4.3 %all-to-all-start.4 = ((f32[32,8,128]{2,1,0:T(8,128)}), f32[32,8,128]{2,1,0:T(8,128)S(1)}, u32[]{:S(2)}, u32[]{:S(2)}) async-start(f32[32,8,128]{2,1,0:T(8,128)} %shard_map.226), calls=%async_computation.4 | async-start | bytes 262144 | tf_op jit(solution)/shard_map/all_to_all | solution.py:560
  105.0 2.2 %shard_map.227 = (f32[256,256]{1,0:T(8,128)S(1)}, f32[256,128]{1,0:T(8,128)S(1)}, f32[256,128]{1,0:T(8,128)S(1)}, f32[256,128]{1,0:T(8,128)S(1)}, f32[256,128]{1...) custom-call(bf16[256,1152]{1,0:T(8,128)(2,1)S(1)} %bitcast.12, ...), custom_call_target="tpu_custom_call" | custom-call | flops 300000000 | bytes 4000000 | tf_op jit(solution)/shard_map/pallas_call | solution.py:607
  109.8 6.6 %all-to-all-done.4 = f32[32,8,128]{2,1,0:T(8,128)S(1)} async-done(((f32[32,8,128]{2,1,0:T(8,128)}), f32[32,8,128]{2,1,0:T(8,128)S(1)}, u32[]{:S(2)}, u32[]{:S(2)}) %all-to-all-start.4) | async-done | bytes 131104 | tf_op jit(solution)/shard_map/all_to_all | solution.py:560
  116.4 0.9 copy-done.3
  120.0 2.3 %shard_map.228 = (f32[256,512]{1,0:T(8,128)S(1)}, f32[256,128]{1,0:T(8,128)S(1)}, f32[8,512]{1,0:T(8,128)S(1)}, f32[32,24,128]{2,1,0:T(8,128)}) custom-call(f32[256,128]{1,0:T(8,128)S(1)} %bitcast.17, bf16[256,1152]{1,0:T(8,128)(2,1)S(1)} %bitcast.13, bf16[16,512]{1,0:T(8,128)(2,1)S(1)} %collective-permute-done.halo, f32[12]{0:T(128)S(1)} %pad_maximum_fusion.head, ...), custom_call_target="tpu_custom_call" | custom-call | tf_op jit(solution)/shard_map/pallas_call | solution.py:617
  122.3 5.0 %all-to-all-start.5 = ((f32[32,24,128]{2,1,0:T(8,128)}), f32[32,24,128]{2,1,0:T(8,128)S(1)}, u32[]{:S(2)}, u32[]{:S(2)}) async-start(f32[32,24,128]{2,1,0:T(8,128)} %get-tuple-element.74), calls=%async_computation.5 | async-start | bytes 786432 | tf_op jit(solution)/shard_map/all_to_all | solution.py:560
  127.3 1.3 collective-permute-start.1
  128.6 4.4 %collective-permute-done.1.following = f32[8,512]{1,0:T(8,128)S(1)} collective-permute-done((f32[8,512]{1,0:T(8,128)S(1)}, f32[8,512]{1,0:T(8,128)S(1)}, u32[]{:S(2)}, u32[]{:S(2)}) %collective-permute-start.1) | collective-permute-done | bytes 16416 | tf_op jit(solution)/shard_map/ppermute | solution.py:626
  133.0 7.8 %all-to-all-done.5.received = f32[32,24,128]{2,1,0:T(8,128)S(1)} async-done(((f32[32,24,128]{2,1,0:T(8,128)}), f32[32,24,128]{2,1,0:T(8,128)S(1)}, u32[]{:S(2)}, u32[]{:S(2)}) %all-to-all-start.5) | async-done | bytes 393248 | tf_op jit(solution)/shard_map/all_to_all | solution.py:560
  140.8 1.6 %shard_map.229 = (bf16[16,16,1152]{2,1,0:T(8,128)(2,1)S(1)}, f32[4,256]{1,0:T(4,128)}, f32[4]{0:T(128)}, f32[4]{0:T(128)}, f32[4]{0:T(128)}) custom-call(f32[32,24,128]{2,1,0:T(8,128)S(1)} %all-to-all-done.5.received, f32[8,512]{1,0:T(8,128)S(1)} %collective-permute-done.1.following, s32[2]{0:T(128)S(1)} %pad_add_fusion.where, f32[4,256]{1,0:T(4,128)S(1)} %copy-done.14, ...), custom_call_target="tpu_custom_call" | custom-call | tf_op jit(solution)/shard_map/pallas_call | solution.py:629
  142.4 17.7 %all_to_all.37.received = bf16[16,16,1152]{2,1,0:T(8,128)(2,1)S(1)} all-to-all(bf16[16,16,1152]{2,1,0:T(8,128)(2,1)S(1)} %get-tuple-element.79), channel_id=1, replica_groups=mesh['ctx'=32,'head'=16] {'head'}, dimensions={0} | all-to-all | bytes 1179648 | tf_op jit(solution)/shard_map/all_to_all | solution.py:563
  (48 shorter events, 13.4 us)
Async XLA Ops:
  0.6 0.9 copy-start.10
  1.6 0.9 copy-start.11
  2.5 0.9 copy-start.12
  3.4 0.8 copy-start.15
  4.1 0.8 copy-start.16
  4.9 0.7 copy-start.17
  7.1 20.9 %all-to-all-start = ((bf16[16,16,1152]{2,1,0:T(8,128)(2,1)}), bf16[16,16,1152]{2,1,0:T(8,128)(2,1)S(1)}, u32[]{:S(2)}, u32[]{:S(2)}) async-start(bf16[16,16,1152]{2,1,0:T(8,128)(2,1)} %shard_map.220), calls=%async_computation | async-start | bytes 1179648 | tf_op jit(solution)/shard_map/all_to_all | solution.py:563
  17.4 13.7 %copy-start.18 = (f32[4]{0:T(128)S(1)}, f32[4]{0:T(128)}, u32[]{:S(2)}) copy-start(f32[4]{0:T(128)} %param.24) | copy-start | bytes 52
  17.4 13.7 %copy-start.19 = (f32[4]{0:T(128)S(1)}, f32[4]{0:T(128)}, u32[]{:S(2)}) copy-start(f32[4]{0:T(128)} %param.23) | copy-start | bytes 52
  17.4 13.7 %copy-start.20 = (f32[4]{0:T(128)S(1)}, f32[4]{0:T(128)}, u32[]{:S(2)}) copy-start(f32[4]{0:T(128)} %param.22) | copy-start | bytes 52
  17.4 14.5 %copy-start.14 = (f32[4,256]{1,0:T(4,128)S(1)}, f32[4,256]{1,0:T(4,128)}, u32[]{:S(2)}) copy-start(f32[4,256]{1,0:T(4,128)} %wx.5) | copy-start | bytes 12292
  17.5 14.5 %copy-start = (f32[4,1024]{1,0:T(4,128)S(1)}, f32[4,1024]{1,0:T(4,128)}, u32[]{:S(2)}) copy-start(f32[4,1024]{1,0:T(4,128)} %wb.5) | copy-start | bytes 49156
  17.5 14.5 %copy-start.1 = (f32[4,1024]{1,0:T(4,128)S(1)}, f32[4,1024]{1,0:T(4,128)}, u32[]{:S(2)}) copy-start(f32[4,1024]{1,0:T(4,128)} %wc.5) | copy-start | bytes 49156
  28.0 3.9 %collective-permute-start = (bf16[16,512]{1,0:T(8,128)(2,1)S(1)}, bf16[16,512]{1,0:T(8,128)(2,1)S(1)}, u32[]{:S(2)}, u32[]{:S(2)}) collective-permute-start(bf16[16,512]{1,0:T(8,128)(2,1)S(1)} %slice_bitcast_fusion), channel_id=1, source_target_pairs={{0,16},{16,32},{32,48},{48,64},{64,80},{80,96},{96,112},{112,128},... | collective-permute-start | bytes 49160 | tf_op jit(solution)/shard_map/ppermute | solution.py:574
  60.6 15.8 %all-to-all-start.2 = ((f32[32,8,128]{2,1,0:T(8,128)}), f32[32,8,128]{2,1,0:T(8,128)S(1)}, u32[]{:S(2)}, u32[]{:S(2)}) async-start(f32[32,8,128]{2,1,0:T(8,128)} %get-tuple-element.53), calls=%async_computation.2 | async-start | bytes 262144 | tf_op jit(solution)/shard_map/all_to_all | solution.py:560
  65.1 11.3 %copy-start.13 = (f32[4096]{0:T(1024)S(1)}, f32[4096]{0:T(1024)}, u32[]{:S(2)}) copy-start(f32[4096]{0:T(1024)} %param.25) | copy-start | bytes 49156
  100.7 15.7 %all-to-all-start.4 = ((f32[32,8,128]{2,1,0:T(8,128)}), f32[32,8,128]{2,1,0:T(8,128)S(1)}, u32[]{:S(2)}, u32[]{:S(2)}) async-start(f32[32,8,128]{2,1,0:T(8,128)} %shard_map.226), calls=%async_computation.4 | async-start | bytes 262144 | tf_op jit(solution)/shard_map/all_to_all | solution.py:560
  107.2 0.7 copy-start.2
  116.4 0.9 copy-start.3
  117.3 0.9 copy-start.5
  118.2 0.9 copy-start.7
  119.1 0.9 copy-start.9
  122.3 18.5 %all-to-all-start.5 = ((f32[32,24,128]{2,1,0:T(8,128)}), f32[32,24,128]{2,1,0:T(8,128)S(1)}, u32[]{:S(2)}, u32[]{:S(2)}) async-start(f32[32,24,128]{2,1,0:T(8,128)} %get-tuple-element.74), calls=%async_computation.5 | async-start | bytes 786432 | tf_op jit(solution)/shard_map/all_to_all | solution.py:560
  127.3 5.7 %collective-permute-start.1 = (f32[8,512]{1,0:T(8,128)S(1)}, f32[8,512]{1,0:T(8,128)S(1)}, u32[]{:S(2)}, u32[]{:S(2)}) collective-permute-start(f32[8,512]{1,0:T(8,128)S(1)} %get-tuple-element.75), channel_id=1, source_target_pairs={{16,0},{32,16},{48,32},{64,48},{80,64},{96,80},{112,96},{128,112},... | collective-permute-start | bytes 49160 | tf_op jit(solution)/shard_map/ppermute | solution.py:626
  (3 other events, 1.9 us)

commit v3 on v2

--- a/solution.py
+++ b/solution.py
@@ -18,7 +18,8 @@
 ROWS = 16
 IN_W = 1152
 OUT_W = 1152
-VMEM_LIMIT = 16 * 1024 * 1024
+VMEM_LIMIT = 8 * 1024 * 1024
+PACK_LIMIT = 60 * 1024 * 1024
 
 
 def dot(a, b, ca, cb):
@@ -125,18 +126,20 @@
     ).astype(BF)
 
 
-def enter_math(ext, dt_cols, wx, wb, wc, bias_row, alog_row):
+def enter_math(ext, dt_cols, wx, wb, bias_row, alog_row):
     def act(weight, lo, hi):
         pre = taps(ext, weight, lo, hi)
         return (pre * jax.nn.sigmoid(pre)).astype(BF)
 
-    x_act, b_act, c_act = act(wx, 0, 256), act(wb, 256, 384), act(wc, 384, 512)
+    x_act, b_act = act(wx, 0, 256), act(wb, 256, 384)
     shifted, step, logd, cum = rates(dt_cols, bias_row, alog_row)
     final = cum[T - 1 : T, :]
     to_end = jnp.exp(final - cum) * step
-    weighted = x_act.astype(F32) * spread(to_end)
+    wide_end = spread(to_end)
+    late = iota((T, CW), 0) >= KT - 1
+    weighted = jnp.where(late, x_act.astype(F32) * wide_end, 0.0)
     fresh = dot_parts(weighted, b_act, 0, 0, 2)
-    return x_act, b_act, c_act, step, cum, fresh, final
+    return step, cum, fresh, wide_end[0:8], spread(jnp.broadcast_to(final, (8, 128)))
 
 
 def within_math(x_act, b_act, c_act, step, cum, cum_t):
@@ -177,10 +180,11 @@
     grown = spread(jnp.exp(cum))
     lifted = y_grad.astype(F32) * grown
     start_grad = dot_parts(lifted, c_act, 0, 0, 2)
-    return y_grad, gate_grad, gain_grad, lifted, start_grad
-
-
-def within_back_math(x_act, b_act, c_act, step, cum, cum_t, kept, y, y_grad, lifted, carried):
+    return y_grad, gate_grad, gain_grad, start_grad
+
+
+def within_back_math(x_act, b_act, c_act, step, cum, cum_t, kept, y, y_grad, carried):
+    lifted = y_grad.astype(F32) * spread(jnp.exp(cum))
     score_grad = jnp.zeros((T, T), F32)
     x_parts = []
     step_t = step.T
@@ -252,7 +256,7 @@
     return total
 
 
-def call(kernel, out_shape, in_specs, out_specs=None, scratch=(), flops=0, bytes_accessed=0):
+def call(kernel, out_shape, in_specs, out_specs=None, scratch=(), flops=0, bytes_accessed=0, limit=VMEM_LIMIT):
     place = {
         "v": pl.BlockSpec(memory_space=pltpu.VMEM),
         "s": pl.BlockSpec(memory_space=pltpu.SMEM),
@@ -264,7 +268,7 @@
         in_specs=[place[c] for c in in_specs],
         out_specs=[place[c] for c in (out_specs or "v" * len(out_shape))],
         scratch_shapes=list(scratch),
-        compiler_params=pltpu.CompilerParams(vmem_limit_bytes=VMEM_LIMIT),
+        compiler_params=pltpu.CompilerParams(vmem_limit_bytes=limit),
         cost_estimate=pl.CostEstimate(
             flops=flops, bytes_accessed=bytes_accessed, transcendentals=0
         ),
@@ -319,43 +323,78 @@
     )
 
 
-def enter_kernel(rows, halo, wx, wb, wc, head, where, xbc, step_out, cum_out, send, ext):
-    ext[0:ROWS] = halo[...].astype(F32)
-    ext[ROWS : ROWS + T] = rows[:, 0:512].astype(F32)
-    x_act, b_act, c_act, step, cum, fresh, final = enter_math(
+def enter_kernel(rows, wx, wb, head, where, step_out, cum_out, send, ext):
+    ext[0:ROWS] = jnp.zeros((ROWS, 384), F32)
+    ext[ROWS : ROWS + T] = rows[:, 0:384].astype(F32)
+    step, cum, fresh, first_end, final = enter_math(
         ext,
         rows[:, 1024:1152].astype(F32),
         wx[...],
         group_lanes(wb, where),
-        group_lanes(wc, where),
         scalar_row(head, HD, 128, 1),
         scalar_row(head, 0, 128, 1),
     )
-    xbc[:, 0:256] = x_act
-    xbc[:, 256:384] = b_act
-    xbc[:, 384:512] = c_act
     step_out[...] = step
     cum_out[...] = cum
-    pieces_of = send.shape[0]
-    send[:, 0:8] = fresh.reshape(pieces_of, 8, 128)
-    send[:, 8:16] = head_column(final).reshape(pieces_of, 8, 128)
-
-
-def within_kernel(xbc, step, cum, inside, kept):
+    count = send.shape[0]
+    first = ext[ROWS : ROWS + 8]
+    last = pltpu.roll(ext[ROWS + T - 8 : ROWS + T], 6, 0)
+    rim = jnp.where(iota((8, 384), 0) < 3, first, last)
+    ends = jnp.where(iota((8, CW), 0) < 3, first_end, final)
+    columns = jnp.concatenate([rim[:, 0:CW], ends, jnp.zeros((112, CW), F32)], axis=0).T
+    send[:, 0:8] = fresh.reshape(count, 8, 128)
+    send[:, 8:16] = columns.reshape(count, 8, 128)
+    for i in range(count):
+        send[i, 16:24] = rim[:, 256:384]
+
+
+def within_kernel(rows, halo, wx, wb, wc, where, step, cum, xbc, slopes, inside, kept, ext):
+    ext[0:ROWS] = halo[...].astype(F32)
+    ext[ROWS : ROWS + T] = rows[:, 0:512].astype(F32)
+    acts = []
+    for weight, lo, hi in (
+        (wx[...], 0, 256),
+        (group_lanes(wb, where), 256, 384),
+        (group_lanes(wc, where), 384, 512),
+    ):
+        value, slope = silu_slope(taps(ext, weight, lo, hi))
+        acts.append(value.astype(BF))
+        xbc[:, lo:hi] = acts[-1]
+        slopes[:, lo:hi] = slope
     step, cum = step[...], cum[...]
-    out, mixes = within_math(xbc[:, 0:256], xbc[:, 256:384], xbc[:, 384:512], step, cum, cum.T)
+    out, mixes = within_math(*acts, step, cum, cum.T)
     inside[...] = out
     for e in range(HD):
         kept[e] = mixes[e]
 
 
-def scan_kernel(received, send, decays):
+def scan_kernel(received, wx, wb, where, send, decays, columns):
+    count = received.shape[0]
+    columns[...] = jnp.concatenate([wx[...], jnp.zeros((128 - KT, CW), F32)], axis=0).T
+    mine = columns[pl.ds(pl.multiple_of(where[2] * 8, 8), 8), :]
+    taps_b = group_lanes(wb, where)
+    lane, row = iota((8, 128), 1), iota((8, 128), 0)
     state = jnp.zeros((8, 128), F32)
-    for i in range(received.shape[0]):
+    x_last, b_last = state, state
+    for i in range(count):
+        x_rim, b_rim = received[i, 8:16], received[i, 16:24]
+        x_seen = jnp.where(lane < 3, pltpu.roll(x_last, 125, 1), pltpu.roll(x_rim, 3, 1))
+        b_seen = jnp.where(row < 3, pltpu.roll(b_last, 5, 0), pltpu.roll(b_rim, 3, 0))
+        x_pre = mine[:, 0:1] * x_seen
+        b_pre = taps_b[0:1] * b_seen
+        for k in range(1, KT):
+            x_pre = x_pre + mine[:, k : k + 1] * pltpu.roll(x_seen, 128 - k, 1)
+            b_pre = b_pre + taps_b[k : k + 1] * pltpu.roll(b_seen, 8 - k, 0)
+        x_act = (x_pre * jax.nn.sigmoid(x_pre)).astype(BF).astype(F32) * pltpu.roll(x_rim, 120, 1)
+        b_act = (b_pre * jax.nn.sigmoid(b_pre)).astype(BF).astype(F32)
+        fresh = received[i, 0:8]
+        for t in range(KT - 1):
+            fresh = fresh + x_act[:, t : t + 1] * b_act[t : t + 1, :]
+        decay = jnp.exp(jnp.broadcast_to(x_rim[:, 11:12], (8, 128)))
         send[i] = state
-        decay = jnp.exp(received[i, 8:16])
         decays[i] = decay
-        state = decay * state + received[i, 0:8]
+        state = decay * state + fresh
+        x_last, b_last = x_rim, b_rim
 
 
 def scan_back_kernel(received, decays, send):
@@ -388,9 +427,9 @@
     message[...] = pair_rows(squares, along)
 
 
-def norm_kernel(message, mixed, rows, gain, xbc, cum, where, y_grad_out, gate_out, gain_out, lifted_out, send):
+def norm_kernel(message, mixed, rows, gain, xbc, cum, where, y_grad_out, gate_out, gain_out, send):
     sums = jnp.concatenate([message[...], jnp.zeros((120, T), F32)], axis=0).T
-    y_grad, gate_grad, gain_grad, lifted, start_grad = norm_math(
+    y_grad, gate_grad, gain_grad, start_grad = norm_math(
         mixed[...],
         rows[:, 512:768].astype(F32),
         rows[:, 768:1024].astype(F32),
@@ -403,19 +442,10 @@
     y_grad_out[...] = y_grad
     gate_out[...] = gate_grad
     gain_out[...] = jnp.broadcast_to(gain_grad, (8, CW))
-    lifted_out[...] = lifted
     send[...] = start_grad.reshape(send.shape)
 
 
-def back_kernel(
-    rows, halo, wx, wb, wc, where, xbc, step, cum, kept, y, y_grad, lifted, carried,
-    x_in_out, b_in_out, c_grad_out, out_dots_out, in_dots_out, skip_out, slopes_out, ext,
-):
-    ext[0:ROWS] = halo[...].astype(F32)
-    ext[ROWS : ROWS + T] = rows[:, 0:512].astype(F32)
-    slopes_out[...] = conv_slopes(
-        ext, wx[...], group_lanes(wb, where), group_lanes(wc, where)
-    )
+def back_kernel(xbc, step, cum, kept, y, y_grad, carried, middle, dots):
     cum = cum[...]
     x_in, b_in, c_grad, out_dots, in_dots, skip_grad = within_back_math(
         xbc[:, 0:256],
@@ -427,25 +457,25 @@
         [kept[e] for e in range(HD)],
         y[...],
         y_grad[...],
-        lifted[...],
         carried[...],
     )
-    x_in_out[...] = x_in
-    b_in_out[...] = b_in
-    c_grad_out[...] = c_grad
-    out_dots_out[...] = out_dots
-    in_dots_out[...] = in_dots
-    skip_out[...] = jnp.broadcast_to(skip_grad, (8, CW))
+    middle[:, 0:256] = x_in
+    middle[:, 256:384] = b_in
+    middle[:, 384:512] = c_grad
+    dots[0:T] = out_dots + pltpu.roll(in_dots, 64, 1)
+    dots[T : T + 8] = head_sums(jnp.broadcast_to(skip_grad, (8, CW)))
 
 
 def leave_kernel(
-    end_grad, rows, halo, head, xbc, step, cum, y_grad, x_in, b_in, c_grad, out_dots, in_dots,
-    carried, gain_grad, skip_grad, slopes, pre_out, dt_out, rim, send, ext,
+    end_grad, rows, halo, head, xbc, step, cum, y_grad, middle, dots, carried, gain_grad, slopes,
+    pre_out, dt_out, send, ext,
 ):
     ext[0:ROWS] = halo[...].astype(F32)
     ext[ROWS : ROWS + T] = rows[:, 0:512].astype(F32)
     alog_row = scalar_row(head, 0, 128, 1)
     step = step[...]
+    both = dots[0:T]
+    live = iota((T, 128), 1) < HD
     x_grad, b_grad, dt_grad, alog_grad, bias_grad = leave_math(
         xbc[:, 0:256],
         xbc[:, 256:384],
@@ -456,45 +486,50 @@
         alog_row,
         scalar_row(head, 2 * HD, CW, PS),
         y_grad[...],
-        x_in[...],
-        b_in[...],
-        out_dots[...],
-        in_dots[...],
+        middle[:, 0:256],
+        middle[:, 256:384],
+        jnp.where(live, both, 0.0),
+        jnp.where(live, pltpu.roll(both, 64, 1), 0.0),
         carried[...],
         end_grad[...],
     )
     dt_out[...] = dt_grad
-    pre = jnp.concatenate([x_grad, b_grad, c_grad[...]], axis=1) * slopes[...]
+    pre = jnp.concatenate([x_grad, b_grad, middle[:, 384:512]], axis=1) * slopes[...]
     pre_out[...] = pre
-    rim[...] = pre[0:8]
     weights = jnp.concatenate(weight_grads(ext, pre), axis=0)
+    sums = jnp.concatenate([alog_grad, bias_grad, dots[T : T + 1], jnp.zeros((5, 128), F32)], axis=0)
+    line = sums[0:1] + pltpu.roll(sums, 32, 1)[1:2] + pltpu.roll(sums, 64, 1)[2:3]
     block = jnp.concatenate(
         [weights[:, i * 128 : (i + 1) * 128] for i in range(4)]
-        + [gain_grad[0:1, 0:128], gain_grad[0:1, 128:256]]
-        + [skip_grad[0:1, 0:128], skip_grad[0:1, 128:256]]
-        + [alog_grad, bias_grad, jnp.zeros((2, 128), F32)],
+        + [gain_grad[0:1, 0:128], gain_grad[0:1, 128:256], line]
+        + [pre[0:3, i * 128 : (i + 1) * 128] for i in range(4)]
+        + [jnp.zeros((1, 128), F32)],
         axis=0,
     )
     for i in range(send.shape[0]):
         send[i] = block
 
 
-def finish_kernel(received, following, where, wx, wb, wc, pre, dt_grad, gate_grad, send, conv_x_out, alog_out, bias_out, skip_out, ext):
-    total = received[0]
-    for i in range(1, received.shape[0]):
-        total = total + received[i]
+def finish_kernel(received, where, wx, wb, wc, pre, dt_grad, gate_grad, send, conv_x_out, alog_out, bias_out, skip_out, ext):
+    count = received.shape[0]
+    total = received[0, 0:24]
+    for i in range(1, count):
+        total = total + received[i, 0:24]
+    after = where[2] + 1
+    next_block = received[jnp.minimum(after, count - 1)]
+    following = jnp.concatenate(
+        [next_block[19 + 3 * i : 22 + 3 * i] for i in range(4)], axis=1
+    )
     ext[0:T] = pre[...]
-    ext[T : T + 8] = following[...]
+    ext[T : T + 3] = jnp.where(after < count, following, 0.0)
     x_grad = conv_back(ext, wx[...], 0, 256).astype(BF)
     b_grad = conv_back(ext, group_lanes(wb, where), 256, 384).astype(BF)
     c_grad = conv_back(ext, group_lanes(wc, where), 384, 512).astype(BF)
     conv_x_out[...] = jnp.concatenate([total[0:4], total[4:8]], axis=1)
     for e in range(HD):
-        at = 18 + e // 2
-        cut = slice((e % 2) * PS, (e % 2 + 1) * PS)
-        alog_out[e] = jnp.sum(total[20:21, e : e + 1])
-        bias_out[e] = jnp.sum(total[21:22, e : e + 1])
-        skip_out[e] = jnp.sum(total[at : at + 1, cut])
+        alog_out[e] = jnp.sum(total[18:19, e : e + 1])
+        bias_out[e] = jnp.sum(total[18:19, 32 + e : 33 + e])
+        skip_out[e] = jnp.sum(total[18:19, 64 + e : 65 + e])
     shared = jnp.concatenate(
         [
             jnp.concatenate([total[8:12], total[12:16]], axis=1),
@@ -552,7 +587,7 @@
     ways = lax.axis_size("head")
     blocks = lax.axis_size("ctx")
     head_at = lax.axis_index("head")
-    where = jnp.stack([head_at, (head_at * GROUPS) // ways]).astype(jnp.int32)
+    where = jnp.stack([head_at, (head_at * GROUPS) // ways, lax.axis_index("ctx")]).astype(jnp.int32)
     head = jnp.concatenate([a_log, dt_bias, d_skip])
     gain = norm_gain.reshape(1, -1)
 
@@ -568,6 +603,7 @@
         [sds((ways, ROWS, IN_W), BF)],
         "hhhhhh",
         scratch=[pltpu.VMEM(a.shape, a.dtype) for a in inputs] + [pltpu.SemaphoreType.DMA((6,))],
+        limit=PACK_LIMIT,
     )(*inputs)[0]
     arrived = head_swap(sent)
     rows = arrived.reshape(T, IN_W)
@@ -579,17 +615,24 @@
     chunk = sds((blocks, T // blocks, 128), F32)
     ext = pltpu.VMEM((ROWS + T, 512), F32)
 
-    xbc, step, cum, send = call(
+    step, cum, send = call(
         enter_kernel,
-        [sds((T, 512), BF), slim, slim, sds((blocks, 2 * T // blocks, 128), F32)],
-        "vvvvvss",
+        [slim, slim, sds((blocks, 24, 128), F32)],
+        "vvvss",
+        scratch=[pltpu.VMEM((ROWS + T, 384), F32)],
+    )(rows, conv_x, conv_b, head, where)
+    received = ctx_swap(send)
+    xbc, slopes, inside, kept = call(
+        within_kernel,
+        [sds((T, 512), BF), sds((T, 512), F32), wide, sds((HD, T, T), BF)],
+        "vvvvvsvv",
         scratch=[ext],
-    )(rows, halo, conv_x, conv_b, conv_c, head, where)
-    received = ctx_swap(send)
-    inside, kept = call(
-        within_kernel, [wide, sds((HD, T, T), BF)], "vvv", flops=10**8, bytes_accessed=2 * 10**6
-    )(xbc, step, cum)
-    send, decays = call(scan_kernel, [chunk, chunk], "v")(received)
+        flops=10**8,
+        bytes_accessed=3 * 10**6,
+    )(rows, halo, conv_x, conv_b, conv_c, where, step, cum)
+    send, decays = call(
+        scan_kernel, [chunk, chunk], "vvvs", scratch=[pltpu.VMEM((CW, 128), F32)]
+    )(received, conv_x, conv_b, where)
     carried = ctx_swap(send).reshape(T, 128)
     y, mixed, sums = call(
         mix_kernel, [wide, sds((T, CW), BF), sds((8, T), F32)], "vvvvvvss"
@@ -598,41 +641,38 @@
     sums = lax.psum(
         sums, "head", axis_index_groups=[[g * per + i for i in range(per)] for g in range(GROUPS)]
     )
-    y_grad, gate_grad, gain_grad, lifted, send = call(
+    y_grad, gate_grad, gain_grad, send = call(
         norm_kernel,
-        [sds((T, CW), BF), sds((T, CW), BF), sds((8, CW), F32), wide, chunk],
+        [sds((T, CW), BF), sds((T, CW), BF), sds((8, CW), F32), chunk],
         "vvvvvvs",
     )(sums, mixed, rows, gain, xbc, cum, where)
     received = ctx_swap(send)
-    x_part, b_part, c_grad, out_dots, in_dots, skip_grad, slopes = call(
+    middle, dots = call(
         back_kernel,
-        [wide, slim, slim, slim, slim, sds((8, CW), F32), sds((T, 512), F32)],
-        "vvvvvsvvvvvvvv",
-        scratch=[ext],
+        [sds((T, 512), F32), sds((T + 8, 128), F32)],
+        "vvvvvvv",
         flops=3 * 10**8,
         bytes_accessed=4 * 10**6,
-    )(rows, halo, conv_x, conv_b, conv_c, where, xbc, step, cum, kept, y, y_grad, lifted, carried)
+    )(xbc, step, cum, kept, y, y_grad, carried)
     send = call(scan_back_kernel, [chunk], "vv")(received, decays)[0]
     end_grad = ctx_swap(send).reshape(T, 128)
-    pre, dt_grad, rim, send = call(
+    pre, dt_grad, send = call(
         leave_kernel,
-        [sds((T, 512), F32), slim, sds((8, 512), F32), sds((blocks, 24, 128), F32)],
-        "vvvs" + "v" * 13,
+        [sds((T, 512), F32), slim, sds((blocks, 32, 128), F32)],
+        "vvvs" + "v" * 9,
         scratch=[ext],
     )(
-        end_grad, rows, halo, head, xbc, step, cum, y_grad, x_part, b_part, c_grad, out_dots,
-        in_dots, carried, gain_grad, skip_grad, slopes,
-    )
-    following = lax.ppermute(rim, "ctx", [(i + 1, i) for i in range(blocks - 1)])
+        end_grad, rows, halo, head, xbc, step, cum, y_grad, middle, dots, carried, gain_grad, slopes,
+    )
     received = ctx_swap(send)
     four = sds((HD,), F32)
     send, conv_x_grad, alog_grad, bias_grad, skip_sum = call(
         finish_kernel,
         [sds((ways, ROWS, OUT_W), BF), sds((KT, CW), F32), four, four, four],
-        "vvsvvvvvv",
+        "vsvvvvvv",
         "vvsss",
         scratch=[pltpu.VMEM((T + 8, 512), F32)],
-    )(received, following, where, conv_x, conv_b, conv_c, pre, dt_grad, gate_grad)
+    )(received, where, conv_x, conv_b, conv_c, pre, dt_grad, gate_grad)
     received = head_swap(send)
     x_grad, b_grad, c_grad, dt_out, gate_out, conv_b_grad, conv_c_grad, gain_sum = call(
         unpack_kernel,

time: 162 us -> 159 us (0.981)
  blocking collectives: 65.1 us -> 88.7 us
  waiting for transfers between devices: 40 us -> 25 us
  local copies, waits for them, and re-layouts: 11.1 us -> 0.61 us
  starting transfers between devices: 28.5 us -> 25.1 us
  Pallas kernels: 15.1 us -> 18.3 us
    all_to_all x2 -> x3, blocking collectives: 40.5 us -> 65.8 us  [ctx_swap(): return lax.all_to_all(value, 'ctx', 0, 0, tiled=True)]
    unnamed x42 -> x18, local copies, waits for them, and re-layouts: 11.1 us -> 0.61 us
    all_to_all x3 -> x2, waiting for transfers between devices: 24.4 us -> 14.3 us  [ctx_swap(): return lax.all_to_all(value, 'ctx', 0, 0, tiled=True)]
    ppermute x1 -> x0, waiting for transfers between devices: 4.35 us -> none  [per_device(): lax.ppermute(rim, 'ctx', [(i + 1, i) for i in range(blocks - 1)])]
    all_to_all x3 -> x2, starting transfers between devices: 13.9 us -> 10.8 us  [ctx_swap(): return lax.all_to_all(value, 'ctx', 0, 0, tiled=True)]
    pallas_call x5, Pallas kernels: 8.17 us -> 10.8 us  [the longest x1 4.15 us: per_device(): call(scan_kernel, [chunk, chunk], 'vvvs', scratch=[pltpu.VMEM((CW, 128),...]
    psum x1, blocking collectives: 6.88 us -> 4.74 us  [per_device(): lax.psum(sums, 'head', axis_index_groups=[[g * per + i for i in range(per...]
  transfers between devices with their start and end apart: 6 -> 4, of which waited for: 6 -> 4; matrix products, arithmetic and copies ran while one was open for 0% -> 0% of each run, Pallas kernels for 2% -> 2%
where the time goes in v3:
time: 159 us
  blocking collectives  88.7 us (56%)
  starting transfers between devices  25.1 us (16%)
  waiting for transfers between devices  25 us (16%)
  Pallas kernels  18.3 us (12%)
    all_to_all x3, blocking collectives, ctx_swap(): return lax.all_to_all(value, 'ctx', 0, 0, tiled=True)  65.8 us
    all_to_all x1, blocking collectives, head_swap(): return lax.all_to_all(value, 'head', 0, 0, tiled=True)  18.2 us
    all_to_all x2, waiting for transfers between devices, ctx_swap(): return lax.all_to_all(value, 'ctx', 0, 0, tiled=True)  14.3 us
    all_to_all x2, starting transfers between devices, ctx_swap(): return lax.all_to_all(value, 'ctx', 0, 0, tiled=True)  10.8 us
    all_to_all x1, starting transfers between devices, head_swap(): return lax.all_to_all(value, 'head', 0, 0, tiled=True)  10.3 us
    all_to_all x1, waiting for transfers between devices, head_swap(): return lax.all_to_all(value, 'head', 0, 0, tiled=True)  9.85 us
    psum x1, blocking collectives, per_device(): lax.psum(sums, 'head', axis_index_groups=[[g * per + i for i in range(per...  4.74 us
    pallas_call x1, Pallas kernels, per_device(): call(scan_kernel, [chunk, chunk], 'vvvs', scratch=[pltpu.VMEM((CW, 128),...  4.15 us
  transfers between devices with their start and end apart: 4, of which 4 were waited for; matrix products, arithmetic and copies ran while one was open for 0% of the time, Pallas kernels for 2%

profile of v3, /device:TPU:1, one launch (start us, length us, event | category | flops | bytes accessed | tf_op | source)
XLA Modules:
  0.0 158.7 jit_solution(2180449022883131735)
XLA Ops:
  0.6 2.0 %shard_map.220 = bf16[16,16,1152]{2,1,0:T(8,128)(2,1)} custom-call(bf16[16,4096]{1,0:T(8,128)(2,1)} %x_at.1, bf16[16,1024]{1,0:T(8,128)(2,1)} %b_at.1, bf16[16,1024]{1,0:T(8,128)(2,1)} %c_at.1, bf16[16,64]{1,0:T(8,128)(2,1)} %dt_at.1, bf16[16,4096]{1,0:T(8,128)(2,1)} %gate_at.1, bf16[16,4096]{1,0:T(8,128)(2,1)} %grad_at.1), custom_call_target="tpu_custom_call" | custom-call | tf_op jit(solution)/shard_map/pallas_call | solution.py:601
  2.7 10.3 %all-to-all-start = ((bf16[16,16,1152]{2,1,0:T(8,128)(2,1)}), bf16[16,16,1152]{2,1,0:T(8,128)(2,1)S(1)}, u32[]{:S(2)}, u32[]{:S(2)}) async-start(bf16[16,16,1152]{2,1,0:T(8,128)(2,1)} %shard_map.220), calls=%async_computation | async-start | bytes 1179648 | tf_op jit(solution)/shard_map/all_to_all | solution.py:598
  13.7 9.8 %all-to-all-done = bf16[16,16,1152]{2,1,0:T(8,128)(2,1)S(1)} async-done(((bf16[16,16,1152]{2,1,0:T(8,128)(2,1)}), bf16[16,16,1152]{2,1,0:T(8,128)(2,1)S(1)}, u32[]{:S(2)}, u32[]{:S(2)}) %all-to-all-start) | async-done | bytes 589856 | tf_op jit(solution)/shard_map/all_to_all | solution.py:598
  23.6 1.5 shard_map.221
  25.1 26.3 %all_to_all.35.received = f32[32,24,128]{2,1,0:T(8,128)S(1)} all-to-all(f32[32,24,128]{2,1,0:T(8,128)S(1)} %get-tuple-element.46), channel_id=1, replica_groups=mesh['ctx'=32,'head'=16] {'ctx'}, dimensions={0} | all-to-all | bytes 786432 | tf_op jit(solution)/shard_map/all_to_all | solution.py:595
  51.4 4.1 %shard_map.222 = (f32[32,8,128]{2,1,0:T(8,128)}, f32[32,8,128]{2,1,0:T(8,128)S(1)}) custom-call(f32[32,24,128]{2,1,0:T(8,128)S(1)} %all_to_all.35.received, f32[4,256]{1,0:T(4,128)S(1)} %copy-done.5, f32[4,1024]{1,0:T(4,128)S(1)} %copy-done, s32[3]{0:T(128)S(1)} %pad_add_fusion.where), custom_call_target="tpu_custom_call" | custom-call | tf_op jit(solution)/shard_map/pallas_call | solution.py:633
  55.6 6.6 %all-to-all-start.2 = ((f32[32,8,128]{2,1,0:T(8,128)}), f32[32,8,128]{2,1,0:T(8,128)S(1)}, u32[]{:S(2)}, u32[]{:S(2)}) async-start(f32[32,8,128]{2,1,0:T(8,128)} %get-tuple-element.47), calls=%async_computation.2 | async-start | bytes 262144 | tf_op jit(solution)/shard_map/all_to_all | solution.py:595
  62.2 4.0 %collective-permute-start = (bf16[16,512]{1,0:T(8,128)(2,1)S(1)}, bf16[16,512]{1,0:T(8,128)(2,1)S(1)}, u32[]{:S(2)}, u32[]{:S(2)}) collective-permute-start(bf16[16,512]{1,0:T(8,128)(2,1)S(1)} %slice_bitcast_fusion), channel_id=1, source_target_pairs={{0,16},{16,32},{32,48},{48,64},{64,80},{80,96},{96,112},{112,128},... | collective-permute-start | bytes 49160 | tf_op jit(solution)/shard_map/ppermute | solution.py:610
  66.2 0.9 collective-permute-done.halo
  67.1 2.1 %shard_map.223 = (bf16[256,512]{1,0:T(8,128)(2,1)S(1)}, f32[256,512]{1,0:T(8,128)S(1)}, f32[256,256]{1,0:T(8,128)S(1)}, bf16[4,256,256]{2,1,0:T(8,128)(2,1)S(1)}) custom-call(bf16[256,1152]{1,0:T(8,128)(2,1)S(1)} %bitcast.11, bf16[16,512]{1,0:T(8,128)(2,1)S(1)} %collective-permute-done.halo, f32[4,256]{1,0:T(4,128)S(1)} %copy-done.5, f32[4,1024]{1,0:T(4,128)S(1)} %copy-done, ...), custom_call_target="tpu_custom_call" | custom-call | flops 100000000 | bytes 3000000 | tf_op jit(solution)/shard_map/pallas_call | solution.py:625
  69.1 4.4 %all-to-all-done.2 = f32[32,8,128]{2,1,0:T(8,128)S(1)} async-done(((f32[32,8,128]{2,1,0:T(8,128)}), f32[32,8,128]{2,1,0:T(8,128)S(1)}, u32[]{:S(2)}, u32[]{:S(2)}) %all-to-all-start.2) | async-done | bytes 131104 | tf_op jit(solution)/shard_map/all_to_all | solution.py:595
  73.5 1.0 shard_map.224
  74.5 4.7 %psum.7.message = f32[8,256]{1,0:T(8,128)S(1)} all-reduce(f32[8,256]{1,0:T(8,128)S(1)} %get-tuple-element.52), channel_id=1, replica_groups={{0,1},{2,3},{4,5},{6,7},{8,9},{10,11},{12,13},{14,15},{16,17},{18,19},{..., use_global_device_ids=true, to_apply=%region_0.1 | all-reduce | flops 2048 | bytes 16384 | tf_op jit(solution)/shard_map/psum | solution.py:641
  79.2 1.4 shard_map.225
  80.6 20.6 %all_to_all.36.received = f32[32,8,128]{2,1,0:T(8,128)S(1)} all-to-all(f32[32,8,128]{2,1,0:T(8,128)S(1)} %get-tuple-element.54), channel_id=1, replica_groups=mesh['ctx'=32,'head'=16] {'ctx'}, dimensions={0} | all-to-all | bytes 262144 | tf_op jit(solution)/shard_map/all_to_all | solution.py:595
  101.2 0.7 shard_map.226
  101.9 4.3 %all-to-all-start.4 = ((f32[32,8,128]{2,1,0:T(8,128)}), f32[32,8,128]{2,1,0:T(8,128)S(1)}, u32[]{:S(2)}, u32[]{:S(2)}) async-start(f32[32,8,128]{2,1,0:T(8,128)} %shard_map.226), calls=%async_computation.4 | async-start | bytes 262144 | tf_op jit(solution)/shard_map/all_to_all | solution.py:595
  106.2 1.4 shard_map.227
  107.6 9.9 %all-to-all-done.4 = f32[32,8,128]{2,1,0:T(8,128)S(1)} async-done(((f32[32,8,128]{2,1,0:T(8,128)}), f32[32,8,128]{2,1,0:T(8,128)S(1)}, u32[]{:S(2)}, u32[]{:S(2)}) %all-to-all-start.4) | async-done | bytes 131104 | tf_op jit(solution)/shard_map/all_to_all | solution.py:595
  117.6 1.7 %shard_map.228 = (f32[256,512]{1,0:T(8,128)S(1)}, f32[256,128]{1,0:T(8,128)S(1)}, f32[32,32,128]{2,1,0:T(8,128)S(1)}) custom-call(f32[256,128]{1,0:T(8,128)S(1)} %bitcast.18, bf16[256,1152]{1,0:T(8,128)(2,1)S(1)} %bitcast.14, bf16[16,512]{1,0:T(8,128)(2,1)S(1)} %collective-permute-done.halo, f32[12]{0:T(128)S(1)} %pad_maximum_fusion.head, ...), custom_call_target="tpu_custom_call" | custom-call | tf_op jit(solution)/shard_map/pallas_call | solution.py:659
  119.3 18.9 %all_to_all.37.received = f32[32,32,128]{2,1,0:T(8,128)S(1)} all-to-all(f32[32,32,128]{2,1,0:T(8,128)S(1)} %get-tuple-element.63), channel_id=1, replica_groups=mesh['ctx'=32,'head'=16] {'ctx'}, dimensions={0} | all-to-all | bytes 1048576 | tf_op jit(solution)/shard_map/all_to_all | solution.py:595
  138.2 1.6 shard_map.229
  139.7 18.2 %all_to_all.38.received = bf16[16,16,1152]{2,1,0:T(8,128)(2,1)S(1)} all-to-all(bf16[16,16,1152]{2,1,0:T(8,128)(2,1)S(1)} %get-tuple-element.67), channel_id=1, replica_groups=mesh['ctx'=32,'head'=16] {'head'}, dimensions={0} | all-to-all | bytes 1179648 | tf_op jit(solution)/shard_map/all_to_all | solution.py:598
  157.9 0.8 shard_map.230
  (21 shorter events, 0.8 us)
Async XLA Ops:
  2.7 20.9 %all-to-all-start = ((bf16[16,16,1152]{2,1,0:T(8,128)(2,1)}), bf16[16,16,1152]{2,1,0:T(8,128)(2,1)S(1)}, u32[]{:S(2)}, u32[]{:S(2)}) async-start(bf16[16,16,1152]{2,1,0:T(8,128)(2,1)} %shard_map.220), calls=%async_computation | async-start | bytes 1179648 | tf_op jit(solution)/shard_map/all_to_all | solution.py:598
  13.0 10.6 %copy-start = (f32[4,1024]{1,0:T(4,128)S(1)}, f32[4,1024]{1,0:T(4,128)}, u32[]{:S(2)}) copy-start(f32[4,1024]{1,0:T(4,128)} %wb.7) | copy-start | bytes 49156
  13.0 0.7 copy-start.6
  13.0 0.7 copy-start.7
  13.0 0.7 copy-start.8
  13.0 10.6 %copy-start.5 = (f32[4,256]{1,0:T(4,128)S(1)}, f32[4,256]{1,0:T(4,128)}, u32[]{:S(2)}) copy-start(f32[4,256]{1,0:T(4,128)} %wx.7) | copy-start | bytes 12292
  55.6 17.9 %all-to-all-start.2 = ((f32[32,8,128]{2,1,0:T(8,128)}), f32[32,8,128]{2,1,0:T(8,128)S(1)}, u32[]{:S(2)}, u32[]{:S(2)}) async-start(f32[32,8,128]{2,1,0:T(8,128)} %get-tuple-element.47), calls=%async_computation.2 | async-start | bytes 262144 | tf_op jit(solution)/shard_map/all_to_all | solution.py:595
  62.1 4.9 %copy-start.4 = (f32[4,1024]{1,0:T(4,128)S(1)}, f32[4,1024]{1,0:T(4,128)}, u32[]{:S(2)}) copy-start(f32[4,1024]{1,0:T(4,128)} %wc.3) | copy-start | bytes 49156
  62.2 4.9 %collective-permute-start = (bf16[16,512]{1,0:T(8,128)(2,1)S(1)}, bf16[16,512]{1,0:T(8,128)(2,1)S(1)}, u32[]{:S(2)}, u32[]{:S(2)}) collective-permute-start(bf16[16,512]{1,0:T(8,128)(2,1)S(1)} %slice_bitcast_fusion), channel_id=1, source_target_pairs={{0,16},{16,32},{32,48},{48,64},{64,80},{80,96},{96,112},{112,128},... | collective-permute-start | bytes 49160 | tf_op jit(solution)/shard_map/ppermute | solution.py:610
  67.1 6.4 %copy-start.3 = (f32[4096]{0:T(1024)S(1)}, f32[4096]{0:T(1024)}, u32[]{:S(2)}) copy-start(f32[4096]{0:T(1024)} %param.25) | copy-start | bytes 49156
  80.6 20.6 %copy-start.1 = (bf16[256,256]{1,0:T(8,128)(2,1)}, bf16[256,256]{1,0:T(8,128)(2,1)S(1)}, u32[]{:S(2)}) copy-start(bf16[256,256]{1,0:T(8,128)(2,1)S(1)} %get-tuple-element.66.gate_grad) | copy-start | bytes 393220
  101.9 15.7 %all-to-all-start.4 = ((f32[32,8,128]{2,1,0:T(8,128)}), f32[32,8,128]{2,1,0:T(8,128)S(1)}, u32[]{:S(2)}, u32[]{:S(2)}) async-start(f32[32,8,128]{2,1,0:T(8,128)} %shard_map.226), calls=%async_computation.4 | async-start | bytes 262144 | tf_op jit(solution)/shard_map/all_to_all | solution.py:595
  119.2 18.9 %copy-start.2 = (bf16[256,256]{1,0:T(8,128)(2,1)S(1)}, bf16[256,256]{1,0:T(8,128)(2,1)}, u32[]{:S(2)}) copy-start(bf16[256,256]{1,0:T(8,128)(2,1)} %copy-done.1) | copy-start | bytes 393220

commit v4 on v3

--- a/solution.py
+++ b/solution.py
@@ -288,23 +288,23 @@
     ]
     for move in moves:
         move.start()
-    for move in moves:
-        move.wait()
     ways = out.shape[0]
     per = GROUPS * N // ways
+    for move, ref, lo in ((moves[0], x, 0), (moves[4], gate, 512), (moves[5], out_grad, 768)):
+        move.wait()
+        for j in range(ways):
+            out[j, :, lo : lo + CW] = ref[:, j * CW : (j + 1) * CW]
+    for move, ref, lo in ((moves[1], b, 256), (moves[2], c, 384)):
+        move.wait()
+        for j in range(ways):
+            g = (j * per) // N
+            out[j, :, lo : lo + N] = ref[:, g * N : (g + 1) * N]
+    moves[3].wait()
     wide_dt = jnp.concatenate(
         [dt[...].astype(F32), jnp.zeros((ROWS, 128 - dt.shape[1]), F32)], axis=1
     )
     lane = iota((ROWS, 128), 1)
     for j in range(ways):
-        g = (j * per) // N
-        own = slice(j * CW, (j + 1) * CW)
-        shared = slice(g * N, (g + 1) * N)
-        out[j, :, 0:256] = x[:, own]
-        out[j, :, 256:384] = b[:, shared]
-        out[j, :, 384:512] = c[:, shared]
-        out[j, :, 512:768] = gate[:, own]
-        out[j, :, 768:1024] = out_grad[:, own]
         turned = pltpu.roll(wide_dt, (128 - HD * j) % 128, 1)
         out[j, :, 1024:1152] = jnp.where(lane < HD, turned, 0.0).astype(BF)
 
@@ -348,7 +348,7 @@
         send[i, 16:24] = rim[:, 256:384]
 
 
-def within_kernel(rows, halo, wx, wb, wc, where, step, cum, xbc, slopes, inside, kept, ext):
+def within_kernel(rows, halo, wx, wb, wc, where, step, cum, xbc, slopes, inside, kept, order, ext):
     ext[0:ROWS] = halo[...].astype(F32)
     ext[ROWS : ROWS + T] = rows[:, 0:512].astype(F32)
     acts = []
@@ -364,37 +364,42 @@
     step, cum = step[...], cum[...]
     out, mixes = within_math(*acts, step, cum, cum.T)
     inside[...] = out
+    order[...] = out[0:8, 0:128]
     for e in range(HD):
         kept[e] = mixes[e]
 
 
-def scan_kernel(received, wx, wb, where, send, decays, columns):
+def scan_kernel(received, wx, wb, where, order, send, decays, columns, fresh, grown):
+    del order
     count = received.shape[0]
     columns[...] = jnp.concatenate([wx[...], jnp.zeros((128 - KT, CW), F32)], axis=0).T
     mine = columns[pl.ds(pl.multiple_of(where[2] * 8, 8), 8), :]
     taps_b = group_lanes(wb, where)
-    lane, row = iota((8, 128), 1), iota((8, 128), 0)
+    shape = (count, 8, 128)
+    lane, row = iota(shape, 2), iota(shape, 1)
+    x_rim, b_rim = received[:, 8:16], received[:, 16:24]
+    blank = jnp.zeros((1, 8, 128), F32)
+    x_last = jnp.concatenate([blank, x_rim[:-1]], axis=0)
+    b_last = jnp.concatenate([blank, b_rim[:-1]], axis=0)
+    x_seen = jnp.where(lane < 3, pltpu.roll(x_last, 125, 2), pltpu.roll(x_rim, 3, 2))
+    b_seen = jnp.where(row < 3, pltpu.roll(b_last, 5, 1), pltpu.roll(b_rim, 3, 1))
+    x_pre = mine[None, :, 0:1] * x_seen
+    b_pre = taps_b[None, 0:1] * b_seen
+    for k in range(1, KT):
+        x_pre = x_pre + mine[None, :, k : k + 1] * pltpu.roll(x_seen, 128 - k, 2)
+        b_pre = b_pre + taps_b[None, k : k + 1] * pltpu.roll(b_seen, 8 - k, 1)
+    x_act = (x_pre * jax.nn.sigmoid(x_pre)).astype(BF).astype(F32) * pltpu.roll(x_rim, 120, 2)
+    b_act = (b_pre * jax.nn.sigmoid(b_pre)).astype(BF).astype(F32)
+    total = received[:, 0:8]
+    for t in range(KT - 1):
+        total = total + x_act[:, :, t : t + 1] * b_act[:, t : t + 1, :]
+    fresh[...] = total
+    grown[...] = jnp.exp(jnp.broadcast_to(x_rim[:, :, 11:12], shape))
+    decays[...] = grown[...]
     state = jnp.zeros((8, 128), F32)
-    x_last, b_last = state, state
     for i in range(count):
-        x_rim, b_rim = received[i, 8:16], received[i, 16:24]
-        x_seen = jnp.where(lane < 3, pltpu.roll(x_last, 125, 1), pltpu.roll(x_rim, 3, 1))
-        b_seen = jnp.where(row < 3, pltpu.roll(b_last, 5, 0), pltpu.roll(b_rim, 3, 0))
-        x_pre = mine[:, 0:1] * x_seen
-        b_pre = taps_b[0:1] * b_seen
-        for k in range(1, KT):
-            x_pre = x_pre + mine[:, k : k + 1] * pltpu.roll(x_seen, 128 - k, 1)
-            b_pre = b_pre + taps_b[k : k + 1] * pltpu.roll(b_seen, 8 - k, 0)
-        x_act = (x_pre * jax.nn.sigmoid(x_pre)).astype(BF).astype(F32) * pltpu.roll(x_rim, 120, 1)
-        b_act = (b_pre * jax.nn.sigmoid(b_pre)).astype(BF).astype(F32)
-        fresh = received[i, 0:8]
-        for t in range(KT - 1):
-            fresh = fresh + x_act[:, t : t + 1] * b_act[t : t + 1, :]
-        decay = jnp.exp(jnp.broadcast_to(x_rim[:, 11:12], (8, 128)))
         send[i] = state
-        decays[i] = decay
-        state = decay * state + fresh
-        x_last, b_last = x_rim, b_rim
+        state = grown[i] * state + fresh[i]
 
 
 def scan_back_kernel(received, decays, send):
@@ -499,26 +504,27 @@
     weights = jnp.concatenate(weight_grads(ext, pre), axis=0)
     sums = jnp.concatenate([alog_grad, bias_grad, dots[T : T + 1], jnp.zeros((5, 128), F32)], axis=0)
     line = sums[0:1] + pltpu.roll(sums, 32, 1)[1:2] + pltpu.roll(sums, 64, 1)[2:3]
+    coarse = line.astype(BF).astype(F32)
     block = jnp.concatenate(
         [weights[:, i * 128 : (i + 1) * 128] for i in range(4)]
-        + [gain_grad[0:1, 0:128], gain_grad[0:1, 128:256], line]
-        + [pre[0:3, i * 128 : (i + 1) * 128] for i in range(4)]
-        + [jnp.zeros((1, 128), F32)],
+        + [gain_grad[0:1, 0:128], gain_grad[0:1, 128:256], coarse, line - coarse]
+        + [pre[0:3, i * 128 : (i + 1) * 128] for i in range(4)],
         axis=0,
-    )
+    ).astype(BF)
     for i in range(send.shape[0]):
         send[i] = block
 
 
 def finish_kernel(received, where, wx, wb, wc, pre, dt_grad, gate_grad, send, conv_x_out, alog_out, bias_out, skip_out, ext):
     count = received.shape[0]
-    total = received[0, 0:24]
+    total = received[0].astype(F32)
     for i in range(1, count):
-        total = total + received[i, 0:24]
+        total = total + received[i].astype(F32)
+    line = total[18:19] + total[19:20]
     after = where[2] + 1
-    next_block = received[jnp.minimum(after, count - 1)]
+    next_block = received[jnp.minimum(after, count - 1)].astype(F32)
     following = jnp.concatenate(
-        [next_block[19 + 3 * i : 22 + 3 * i] for i in range(4)], axis=1
+        [next_block[20 + 3 * i : 23 + 3 * i] for i in range(4)], axis=1
     )
     ext[0:T] = pre[...]
     ext[T : T + 3] = jnp.where(after < count, following, 0.0)
@@ -527,9 +533,9 @@
     c_grad = conv_back(ext, group_lanes(wc, where), 384, 512).astype(BF)
     conv_x_out[...] = jnp.concatenate([total[0:4], total[4:8]], axis=1)
     for e in range(HD):
-        alog_out[e] = jnp.sum(total[18:19, e : e + 1])
-        bias_out[e] = jnp.sum(total[18:19, 32 + e : 33 + e])
-        skip_out[e] = jnp.sum(total[18:19, 64 + e : 65 + e])
+        alog_out[e] = jnp.sum(line[:, e : e + 1])
+        bias_out[e] = jnp.sum(line[:, 32 + e : 33 + e])
+        skip_out[e] = jnp.sum(line[:, 64 + e : 65 + e])
     shared = jnp.concatenate(
         [
             jnp.concatenate([total[8:12], total[12:16]], axis=1),
@@ -622,17 +628,20 @@
         scratch=[pltpu.VMEM((ROWS + T, 384), F32)],
     )(rows, conv_x, conv_b, head, where)
     received = ctx_swap(send)
-    xbc, slopes, inside, kept = call(
+    xbc, slopes, inside, kept, order = call(
         within_kernel,
-        [sds((T, 512), BF), sds((T, 512), F32), wide, sds((HD, T, T), BF)],
+        [sds((T, 512), BF), sds((T, 512), F32), wide, sds((HD, T, T), BF), sds((8, 128), F32)],
         "vvvvvsvv",
         scratch=[ext],
         flops=10**8,
         bytes_accessed=3 * 10**6,
     )(rows, halo, conv_x, conv_b, conv_c, where, step, cum)
     send, decays = call(
-        scan_kernel, [chunk, chunk], "vvvs", scratch=[pltpu.VMEM((CW, 128), F32)]
-    )(received, conv_x, conv_b, where)
+        scan_kernel,
+        [chunk, chunk],
+        "vvvsv",
+        scratch=[pltpu.VMEM((CW, 128), F32)] + [pltpu.VMEM((blocks, 8, 128), F32)] * 2,
+    )(received, conv_x, conv_b, where, order)
     carried = ctx_swap(send).reshape(T, 128)
     y, mixed, sums = call(
         mix_kernel, [wide, sds((T, CW), BF), sds((8, T), F32)], "vvvvvvss"
@@ -658,7 +667,7 @@
     end_grad = ctx_swap(send).reshape(T, 128)
     pre, dt_grad, send = call(
         leave_kernel,
-        [sds((T, 512), F32), slim, sds((blocks, 32, 128), F32)],
+        [sds((T, 512), F32), slim, sds((blocks, 32, 128), BF)],
         "vvvs" + "v" * 9,
         scratch=[ext],
     )(

time: 159 us -> 149 us (0.937)
  blocking collectives: 88.7 us -> 72.4 us
  starting transfers between devices: 25.1 us -> 30.7 us
  waiting for transfers between devices: 25 us -> 28.1 us
  Pallas kernels: 18.3 us -> 16 us
    all_to_all x3, blocking collectives: 65.8 us -> 50.3 us  [ctx_swap(): return lax.all_to_all(value, 'ctx', 0, 0, tiled=True)]
    all_to_all x2, starting transfers between devices: 10.8 us -> 16.4 us  [ctx_swap(): return lax.all_to_all(value, 'ctx', 0, 0, tiled=True)]
    all_to_all x2, waiting for transfers between devices: 14.3 us -> 17.4 us  [ctx_swap(): return lax.all_to_all(value, 'ctx', 0, 0, tiled=True)]
    pallas_call x2, Pallas kernels: 5.82 us -> 2.78 us  [the longest x1 1.65 us: per_device(): call(leave_kernel, [sds((T, 512), F32), slim, sds((blocks, 32, 128), BF)]...]
where the time goes in v4:
time: 149 us
  blocking collectives  72.4 us (49%)
  starting transfers between devices  30.7 us (21%)
  waiting for transfers between devices  28.1 us (19%)
  Pallas kernels  16 us (11%)
    all_to_all x3, blocking collectives, ctx_swap(): return lax.all_to_all(value, 'ctx', 0, 0, tiled=True)  50.3 us
    all_to_all x1, blocking collectives, head_swap(): return lax.all_to_all(value, 'head', 0, 0, tiled=True)  18.1 us
    all_to_all x2, waiting for transfers between devices, ctx_swap(): return lax.all_to_all(value, 'ctx', 0, 0, tiled=True)  17.4 us
    all_to_all x2, starting transfers between devices, ctx_swap(): return lax.all_to_all(value, 'ctx', 0, 0, tiled=True)  16.4 us
    all_to_all x1, starting transfers between devices, head_swap(): return lax.all_to_all(value, 'head', 0, 0, tiled=True)  10.3 us
    all_to_all x1, waiting for transfers between devices, head_swap(): return lax.all_to_all(value, 'head', 0, 0, tiled=True)  9.85 us
    psum x1, blocking collectives, per_device(): lax.psum(sums, 'head', axis_index_groups=[[g * per + i for i in range(per...  4.04 us
    ppermute x1, starting transfers between devices, per_device(): lax.ppermute(arrived[ways - 1, :, 0:512], 'ctx', [(i, i + 1) for i in ran...  4.03 us
  transfers between devices with their start and end apart: 4, of which 4 were waited for; matrix products, arithmetic and copies ran while one was open for 0% of the time, Pallas kernels for 2%

profile of v4, /device:TPU:1, one launch (start us, length us, event | category | flops | bytes accessed | tf_op | source)
XLA Modules:
  0.0 148.8 jit_solution(2012543195795630378)
XLA Ops:
  0.6 2.1 %shard_map.220 = bf16[16,16,1152]{2,1,0:T(8,128)(2,1)} custom-call(bf16[16,4096]{1,0:T(8,128)(2,1)} %x_at.1, bf16[16,1024]{1,0:T(8,128)(2,1)} %b_at.1, bf16[16,1024]{1,0:T(8,128)(2,1)} %c_at.1, bf16[16,64]{1,0:T(8,128)(2,1)} %dt_at.1, bf16[16,4096]{1,0:T(8,128)(2,1)} %gate_at.1, bf16[16,4096]{1,0:T(8,128)(2,1)} %grad_at.1), custom_call_target="tpu_custom_call" | custom-call | tf_op jit(solution)/shard_map/pallas_call | solution.py:607
  2.7 10.3 %all-to-all-start = ((bf16[16,16,1152]{2,1,0:T(8,128)(2,1)}), bf16[16,16,1152]{2,1,0:T(8,128)(2,1)S(1)}, u32[]{:S(2)}, u32[]{:S(2)}) async-start(bf16[16,16,1152]{2,1,0:T(8,128)(2,1)} %shard_map.220), calls=%async_computation | async-start | bytes 1179648 | tf_op jit(solution)/shard_map/all_to_all | solution.py:604
  13.8 9.8 %all-to-all-done = bf16[16,16,1152]{2,1,0:T(8,128)(2,1)S(1)} async-done(((bf16[16,16,1152]{2,1,0:T(8,128)(2,1)}), bf16[16,16,1152]{2,1,0:T(8,128)(2,1)S(1)}, u32[]{:S(2)}, u32[]{:S(2)}) %all-to-all-start) | async-done | bytes 589856 | tf_op jit(solution)/shard_map/all_to_all | solution.py:604
  23.6 2.3 %shard_map.221 = (f32[256,128]{1,0:T(8,128)S(1)}, f32[256,128]{1,0:T(8,128)S(1)}, f32[32,24,128]{2,1,0:T(8,128)}) custom-call(bf16[256,1152]{1,0:T(8,128)(2,1)S(1)} %bitcast.10, f32[4,256]{1,0:T(4,128)S(1)} %copy-done.5, f32[4,1024]{1,0:T(4,128)S(1)} %copy-done, f32[12]{0:T(128)S(1)} %pad_maximum_fusion.head, s32[3]{0:T(128)S(1)} %pad_add_fusion.where), custom_call_target="tpu_custom_call" | custom-call | tf_op jit(solution)/shard_map/pallas_call | solution.py:624
  25.9 12.1 %all-to-all-start.1 = ((f32[32,24,128]{2,1,0:T(8,128)}), f32[32,24,128]{2,1,0:T(8,128)S(1)}, u32[]{:S(2)}, u32[]{:S(2)}) async-start(f32[32,24,128]{2,1,0:T(8,128)} %get-tuple-element.47), calls=%async_computation.1 | async-start | bytes 786432 | tf_op jit(solution)/shard_map/all_to_all | solution.py:601
  38.0 4.0 %collective-permute-start = (bf16[16,512]{1,0:T(8,128)(2,1)S(1)}, bf16[16,512]{1,0:T(8,128)(2,1)S(1)}, u32[]{:S(2)}, u32[]{:S(2)}) collective-permute-start(bf16[16,512]{1,0:T(8,128)(2,1)S(1)} %slice_bitcast_fusion), channel_id=1, source_target_pairs={{0,16},{16,32},{32,48},{48,64},{64,80},{80,96},{96,112},{112,128},... | collective-permute-start | bytes 49160 | tf_op jit(solution)/shard_map/ppermute | solution.py:616
  42.0 0.9 collective-permute-done.halo
  42.9 2.1 %shard_map.222 = (bf16[256,512]{1,0:T(8,128)(2,1)S(1)}, f32[256,512]{1,0:T(8,128)S(1)}, f32[256,256]{1,0:T(8,128)S(1)}, bf16[4,256,256]{2,1,0:T(8,128)(2,1)S(1)}, f32[8,128]{1,0:T(8,128)S(1)}) custom-call(bf16[256,1152]{1,0:T(8,128)(2,1)S(1)} %bitcast.11, bf16[16,512]{1,0:T(8,128)(2,1)S(1)} %collective-permute-done.halo, f32[4,256]{1,0:T(4,128)S(1)} %copy-done.5, ...), custom_call_target="tpu_custom_call" | custom-call | flops 100000000 | bytes 3000000 | tf_op jit(solution)/shard_map/pallas_call | solution.py:631
  45.0 7.4 %all-to-all-done.1.received = f32[32,24,128]{2,1,0:T(8,128)S(1)} async-done(((f32[32,24,128]{2,1,0:T(8,128)}), f32[32,24,128]{2,1,0:T(8,128)S(1)}, u32[]{:S(2)}, u32[]{:S(2)}) %all-to-all-start.1) | async-done | bytes 393248 | tf_op jit(solution)/shard_map/all_to_all | solution.py:601
  52.4 1.1 shard_map.223
  53.5 21.0 %all_to_all.35 = f32[32,8,128]{2,1,0:T(8,128)S(1)} all-to-all(f32[32,8,128]{2,1,0:T(8,128)S(1)} %get-tuple-element.51), channel_id=1, replica_groups=mesh['ctx'=32,'head'=16] {'ctx'}, dimensions={0} | all-to-all | bytes 262144 | tf_op jit(solution)/shard_map/all_to_all | solution.py:601
  74.6 1.0 shard_map.224
  75.5 4.0 %psum.7.message = f32[8,256]{1,0:T(8,128)S(1)} all-reduce(f32[8,256]{1,0:T(8,128)S(1)} %get-tuple-element.54), channel_id=1, replica_groups={{0,1},{2,3},{4,5},{6,7},{8,9},{10,11},{12,13},{14,15},{16,17},{18,19},{..., use_global_device_ids=true, to_apply=%region_0.1 | all-reduce | flops 2048 | bytes 16384 | tf_op jit(solution)/shard_map/psum | solution.py:650
  79.6 1.4 shard_map.225
  81.0 14.5 %all_to_all.36.received = f32[32,8,128]{2,1,0:T(8,128)S(1)} all-to-all(f32[32,8,128]{2,1,0:T(8,128)S(1)} %get-tuple-element.56), channel_id=1, replica_groups=mesh['ctx'=32,'head'=16] {'ctx'}, dimensions={0} | all-to-all | bytes 262144 | tf_op jit(solution)/shard_map/all_to_all | solution.py:601
  95.4 0.7 shard_map.226
  96.1 4.3 %all-to-all-start.4 = ((f32[32,8,128]{2,1,0:T(8,128)}), f32[32,8,128]{2,1,0:T(8,128)S(1)}, u32[]{:S(2)}, u32[]{:S(2)}) async-start(f32[32,8,128]{2,1,0:T(8,128)} %shard_map.226), calls=%async_computation.4 | async-start | bytes 262144 | tf_op jit(solution)/shard_map/all_to_all | solution.py:601
  100.5 1.4 shard_map.227
  101.9 9.9 %all-to-all-done.4 = f32[32,8,128]{2,1,0:T(8,128)S(1)} async-done(((f32[32,8,128]{2,1,0:T(8,128)}), f32[32,8,128]{2,1,0:T(8,128)S(1)}, u32[]{:S(2)}, u32[]{:S(2)}) %all-to-all-start.4) | async-done | bytes 131104 | tf_op jit(solution)/shard_map/all_to_all | solution.py:601
  111.8 1.6 %shard_map.228 = (f32[256,512]{1,0:T(8,128)S(1)}, f32[256,128]{1,0:T(8,128)S(1)}, bf16[32,32,128]{2,1,0:T(8,128)(2,1)S(1)}) custom-call(f32[256,128]{1,0:T(8,128)S(1)} %bitcast.18, bf16[256,1152]{1,0:T(8,128)(2,1)S(1)} %bitcast.14, bf16[16,512]{1,0:T(8,128)(2,1)S(1)} %collective-permute-done.halo, f32[12]{0:T(128)S(1)} %pad_maximum_fusion.head, ...), custom_call_target="tpu_custom_call" | custom-call | tf_op jit(solution)/shard_map/pallas_call | solution.py:668
  113.5 14.8 %all_to_all.37.received = bf16[32,32,128]{2,1,0:T(8,128)(2,1)S(1)} all-to-all(bf16[32,32,128]{2,1,0:T(8,128)(2,1)S(1)} %get-tuple-element.65), channel_id=1, replica_groups=mesh['ctx'=32,'head'=16] {'ctx'}, dimensions={0} | all-to-all | bytes 524288 | tf_op jit(solution)/shard_map/all_to_all | solution.py:601
  128.3 1.6 %shard_map.229 = (bf16[16,16,1152]{2,1,0:T(8,128)(2,1)S(1)}, f32[4,256]{1,0:T(4,128)}, f32[4]{0:T(128)}, f32[4]{0:T(128)}, f32[4]{0:T(128)}) custom-call(bf16[32,32,128]{2,1,0:T(8,128)(2,1)S(1)} %all_to_all.37.received, s32[3]{0:T(128)S(1)} %pad_add_fusion.where, f32[4,256]{1,0:T(4,128)S(1)} %copy-done.5, f32[4,1024]{1,0:T(4,128)S(1)} %copy-done, ...), custom_call_target="tpu_custom_call" | custom-call | tf_op jit(solution)/shard_map/pallas_call | solution.py:678
  129.9 18.1 %all_to_all.38.received = bf16[16,16,1152]{2,1,0:T(8,128)(2,1)S(1)} all-to-all(bf16[16,16,1152]{2,1,0:T(8,128)(2,1)S(1)} %get-tuple-element.69), channel_id=1, replica_groups=mesh['ctx'=32,'head'=16] {'head'}, dimensions={0} | all-to-all | bytes 1179648 | tf_op jit(solution)/shard_map/all_to_all | solution.py:604
  148.0 0.8 shard_map.230
  (21 shorter events, 0.8 us)
Async XLA Ops:
  2.7 20.9 %all-to-all-start = ((bf16[16,16,1152]{2,1,0:T(8,128)(2,1)}), bf16[16,16,1152]{2,1,0:T(8,128)(2,1)S(1)}, u32[]{:S(2)}, u32[]{:S(2)}) async-start(bf16[16,16,1152]{2,1,0:T(8,128)(2,1)} %shard_map.220), calls=%async_computation | async-start | bytes 1179648 | tf_op jit(solution)/shard_map/all_to_all | solution.py:604
  13.0 10.6 %copy-start = (f32[4,1024]{1,0:T(4,128)S(1)}, f32[4,1024]{1,0:T(4,128)}, u32[]{:S(2)}) copy-start(f32[4,1024]{1,0:T(4,128)} %wb.7) | copy-start | bytes 49156
  13.0 0.7 copy-start.6
  13.0 0.7 copy-start.7
  13.0 0.7 copy-start.8
  13.0 10.6 %copy-start.5 = (f32[4,256]{1,0:T(4,128)S(1)}, f32[4,256]{1,0:T(4,128)}, u32[]{:S(2)}) copy-start(f32[4,256]{1,0:T(4,128)} %wx.7) | copy-start | bytes 12292
  25.9 26.5 %all-to-all-start.1 = ((f32[32,24,128]{2,1,0:T(8,128)}), f32[32,24,128]{2,1,0:T(8,128)S(1)}, u32[]{:S(2)}, u32[]{:S(2)}) async-start(f32[32,24,128]{2,1,0:T(8,128)} %get-tuple-element.47), calls=%async_computation.1 | async-start | bytes 786432 | tf_op jit(solution)/shard_map/all_to_all | solution.py:601
  38.0 4.9 %copy-start.4 = (f32[4,1024]{1,0:T(4,128)S(1)}, f32[4,1024]{1,0:T(4,128)}, u32[]{:S(2)}) copy-start(f32[4,1024]{1,0:T(4,128)} %wc.3) | copy-start | bytes 49156
  38.0 4.9 %collective-permute-start = (bf16[16,512]{1,0:T(8,128)(2,1)S(1)}, bf16[16,512]{1,0:T(8,128)(2,1)S(1)}, u32[]{:S(2)}, u32[]{:S(2)}) collective-permute-start(bf16[16,512]{1,0:T(8,128)(2,1)S(1)} %slice_bitcast_fusion), channel_id=1, source_target_pairs={{0,16},{16,32},{32,48},{48,64},{64,80},{80,96},{96,112},{112,128},... | collective-permute-start | bytes 49160 | tf_op jit(solution)/shard_map/ppermute | solution.py:616
  53.5 21.0 %copy-start.3 = (f32[4096]{0:T(1024)S(1)}, f32[4096]{0:T(1024)}, u32[]{:S(2)}) copy-start(f32[4096]{0:T(1024)} %param.25) | copy-start | bytes 49156
  81.0 14.5 %copy-start.1 = (bf16[256,256]{1,0:T(8,128)(2,1)}, bf16[256,256]{1,0:T(8,128)(2,1)S(1)}, u32[]{:S(2)}) copy-start(bf16[256,256]{1,0:T(8,128)(2,1)S(1)} %get-tuple-element.68.gate_grad) | copy-start | bytes 393220
  96.1 15.7 %all-to-all-start.4 = ((f32[32,8,128]{2,1,0:T(8,128)}), f32[32,8,128]{2,1,0:T(8,128)S(1)}, u32[]{:S(2)}, u32[]{:S(2)}) async-start(f32[32,8,128]{2,1,0:T(8,128)} %shard_map.226), calls=%async_computation.4 | async-start | bytes 262144 | tf_op jit(solution)/shard_map/all_to_all | solution.py:601
  113.5 14.8 %copy-start.2 = (bf16[256,256]{1,0:T(8,128)(2,1)S(1)}, bf16[256,256]{1,0:T(8,128)(2,1)}, u32[]{:S(2)}) copy-start(bf16[256,256]{1,0:T(8,128)(2,1)} %copy-done.1) | copy-start | bytes 393220

commit v5 on v4

--- a/solution.py
+++ b/solution.py
@@ -17,7 +17,8 @@
 KT = 4
 ROWS = 16
 IN_W = 1152
-OUT_W = 1152
+OUT_W = 896
+BASE = 21
 VMEM_LIMIT = 8 * 1024 * 1024
 PACK_LIMIT = 60 * 1024 * 1024
 
@@ -114,16 +115,6 @@
 def silu_slope(pre):
     gate = jax.nn.sigmoid(pre)
     return pre * gate, gate * (1.0 + pre * (1.0 - gate))
-
-
-def three_rows(row, count):
-    at = iota((count, row.shape[1]), 0)
-    high, middle, low = pieces(row, 3)
-    return jnp.where(
-        at == 0,
-        high.astype(F32),
-        jnp.where(at == 1, middle.astype(F32), jnp.where(at == 2, low.astype(F32), 0.0)),
-    ).astype(BF)
 
 
 def enter_math(ext, dt_cols, wx, wb, bias_row, alog_row):
@@ -145,26 +136,49 @@
 def within_math(x_act, b_act, c_act, step, cum, cum_t):
     scores = dot(c_act, b_act, 1, 1)
     stepped = x_act.astype(F32) * spread(step)
-    outs, kept = [], []
+    outs = []
     for e in range(HD):
         mix = (scores * gap_decay(cum, cum_t, e)).astype(BF)
-        kept.append(mix)
         part = stepped[:, e * PS : (e + 1) * PS]
         high, low = pieces(part, 2)
         both = dot(mix, jnp.concatenate([high, low], axis=1), 1, 0)
         outs.append(both[:, :PS] + both[:, PS:])
-    return jnp.concatenate(outs, axis=1), kept
-
-
-def mix_math(x_act, c_act, inside, carried, cum, skip_row, gate, out_grad, gain):
-    grown = spread(jnp.exp(cum))
-    y = inside + grown * dot_right(c_act, carried, 1, 1)
-    mixed = (y + skip_row * x_act.astype(F32)).astype(BF)
-    gate_act = gate * jax.nn.sigmoid(gate)
-    v = mixed.astype(F32) * gate_act
-    squares = jnp.sum(v * v, axis=1, keepdims=True)
-    along = jnp.sum(out_grad * gain * v, axis=1, keepdims=True)
-    return y, mixed, squares, along
+    return jnp.concatenate(outs, axis=1)
+
+
+def rim_rows(columns):
+    x_rim = columns.T[0:8]
+    lane = iota((8, 128), 1)
+    both = jnp.zeros((8, 128), F32)
+    for i in range(T // 8):
+        part = pltpu.roll(columns[8 * i : 8 * i + 8], (4 * i + 4 - BASE) % 128, 1)
+        both = jnp.where(lane // 4 == i, part, both)
+    return jnp.concatenate([x_rim, both, pltpu.roll(both, 5, 0)], axis=1)
+
+
+def spread_eight(cols):
+    lane = iota(cols.shape, 1)
+    out = jnp.zeros(cols.shape, F32)
+    for e in range(HD):
+        out = jnp.where(lane // 8 == e, jnp.broadcast_to(cols[:, e : e + 1], cols.shape), out)
+    return out
+
+
+def early_math(x_first, b_first, c_act, step, cum):
+    lane, row = iota((T, 128), 1), iota((T, 128), 0)
+    b_rows = jnp.concatenate([b_first] * HD + [jnp.zeros((128 - 8 * HD, 128), F32)], axis=0)
+    scores = dot(c_act, b_rows.astype(BF), 1, 1)
+    at_first = spread_eight(cum[0:8])
+    at_first = jnp.sum(
+        jnp.where(iota((8, 128), 0) == iota((8, 128), 1) % 8, at_first, 0.0), axis=0, keepdims=True
+    )
+    use = (lane % 8 < KT - 1) & (lane < 8 * HD) & (row >= lane % 8)
+    gap = jnp.where(use, spread_eight(cum) - at_first, 0.0)
+    mix = jnp.where(use, scores * jnp.exp(gap), 0.0).astype(BF)
+    stepped = x_first * spread(step[0:8])
+    blocks = jnp.concatenate([stepped] * HD + [jnp.zeros((128 - 8 * HD, CW), F32)], axis=0)
+    blocks = jnp.where(iota((128, CW), 0) // 8 == iota((128, CW), 1) // PS, blocks, 0.0)
+    return dot_right(mix, blocks, 1, 0)
 
 
 def norm_math(mixed, gate, out_grad, gain, squares, along, c_act, cum):
@@ -183,16 +197,18 @@
     return y_grad, gate_grad, gain_grad, start_grad
 
 
-def within_back_math(x_act, b_act, c_act, step, cum, cum_t, kept, y, y_grad, carried):
+def within_back_math(x_act, b_act, c_act, step, cum, cum_t, y, y_grad, carried):
     lifted = y_grad.astype(F32) * spread(jnp.exp(cum))
+    scores = dot(c_act, b_act, 1, 1)
     score_grad = jnp.zeros((T, T), F32)
     x_parts = []
     step_t = step.T
     for e in range(HD):
         cut = slice(e * PS, (e + 1) * PS)
-        x_parts.append(dot(kept[e], y_grad[:, cut], 0, 0))
+        decay = gap_decay(cum, cum_t, e)
+        x_parts.append(dot((scores * decay).astype(BF), y_grad[:, cut], 0, 0))
         mix_grad = dot(y_grad[:, cut], x_act[:, cut], 1, 1)
-        score_grad = score_grad + mix_grad * (gap_decay(cum, cum_t, e) * step_t[e : e + 1, :])
+        score_grad = score_grad + mix_grad * (decay * step_t[e : e + 1, :])
     x_in = jnp.concatenate(x_parts, axis=1)
     score_grad = score_grad.astype(BF)
     c_grad = dot(score_grad, b_act, 1, 0) + dot_both(lifted, carried, 1, 0)
@@ -234,13 +250,6 @@
     return x_grad, b_grad, dt_grad, alog_grad, bias_grad
 
 
-def conv_slopes(ext, wx, wb, wc):
-    def slope(weight, lo, hi):
-        return silu_slope(taps(ext, weight, lo, hi))[1]
-
-    return jnp.concatenate([slope(wx, 0, 256), slope(wb, 256, 384), slope(wc, 384, 512)], axis=1)
-
-
 def weight_grads(ext, pre_grad):
     return [
         jnp.sum(pre_grad * ext[ROWS - KT + 1 + k : ROWS - KT + 1 + k + T], axis=0, keepdims=True)
@@ -337,47 +346,75 @@
     step_out[...] = step
     cum_out[...] = cum
     count = send.shape[0]
+    lane, row = iota((8, 128), 1), iota((8, 128), 0)
     first = ext[ROWS : ROWS + 8]
+    end = rows[T - ROWS : T, 256:512].astype(F32)[8:16]
     last = pltpu.roll(ext[ROWS + T - 8 : ROWS + T], 6, 0)
     rim = jnp.where(iota((8, 384), 0) < 3, first, last)
-    ends = jnp.where(iota((8, CW), 0) < 3, first_end, final)
-    columns = jnp.concatenate([rim[:, 0:CW], ends, jnp.zeros((112, CW), F32)], axis=0).T
-    send[:, 0:8] = fresh.reshape(count, 8, 128)
-    send[:, 8:16] = columns.reshape(count, 8, 128)
+    end_high = first_end.astype(BF).astype(F32)
+    final_parts = [piece.astype(F32) for piece in pieces(final, 3)]
+    wide_row = iota((8, CW), 0)
+    ends = jnp.where(wide_row < 3, end_high, pltpu.roll(first_end - end_high, 3, 0))
+    ends = jnp.where(wide_row == 6, final_parts[0], jnp.where(wide_row == 7, final_parts[1], ends))
+    columns = jnp.concatenate(
+        [rim[:, 0:CW], ends, final_parts[2], jnp.zeros((104, CW), F32)], axis=0
+    ).T
+    both = jnp.where(row < 3, pltpu.roll(end, 3, 0)[:, 0:128], pltpu.roll(end, 6, 0)[:, 128:256])
+    b_rim = rim[:, 256:384]
+    b_part = b_rim
+    for t in range(3):
+        moved = pltpu.roll(b_rim, BASE * (t + 1), 1)
+        there = lane // BASE == t + 1
+        b_part = jnp.where((row == 6) & there, moved[t : t + 1], b_part)
+        b_part = jnp.where((row == 7) & there, moved[t + 3 : t + 4], b_part)
+    tiles = []
     for i in range(count):
-        send[i, 16:24] = rim[:, 256:384]
-
-
-def within_kernel(rows, halo, wx, wb, wc, where, step, cum, xbc, slopes, inside, kept, order, ext):
-    ext[0:ROWS] = halo[...].astype(F32)
-    ext[ROWS : ROWS + T] = rows[:, 0:512].astype(F32)
-    acts = []
+        part = pltpu.roll(both, (BASE - 4 - 4 * i) % 128, 1)
+        tile = jnp.where(lane < BASE - 4, columns[8 * i : 8 * i + 8], part)
+        tiles.append(jnp.where(lane < BASE, tile, b_part)[None])
+    high = fresh.astype(BF).astype(F32)
+    shape = (count, 8, 128)
+    send[...] = jnp.concatenate(
+        [high.reshape(shape), (fresh - high).reshape(shape), jnp.concatenate(tiles, axis=0)], axis=1
+    ).astype(BF)
+
+
+def conv_rows(ext, wx, wb, wc, where):
     for weight, lo, hi in (
         (wx[...], 0, 256),
         (group_lanes(wb, where), 256, 384),
         (group_lanes(wc, where), 384, 512),
     ):
-        value, slope = silu_slope(taps(ext, weight, lo, hi))
-        acts.append(value.astype(BF))
+        yield lo, hi, taps(ext, weight, lo, hi)
+
+
+def within_kernel(rows, wx, wb, wc, where, step, cum, after, xbc, inside, ext):
+    del after
+    ext[0:ROWS] = jnp.zeros((ROWS, 512), F32)
+    ext[ROWS : ROWS + T] = rows[:, 0:512].astype(F32)
+    acts = []
+    for lo, hi, pre in conv_rows(ext, wx, wb, wc, where):
+        late = iota((T, hi - lo), 0) >= KT - 1
+        acts.append(jnp.where(late, pre * jax.nn.sigmoid(pre), 0.0).astype(BF))
         xbc[:, lo:hi] = acts[-1]
-        slopes[:, lo:hi] = slope
     step, cum = step[...], cum[...]
-    out, mixes = within_math(*acts, step, cum, cum.T)
-    inside[...] = out
-    order[...] = out[0:8, 0:128]
-    for e in range(HD):
-        kept[e] = mixes[e]
-
-
-def scan_kernel(received, wx, wb, where, order, send, decays, columns, fresh, grown):
-    del order
+    inside[...] = within_math(*acts, step, cum, cum.T)
+
+
+def scan_kernel(received, wx, wb, where, send, decays, columns, fresh, states):
     count = received.shape[0]
     columns[...] = jnp.concatenate([wx[...], jnp.zeros((128 - KT, CW), F32)], axis=0).T
     mine = columns[pl.ds(pl.multiple_of(where[2] * 8, 8), 8), :]
     taps_b = group_lanes(wb, where)
     shape = (count, 8, 128)
     lane, row = iota(shape, 2), iota(shape, 1)
-    x_rim, b_rim = received[:, 8:16], received[:, 16:24]
+    message = received[...].astype(F32)
+    x_rim = message[:, 16:24]
+    low = x_rim
+    for t in range(3):
+        moved = pltpu.roll(x_rim, 128 - BASE * (t + 1), 2)
+        low = jnp.where(row == t, moved[:, 6:7], jnp.where(row == t + 3, moved[:, 7:8], low))
+    b_rim = jnp.where(lane < BASE, low, x_rim)
     blank = jnp.zeros((1, 8, 128), F32)
     x_last = jnp.concatenate([blank, x_rim[:-1]], axis=0)
     b_last = jnp.concatenate([blank, b_rim[:-1]], axis=0)
@@ -388,25 +425,32 @@
     for k in range(1, KT):
         x_pre = x_pre + mine[None, :, k : k + 1] * pltpu.roll(x_seen, 128 - k, 2)
         b_pre = b_pre + taps_b[None, k : k + 1] * pltpu.roll(b_seen, 8 - k, 1)
-    x_act = (x_pre * jax.nn.sigmoid(x_pre)).astype(BF).astype(F32) * pltpu.roll(x_rim, 120, 2)
+    to_end = pltpu.roll(x_rim, 120, 2) + pltpu.roll(x_rim, 117, 2)
+    x_act = (x_pre * jax.nn.sigmoid(x_pre)).astype(BF).astype(F32) * to_end
     b_act = (b_pre * jax.nn.sigmoid(b_pre)).astype(BF).astype(F32)
-    total = received[:, 0:8]
+    total = message[:, 0:8] + message[:, 8:16]
     for t in range(KT - 1):
         total = total + x_act[:, :, t : t + 1] * b_act[:, t : t + 1, :]
     fresh[...] = total
-    grown[...] = jnp.exp(jnp.broadcast_to(x_rim[:, :, 11:12], shape))
-    decays[...] = grown[...]
+    final = x_rim[:, :, 14:15] + x_rim[:, :, 15:16] + x_rim[:, :, 16:17]
+    decays[...] = jnp.exp(jnp.broadcast_to(final, shape))
     state = jnp.zeros((8, 128), F32)
     for i in range(count):
-        send[i] = state
-        state = grown[i] * state + fresh[i]
-
-
-def scan_back_kernel(received, decays, send):
+        states[i] = state
+        state = decays[i] * state + fresh[i]
+    state = states[...]
+    high = state.astype(BF).astype(F32)
+    back = jnp.where(lane < 3, x_seen, x_last)
+    send[...] = jnp.concatenate([high, state - high, back], axis=1).astype(BF)
+
+
+def scan_back_kernel(received, decays, send, states):
+    message = received[...].astype(F32)
     state = jnp.zeros((8, 128), F32)
     for i in reversed(range(received.shape[0])):
-        send[i] = state
-        state = decays[i] * state + received[i]
+        states[i] = state
+        state = decays[i] * state + message[i]
+    send[...] = states[...].astype(BF)
 
 
 def pair_rows(squares, along):
@@ -415,21 +459,39 @@
     return both.T[0:8, :]
 
 
-def mix_kernel(carried, xbc, inside, cum, rows, gain, head, where, y_out, mixed_out, message):
-    y, mixed, squares, along = mix_math(
-        xbc[:, 0:256],
-        xbc[:, 384:512],
-        inside[...],
-        carried[...],
-        cum[...],
-        scalar_row(head, 2 * HD, CW, PS),
-        rows[:, 512:768].astype(F32),
-        rows[:, 768:1024].astype(F32),
-        gain_lanes(gain, where),
-    )
+def mix_kernel(
+    received, xbc_late, inside, step, cum, rows, wx, wb, wc, gain, head, where,
+    y_out, mixed_out, message, xbc, carried_out, rim_out,
+):
+    arrived = received[...].astype(F32)
+    carried = (arrived[:, 0:8] + arrived[:, 8:16]).reshape(T, 128)
+    carried_out[...] = carried
+    rim = rim_rows(arrived[:, 16:24].reshape(T, 128))
+    rim_out[...] = rim
+    raw = rows[0:ROWS, 0:512].astype(F32)[0:8]
+    seen = jnp.where(iota((8, 512), 0) < 3, rim, pltpu.roll(raw, 3, 0))
+    weights = jnp.concatenate([wx[...], group_lanes(wb, where), group_lanes(wc, where)], axis=1)
+    pre = weights[0:1] * seen
+    for k in range(1, KT):
+        pre = pre + weights[k : k + 1] * pltpu.roll(seen, 8 - k, 0)
+    first = jnp.where(iota((8, 512), 0) < 3, pre * jax.nn.sigmoid(pre), 0.0).astype(BF).astype(F32)
+    late = xbc_late[...]
+    whole = jnp.concatenate([(late[0:ROWS].astype(F32) + jnp.concatenate([first, jnp.zeros((8, 512), F32)], axis=0)).astype(BF), late[ROWS:T]], axis=0)
+    xbc[...] = whole
+    x_act, c_act = whole[:, 0:256], whole[:, 384:512]
+    cum = cum[...]
+    early = early_math(first[:, 0:256], first[:, 256:384], c_act, step[...], cum)
+    grown = spread(jnp.exp(cum))
+    y = inside[...] + early + grown * dot_right(c_act, carried, 1, 1)
+    mixed = (y + scalar_row(head, 2 * HD, CW, PS) * x_act.astype(F32)).astype(BF)
+    gate = rows[:, 512:768].astype(F32)
+    v = mixed.astype(F32) * (gate * jax.nn.sigmoid(gate))
+    scaled = rows[:, 768:1024].astype(F32) * gain_lanes(gain, where)
     y_out[...] = y
     mixed_out[...] = mixed
-    message[...] = pair_rows(squares, along)
+    message[...] = pair_rows(
+        jnp.sum(v * v, axis=1, keepdims=True), jnp.sum(scaled * v, axis=1, keepdims=True)
+    )
 
 
 def norm_kernel(message, mixed, rows, gain, xbc, cum, where, y_grad_out, gate_out, gain_out, send):
@@ -447,10 +509,21 @@
     y_grad_out[...] = y_grad
     gate_out[...] = gate_grad
     gain_out[...] = jnp.broadcast_to(gain_grad, (8, CW))
-    send[...] = start_grad.reshape(send.shape)
-
-
-def back_kernel(xbc, step, cum, kept, y, y_grad, carried, middle, dots):
+    send[...] = start_grad.reshape(send.shape).astype(BF)
+
+
+def place_rim(ext, rim):
+    ext[0:8] = jnp.zeros((8, ext.shape[1]), F32)
+    ext[8:ROWS] = pltpu.roll(rim, 5, 0)
+
+
+def back_kernel(
+    rows, rim, wx, wb, wc, where, xbc, step, cum, y, y_grad, carried, middle, dots, slopes, ext
+):
+    place_rim(ext, rim[...])
+    ext[ROWS : ROWS + T] = rows[:, 0:512].astype(F32)
+    for lo, hi, pre in conv_rows(ext, wx, wb, wc, where):
+        slopes[:, lo:hi] = silu_slope(pre)[1]
     cum = cum[...]
     x_in, b_in, c_grad, out_dots, in_dots, skip_grad = within_back_math(
         xbc[:, 0:256],
@@ -459,7 +532,6 @@
         step[...],
         cum,
         cum.T,
-        [kept[e] for e in range(HD)],
         y[...],
         y_grad[...],
         carried[...],
@@ -472,10 +544,10 @@
 
 
 def leave_kernel(
-    end_grad, rows, halo, head, xbc, step, cum, y_grad, middle, dots, carried, gain_grad, slopes,
+    end_grad, rows, rim, head, xbc, step, cum, y_grad, middle, dots, carried, gain_grad, slopes,
     pre_out, dt_out, send, ext,
 ):
-    ext[0:ROWS] = halo[...].astype(F32)
+    place_rim(ext, rim[...])
     ext[ROWS : ROWS + T] = rows[:, 0:512].astype(F32)
     alog_row = scalar_row(head, 0, 128, 1)
     step = step[...]
@@ -496,7 +568,7 @@
         jnp.where(live, both, 0.0),
         jnp.where(live, pltpu.roll(both, 64, 1), 0.0),
         carried[...],
-        end_grad[...],
+        end_grad[...].astype(F32),
     )
     dt_out[...] = dt_grad
     pre = jnp.concatenate([x_grad, b_grad, middle[:, 384:512]], axis=1) * slopes[...]
@@ -536,43 +608,40 @@
         alog_out[e] = jnp.sum(line[:, e : e + 1])
         bias_out[e] = jnp.sum(line[:, 32 + e : 33 + e])
         skip_out[e] = jnp.sum(line[:, 64 + e : 65 + e])
-    shared = jnp.concatenate(
-        [
-            jnp.concatenate([total[8:12], total[12:16]], axis=1),
-            jnp.concatenate([total[16:17], total[17:18]], axis=1),
-        ],
-        axis=0,
-    )
-    high = shared.astype(BF).astype(F32)
-    middle = (shared - high).astype(BF).astype(F32)
-    low = shared - high - middle
-    shared = jnp.concatenate([high, middle, low, jnp.zeros((1, 256), F32)], axis=0).astype(BF)
     dt_low = dt_grad[...].astype(BF)
-    for j in range(send.shape[0]):
+    lane, row = iota((128, 128), 1), iota((128, 128), 0)
+    apart = dot(dt_low, ((lane // ROWS == row) & (row < HD)).astype(BF), 1, 0)
+    apart = jnp.where(iota((T, 128), 0) % ROWS == iota((T, 128), 1) % ROWS, apart, 0.0).astype(BF)
+    ways = send.shape[0]
+    joined = dot((iota((ways, T), 1) // ROWS == iota((ways, T), 0)).astype(BF), apart, 1, 0)
+    shared = jnp.concatenate([total[8:18], jnp.zeros((6, 128), F32)], axis=0)
+    row = iota((ROWS, 128), 0)
+    for j in range(ways):
         cut = slice(j * ROWS, (j + 1) * ROWS)
         send[j, :, 0:256] = x_grad[cut]
         send[j, :, 256:384] = b_grad[cut]
         send[j, :, 384:512] = c_grad[cut]
         send[j, :, 512:768] = gate_grad[cut, :]
-        send[j, :, 768:896] = dt_low[cut]
-        send[j, :, 896:1152] = shared
+        send[j, :, 768:896] = jnp.where(row == 10, joined[j : j + 1], shared).astype(BF)
 
 
 def unpack_kernel(received, x_out, b_out, c_out, dt_out, gate_out, conv_b_out, conv_c_out, gain_out):
     ways = received.shape[0]
-    lane = iota((ROWS, 128), 1)
-    dt = jnp.zeros((ROWS, 128), F32)
-    shared = []
+    shared, lines = [], []
     for j in range(ways):
         own = slice(j * CW, (j + 1) * CW)
         x_out[:, own] = received[j, :, 0:256]
         gate_out[:, own] = received[j, :, 512:768]
-        turned = pltpu.roll(received[j, :, 768:896].astype(F32), HD * j, 1)
-        dt = jnp.where(lane // HD == j, turned, dt)
-        three = received[j, :, 896:1152].astype(F32)
-        shared.append(three[0:5] + three[5:10] + three[10:15])
-        gain_out[:, own] = shared[j][4:5, :]
-    dt_out[...] = dt[:, 0 : dt_out.shape[1]].astype(BF)
+        shared.append(received[j, :, 768:896].astype(F32))
+        lines.append(shared[j][10:11])
+        gain_out[:, own] = jnp.concatenate([shared[j][8:9], shared[j][9:10]], axis=1)
+    lines = jnp.concatenate(lines, axis=0)
+    heads = dt_out.shape[1]
+    dt = jnp.zeros((ROWS, heads), F32)
+    for e in range(HD):
+        place = (iota((ways, heads), 1) == HD * iota((ways, heads), 0) + e).astype(BF)
+        dt = dt + dot(lines[:, e * ROWS : (e + 1) * ROWS].astype(BF), place, 0, 0)
+    dt_out[...] = dt.astype(BF)
     per = ways // GROUPS
     for g in range(GROUPS):
         cut = slice(g * N, (g + 1) * N)
@@ -583,8 +652,8 @@
             w_sum = w_sum + shared[j]
         b_out[:, cut] = b_sum.astype(BF)
         c_out[:, cut] = c_sum.astype(BF)
-        conv_b_out[:, cut] = w_sum[0:KT, 0:128]
-        conv_c_out[:, cut] = w_sum[0:KT, 128:256]
+        conv_b_out[:, cut] = w_sum[0:KT]
+        conv_c_out[:, cut] = w_sum[KT : 2 * KT]
 
 
 def per_device(
@@ -613,57 +682,60 @@
     )(*inputs)[0]
     arrived = head_swap(sent)
     rows = arrived.reshape(T, IN_W)
-    halo = lax.ppermute(
-        arrived[ways - 1, :, 0:512], "ctx", [(i, i + 1) for i in range(blocks - 1)]
-    )
     wide = sds((T, CW), F32)
     slim = sds((T, 128), F32)
     chunk = sds((blocks, T // blocks, 128), F32)
+    half_chunk = sds((blocks, T // blocks, 128), BF)
     ext = pltpu.VMEM((ROWS + T, 512), F32)
 
     step, cum, send = call(
         enter_kernel,
-        [slim, slim, sds((blocks, 24, 128), F32)],
+        [slim, slim, sds((blocks, 24, 128), BF)],
         "vvvss",
         scratch=[pltpu.VMEM((ROWS + T, 384), F32)],
     )(rows, conv_x, conv_b, head, where)
     received = ctx_swap(send)
-    xbc, slopes, inside, kept, order = call(
+    send, decays = call(
+        scan_kernel,
+        [sds((blocks, 24, 128), BF), chunk],
+        "vvvs",
+        scratch=[pltpu.VMEM((CW, 128), F32)] + [pltpu.VMEM((blocks, 8, 128), F32)] * 2,
+    )(received, conv_x, conv_b, where)
+    received = ctx_swap(send)
+    xbc, inside = call(
         within_kernel,
-        [sds((T, 512), BF), sds((T, 512), F32), wide, sds((HD, T, T), BF), sds((8, 128), F32)],
-        "vvvvvsvv",
+        [sds((T, 512), BF), wide],
+        "vvvvsvvv",
         scratch=[ext],
         flops=10**8,
         bytes_accessed=3 * 10**6,
-    )(rows, halo, conv_x, conv_b, conv_c, where, step, cum)
-    send, decays = call(
-        scan_kernel,
-        [chunk, chunk],
-        "vvvsv",
-        scratch=[pltpu.VMEM((CW, 128), F32)] + [pltpu.VMEM((blocks, 8, 128), F32)] * 2,
-    )(received, conv_x, conv_b, where, order)
-    carried = ctx_swap(send).reshape(T, 128)
-    y, mixed, sums = call(
-        mix_kernel, [wide, sds((T, CW), BF), sds((8, T), F32)], "vvvvvvss"
-    )(carried, xbc, inside, cum, rows, gain, head, where)
+    )(rows, conv_x, conv_b, conv_c, where, step, cum, decays)
+    y, mixed, sums, xbc, carried, rim = call(
+        mix_kernel,
+        [wide, sds((T, CW), BF), sds((8, T), F32), sds((T, 512), BF), slim, sds((8, 512), F32)],
+        "vvvvvvvvvvss",
+    )(received, xbc, inside, step, cum, rows, conv_x, conv_b, conv_c, gain, head, where)
     per = ways // GROUPS
     sums = lax.psum(
         sums, "head", axis_index_groups=[[g * per + i for i in range(per)] for g in range(GROUPS)]
     )
     y_grad, gate_grad, gain_grad, send = call(
         norm_kernel,
-        [sds((T, CW), BF), sds((T, CW), BF), sds((8, CW), F32), chunk],
+        [sds((T, CW), BF), sds((T, CW), BF), sds((8, CW), F32), half_chunk],
         "vvvvvvs",
     )(sums, mixed, rows, gain, xbc, cum, where)
     received = ctx_swap(send)
-    middle, dots = call(
+    middle, dots, slopes = call(
         back_kernel,
-        [sds((T, 512), F32), sds((T + 8, 128), F32)],
-        "vvvvvvv",
+        [sds((T, 512), F32), sds((T + 8, 128), F32), sds((T, 512), F32)],
+        "vvvvvsvvvvvv",
+        scratch=[ext],
         flops=3 * 10**8,
         bytes_accessed=4 * 10**6,
-    )(xbc, step, cum, kept, y, y_grad, carried)
-    send = call(scan_back_kernel, [chunk], "vv")(received, decays)[0]
+    )(rows, rim, conv_x, conv_b, conv_c, where, xbc, step, cum, y, y_grad, carried)
+    send = call(
+        scan_back_kernel, [half_chunk], "vv", scratch=[pltpu.VMEM((blocks, 8, 128), F32)]
+    )(received, decays)[0]
     end_grad = ctx_swap(send).reshape(T, 128)
     pre, dt_grad, send = call(
         leave_kernel,
@@ -671,7 +743,7 @@
         "vvvs" + "v" * 9,
         scratch=[ext],
     )(
-        end_grad, rows, halo, head, xbc, step, cum, y_grad, middle, dots, carried, gain_grad, slopes,
+        end_grad, rows, rim, head, xbc, step, cum, y_grad, middle, dots, carried, gain_grad, slopes,
     )
     received = ctx_swap(send)
     four = sds((HD,), F32)

time: 149 us -> 142 us (0.953)
  starting transfers between devices: 30.7 us -> 19.7 us
  Pallas kernels: 16 us -> 17.7 us
    all_to_all x2, starting transfers between devices: 16.4 us -> 9.48 us  [ctx_swap(): return lax.all_to_all(value, 'ctx', 0, 0, tiled=True)]
    ppermute x1 -> x0, starting transfers between devices: 4.03 us -> none  [per_device(): lax.ppermute(arrived[ways - 1, :, 0:512], 'ctx', [(i, i + 1) for i in ran...]
    all_to_all x3, blocking collectives: 50.3 us -> 52.9 us  [ctx_swap(): return lax.all_to_all(value, 'ctx', 0, 0, tiled=True)]
    all_to_all x1, blocking collectives: 18.1 us -> 16 us  [head_swap(): return lax.all_to_all(value, 'head', 0, 0, tiled=True)]
  transfers between devices with their start and end apart: 4 -> 3, of which waited for: 4 -> 3; matrix products, arithmetic and copies ran while one was open for 0% -> 0% of each run, Pallas kernels for 2% -> 3%
where the time goes in v5:
time: 142 us; the launch traced here: 141 us
  blocking collectives  73.8 us (52%)
  waiting for transfers between devices  27.9 us (20%)
  starting transfers between devices  19.7 us (14%)
  Pallas kernels  17.7 us (12%)
    all_to_all x3, blocking collectives, ctx_swap(): return lax.all_to_all(value, 'ctx', 0, 0, tiled=True)  52.9 us
    all_to_all x2, waiting for transfers between devices, ctx_swap(): return lax.all_to_all(value, 'ctx', 0, 0, tiled=True)  18.1 us
    all_to_all x1, blocking collectives, head_swap(): return lax.all_to_all(value, 'head', 0, 0, tiled=True)  16 us
    all_to_all x1, starting transfers between devices, head_swap(): return lax.all_to_all(value, 'head', 0, 0, tiled=True)  10.3 us
    all_to_all x1, waiting for transfers between devices, head_swap(): return lax.all_to_all(value, 'head', 0, 0, tiled=True)  9.85 us
    all_to_all x2, starting transfers between devices, ctx_swap(): return lax.all_to_all(value, 'ctx', 0, 0, tiled=True)  9.48 us
    psum x1, blocking collectives, per_device(): lax.psum(sums, 'head', axis_index_groups=[[g * per + i for i in range(per...  4.79 us
  transfers between devices with their start and end apart: 3, of which 3 were waited for; matrix products, arithmetic and copies ran while one was open for 0% of the time, Pallas kernels for 3%

profile of v5, /device:TPU:1, one launch (start us, length us, event | category | flops | bytes accessed | tf_op | source)
XLA Modules:
  0.0 140.6 jit_solution(200201989447140326)
XLA Ops:
  0.6 2.1 %shard_map.220 = bf16[16,16,1152]{2,1,0:T(8,128)(2,1)} custom-call(bf16[16,4096]{1,0:T(8,128)(2,1)} %x_at.1, bf16[16,1024]{1,0:T(8,128)(2,1)} %b_at.1, bf16[16,1024]{1,0:T(8,128)(2,1)} %c_at.1, bf16[16,64]{1,0:T(8,128)(2,1)} %dt_at.1, bf16[16,4096]{1,0:T(8,128)(2,1)} %gate_at.1, bf16[16,4096]{1,0:T(8,128)(2,1)} %grad_at.1), custom_call_target="tpu_custom_call" | custom-call | tf_op jit(solution)/shard_map/pallas_call | solution.py:676
  2.7 10.3 %all-to-all-start = ((bf16[16,16,1152]{2,1,0:T(8,128)(2,1)}), bf16[16,16,1152]{2,1,0:T(8,128)(2,1)S(1)}, u32[]{:S(2)}, u32[]{:S(2)}) async-start(bf16[16,16,1152]{2,1,0:T(8,128)(2,1)} %shard_map.220), calls=%async_computation | async-start | bytes 1179648 | tf_op jit(solution)/shard_map/all_to_all | solution.py:673
  13.1 0.1 pad_add_fusion.where
  13.1 0.5 copy-done.4
  13.8 9.8 %all-to-all-done = bf16[16,16,1152]{2,1,0:T(8,128)(2,1)S(1)} async-done(((bf16[16,16,1152]{2,1,0:T(8,128)(2,1)}), bf16[16,16,1152]{2,1,0:T(8,128)(2,1)S(1)}, u32[]{:S(2)}, u32[]{:S(2)}) %all-to-all-start) | async-done | bytes 589856 | tf_op jit(solution)/shard_map/all_to_all | solution.py:673
  23.6 1.5 %shard_map.221 = (f32[256,128]{1,0:T(8,128)S(1)}, f32[256,128]{1,0:T(8,128)S(1)}, bf16[32,24,128]{2,1,0:T(8,128)(2,1)S(1)}) custom-call(bf16[256,1152]{1,0:T(8,128)(2,1)S(1)} %bitcast.7, f32[4,256]{1,0:T(4,128)S(1)} %copy-done.2, f32[4,1024]{1,0:T(4,128)S(1)} %copy-done, f32[12]{0:T(128)S(1)} %pad_maximum_fusion.head, s32[3]{0:T(128)S(1)} %pad_add_fusion.where), custom_call_target="tpu_custom_call" | custom-call | tf_op jit(solution)/shard_map/pallas_call | solution.py:691
  25.2 23.4 %all_to_all.35.received = bf16[32,24,128]{2,1,0:T(8,128)(2,1)S(1)} all-to-all(bf16[32,24,128]{2,1,0:T(8,128)(2,1)S(1)} %get-tuple-element.48), channel_id=1, replica_groups=mesh['ctx'=32,'head'=16] {'ctx'}, dimensions={0} | all-to-all | bytes 393216 | tf_op jit(solution)/shard_map/all_to_all | solution.py:670
  48.5 1.9 %shard_map.222 = (bf16[32,24,128]{2,1,0:T(8,128)(2,1)}, f32[32,8,128]{2,1,0:T(8,128)S(1)}) custom-call(bf16[32,24,128]{2,1,0:T(8,128)(2,1)S(1)} %all_to_all.35.received, f32[4,256]{1,0:T(4,128)S(1)} %copy-done.2, f32[4,1024]{1,0:T(4,128)S(1)} %copy-done, s32[3]{0:T(128)S(1)} %pad_add_fusion.where), custom_call_target="tpu_custom_call" | custom-call | tf_op jit(solution)/shard_map/pallas_call | solution.py:698
  50.5 5.6 %all-to-all-start.2 = ((bf16[32,24,128]{2,1,0:T(8,128)(2,1)}), bf16[32,24,128]{2,1,0:T(8,128)(2,1)S(1)}, u32[]{:S(2)}, u32[]{:S(2)}) async-start(bf16[32,24,128]{2,1,0:T(8,128)(2,1)} %get-tuple-element.49), calls=%async_computation.2 | async-start | bytes 393216 | tf_op jit(solution)/shard_map/all_to_all | solution.py:670
  56.1 1.8 %shard_map.223 = (bf16[256,512]{1,0:T(8,128)(2,1)S(1)}, f32[256,256]{1,0:T(8,128)S(1)}) custom-call(bf16[256,1152]{1,0:T(8,128)(2,1)S(1)} %bitcast.8, f32[4,256]{1,0:T(4,128)S(1)} %copy-done.2, f32[4,1024]{1,0:T(4,128)S(1)} %copy-done, f32[4,1024]{1,0:T(4,128)S(1)} %copy-done.1, s32[3]{0:T(128)S(1)} %pad_add_fusion.where, ...), custom_call_target="tpu_custom_call" | custom-call | flops 100000000 | bytes 3000000 | tf_op jit(solution)/shard_map/pallas_call | solution.py:705
  57.9 9.7 %all-to-all-done.2.received = bf16[32,24,128]{2,1,0:T(8,128)(2,1)S(1)} async-done(((bf16[32,24,128]{2,1,0:T(8,128)(2,1)}), bf16[32,24,128]{2,1,0:T(8,128)(2,1)S(1)}, u32[]{:S(2)}, u32[]{:S(2)}) %all-to-all-start.2) | async-done | bytes 196640 | tf_op jit(solution)/shard_map/all_to_all | solution.py:670
  67.6 1.3 shard_map.224
  68.9 4.8 %psum.7.message = f32[8,256]{1,0:T(8,128)S(1)} all-reduce(f32[8,256]{1,0:T(8,128)S(1)} %get-tuple-element.55), channel_id=1, replica_groups={{0,1},{2,3},{4,5},{6,7},{8,9},{10,11},{12,13},{14,15},{16,17},{18,19},{..., use_global_device_ids=true, to_apply=%region_0.1 | all-reduce | flops 2048 | bytes 16384 | tf_op jit(solution)/shard_map/psum | solution.py:719
  73.7 1.4 shard_map.225
  75.0 14.8 %all_to_all.36.received = bf16[32,8,128]{2,1,0:T(8,128)(2,1)S(1)} all-to-all(bf16[32,8,128]{2,1,0:T(8,128)(2,1)S(1)} %get-tuple-element.58), channel_id=1, replica_groups=mesh['ctx'=32,'head'=16] {'ctx'}, dimensions={0} | all-to-all | bytes 131072 | tf_op jit(solution)/shard_map/all_to_all | solution.py:670
  89.8 0.7 shard_map.226
  90.5 3.9 %all-to-all-start.4 = ((bf16[32,8,128]{2,1,0:T(8,128)(2,1)}), bf16[32,8,128]{2,1,0:T(8,128)(2,1)S(1)}, u32[]{:S(2)}, u32[]{:S(2)}) async-start(bf16[32,8,128]{2,1,0:T(8,128)(2,1)} %shard_map.226), calls=%async_computation.4 | async-start | bytes 131072 | tf_op jit(solution)/shard_map/all_to_all | solution.py:670
  94.4 2.7 %shard_map.227 = (f32[256,512]{1,0:T(8,128)S(1)}, f32[264,128]{1,0:T(8,128)S(1)}, f32[256,512]{1,0:T(8,128)S(1)}) custom-call(bf16[256,1152]{1,0:T(8,128)(2,1)S(1)} %bitcast.11, f32[8,512]{1,0:T(8,128)S(1)} %get-tuple-element.59.rim, f32[4,256]{1,0:T(4,128)S(1)} %copy-done.2, f32[4,1024]{1,0:T(4,128)S(1)} %copy-done, f32[4,1024]{1,0:T(4,128)S(1)} %copy-done.1, ...), custom_call_target="tpu_custom_call" | custom-call | flops 300000000 | bytes 4000000 | tf_op jit(solution)/shard_map/pallas_call | solution.py:728
  97.0 8.4 %all-to-all-done.4 = bf16[32,8,128]{2,1,0:T(8,128)(2,1)S(1)} async-done(((bf16[32,8,128]{2,1,0:T(8,128)(2,1)}), bf16[32,8,128]{2,1,0:T(8,128)(2,1)S(1)}, u32[]{:S(2)}, u32[]{:S(2)}) %all-to-all-start.4) | async-done | bytes 65568 | tf_op jit(solution)/shard_map/all_to_all | solution.py:670
  105.4 1.7 %shard_map.228 = (f32[256,512]{1,0:T(8,128)S(1)}, f32[256,128]{1,0:T(8,128)S(1)}, bf16[32,32,128]{2,1,0:T(8,128)(2,1)S(1)}) custom-call(bf16[256,128]{1,0:T(8,128)(2,1)S(1)} %bitcast.13, bf16[256,1152]{1,0:T(8,128)(2,1)S(1)} %bitcast.12, f32[8,512]{1,0:T(8,128)S(1)} %get-tuple-element.59.rim, f32[12]{0:T(128)S(1)} %pad_maximum_fusion.head, ...), custom_call_target="tpu_custom_call" | custom-call | tf_op jit(solution)/shard_map/pallas_call | solution.py:740
  107.1 14.8 %all_to_all.37.received = bf16[32,32,128]{2,1,0:T(8,128)(2,1)S(1)} all-to-all(bf16[32,32,128]{2,1,0:T(8,128)(2,1)S(1)} %get-tuple-element.67), channel_id=1, replica_groups=mesh['ctx'=32,'head'=16] {'ctx'}, dimensions={0} | all-to-all | bytes 524288 | tf_op jit(solution)/shard_map/all_to_all | solution.py:670
  121.9 1.8 %shard_map.229 = (bf16[16,16,896]{2,1,0:T(8,128)(2,1)S(1)}, f32[4,256]{1,0:T(4,128)}, f32[4]{0:T(128)}, f32[4]{0:T(128)}, f32[4]{0:T(128)}) custom-call(bf16[32,32,128]{2,1,0:T(8,128)(2,1)S(1)} %all_to_all.37.received, s32[3]{0:T(128)S(1)} %pad_add_fusion.where, f32[4,256]{1,0:T(4,128)S(1)} %copy-done.2, f32[4,1024]{1,0:T(4,128)S(1)} %copy-done, ...), custom_call_target="tpu_custom_call" | custom-call | tf_op jit(solution)/shard_map/pallas_call | solution.py:750
  123.7 16.0 %all_to_all.38.received = bf16[16,16,896]{2,1,0:T(8,128)(2,1)S(1)} all-to-all(bf16[16,16,896]{2,1,0:T(8,128)(2,1)S(1)} %get-tuple-element.71), channel_id=1, replica_groups=mesh['ctx'=32,'head'=16] {'head'}, dimensions={0} | all-to-all | bytes 917504 | tf_op jit(solution)/shard_map/all_to_all | solution.py:673
  139.7 0.9 shard_map.230
  (14 shorter events, 0.1 us)
Async XLA Ops:
  2.7 20.9 %all-to-all-start = ((bf16[16,16,1152]{2,1,0:T(8,128)(2,1)}), bf16[16,16,1152]{2,1,0:T(8,128)(2,1)S(1)}, u32[]{:S(2)}, u32[]{:S(2)}) async-start(bf16[16,16,1152]{2,1,0:T(8,128)(2,1)} %shard_map.220), calls=%async_computation | async-start | bytes 1179648 | tf_op jit(solution)/shard_map/all_to_all | solution.py:673
  13.0 10.6 %copy-start = (f32[4,1024]{1,0:T(4,128)S(1)}, f32[4,1024]{1,0:T(4,128)}, u32[]{:S(2)}) copy-start(f32[4,1024]{1,0:T(4,128)} %wb.11) | copy-start | bytes 49156
  13.0 0.7 copy-start.4
  13.0 0.7 copy-start.5
  13.0 0.7 copy-start.6
  13.0 10.6 %copy-start.2 = (f32[4,256]{1,0:T(4,128)S(1)}, f32[4,256]{1,0:T(4,128)}, u32[]{:S(2)}) copy-start(f32[4,256]{1,0:T(4,128)} %wx.11) | copy-start | bytes 12292
  50.4 5.6 %copy-start.1 = (f32[4,1024]{1,0:T(4,128)S(1)}, f32[4,1024]{1,0:T(4,128)}, u32[]{:S(2)}) copy-start(f32[4,1024]{1,0:T(4,128)} %wc.7) | copy-start | bytes 49156
  50.5 17.1 %all-to-all-start.2 = ((bf16[32,24,128]{2,1,0:T(8,128)(2,1)}), bf16[32,24,128]{2,1,0:T(8,128)(2,1)S(1)}, u32[]{:S(2)}, u32[]{:S(2)}) async-start(bf16[32,24,128]{2,1,0:T(8,128)(2,1)} %get-tuple-element.49), calls=%async_computation.2 | async-start | bytes 393216 | tf_op jit(solution)/shard_map/all_to_all | solution.py:670
  56.1 11.5 %copy-start.3 = (f32[4096]{0:T(1024)S(1)}, f32[4096]{0:T(1024)}, u32[]{:S(2)}) copy-start(f32[4096]{0:T(1024)} %param.25) | copy-start | bytes 49156
  90.5 14.9 %all-to-all-start.4 = ((bf16[32,8,128]{2,1,0:T(8,128)(2,1)}), bf16[32,8,128]{2,1,0:T(8,128)(2,1)S(1)}, u32[]{:S(2)}, u32[]{:S(2)}) async-start(bf16[32,8,128]{2,1,0:T(8,128)(2,1)} %shard_map.226), calls=%async_computation.4 | async-start | bytes 131072 | tf_op jit(solution)/shard_map/all_to_all | solution.py:670

commit v6 on v5

--- a/solution.py
+++ b/solution.py
@@ -71,9 +71,9 @@
     return jnp.concatenate(halves, axis=1)
 
 
-def head_sums(wide):
+def head_sums(wide, count=3):
     pick = (iota((CW, 128), 0) // PS == iota((CW, 128), 1)).astype(BF)
-    return dot_parts(wide, pick, 1, 0, 3)
+    return dot_parts(wide, pick, 1, 0, count)
 
 
 def scalar_row(ref, first, width, per):
@@ -193,7 +193,7 @@
     gain_grad = jnp.sum(out_grad * normed, axis=0, keepdims=True)
     grown = spread(jnp.exp(cum))
     lifted = y_grad.astype(F32) * grown
-    start_grad = dot_parts(lifted, c_act, 0, 0, 2)
+    start_grad = dot(lifted.astype(BF), c_act, 0, 0)
     return y_grad, gate_grad, gain_grad, start_grad
 
 
@@ -227,7 +227,7 @@
     x32 = x_act.astype(F32)
     end_b = end_grad.astype(BF)
     x_state = spread(tail) * dot(b_act, end_b, 1, 1)
-    state_dots = head_sums(x32 * x_state)
+    state_dots = head_sums(x32 * x_state, 2)
     wide_step = spread(step)
     x_grad = wide_step * (x_in + x_state) + skip_row * y_grad.astype(F32)
     weighted = (x32 * spread(tail * step)).astype(BF)
@@ -241,7 +241,7 @@
         over = jnp.where(lane == e, jnp.sum(kept_dots[e * PS : (e + 1) * PS, :], axis=0, keepdims=True), over)
     final_grad = jnp.sum(pull, axis=0, keepdims=True) + jnp.exp(final) * over
     triu = (iota((T, T), 0) <= iota((T, T), 1)).astype(BF)
-    log_grad = sum(dot(triu, piece, 1, 0) for piece in pieces(cum_grad, 3)) + final_grad
+    log_grad = sum(dot(triu, piece, 1, 0) for piece in pieces(cum_grad, 2)) + final_grad
     step_grad = in_dots + state_dots - jnp.exp(alog_row) * log_grad
     alog_grad = jnp.sum(log_grad * logd, axis=0, keepdims=True)
     live = iota((T, 128), 1) < HD
@@ -288,27 +288,30 @@
     return jax.ShapeDtypeStruct(shape, dtype)
 
 
-def pack_kernel(x_at, b_at, c_at, dt_at, gate_at, grad_at, out, x, b, c, dt, gate, out_grad, sems):
+def pack_kernel(
+    x_at, b_at, c_at, dt_at, gate_at, grad_at, out_at, x, b, c, dt, gate, out_grad, out, sems, out_sems
+):
     moves = [
         pltpu.make_async_copy(source, target, sems.at[i])
         for i, (source, target) in enumerate(
-            [(x_at, x), (b_at, b), (c_at, c), (dt_at, dt), (gate_at, gate), (grad_at, out_grad)]
+            [(dt_at, dt), (x_at, x), (gate_at, gate), (grad_at, out_grad), (b_at, b), (c_at, c)]
         )
     ]
     for move in moves:
         move.start()
     ways = out.shape[0]
     per = GROUPS * N // ways
-    for move, ref, lo in ((moves[0], x, 0), (moves[4], gate, 512), (moves[5], out_grad, 768)):
-        move.wait()
-        for j in range(ways):
-            out[j, :, lo : lo + CW] = ref[:, j * CW : (j + 1) * CW]
-    for move, ref, lo in ((moves[1], b, 256), (moves[2], c, 384)):
-        move.wait()
-        for j in range(ways):
-            g = (j * per) // N
-            out[j, :, lo : lo + N] = ref[:, g * N : (g + 1) * N]
-    moves[3].wait()
+    leaving = []
+
+    def leave(lo, hi):
+        leaving.append(
+            pltpu.make_async_copy(
+                out.at[:, :, lo:hi], out_at.at[:, :, lo:hi], out_sems.at[len(leaving)]
+            )
+        )
+        leaving[-1].start()
+
+    moves[0].wait()
     wide_dt = jnp.concatenate(
         [dt[...].astype(F32), jnp.zeros((ROWS, 128 - dt.shape[1]), F32)], axis=1
     )
@@ -316,6 +319,19 @@
     for j in range(ways):
         turned = pltpu.roll(wide_dt, (128 - HD * j) % 128, 1)
         out[j, :, 1024:1152] = jnp.where(lane < HD, turned, 0.0).astype(BF)
+    for i, (ref, lo) in enumerate([(x, 0), (gate, 512), (out_grad, 768)]):
+        moves[i + 1].wait()
+        for j in range(ways):
+            out[j, :, lo : lo + CW] = ref[:, j * CW : (j + 1) * CW]
+        leave(lo, IN_W if lo == 768 else lo + CW)
+    for i, (ref, lo) in enumerate([(b, 256), (c, 384)]):
+        moves[i + 4].wait()
+        for j in range(ways):
+            g = (j * per) // N
+            out[j, :, lo : lo + N] = ref[:, g * N : (g + 1) * N]
+    leave(256, 512)
+    for move in leaving:
+        move.wait()
 
 
 def group_lanes(ref, where):
@@ -587,12 +603,12 @@
         send[i] = block
 
 
-def finish_kernel(received, where, wx, wb, wc, pre, dt_grad, gate_grad, send, conv_x_out, alog_out, bias_out, skip_out, ext):
+def finish_kernel(received, where, wx, wb, wc, pre, dt_grad, gate_grad, send, total_out, ext):
     count = received.shape[0]
     total = received[0].astype(F32)
     for i in range(1, count):
         total = total + received[i].astype(F32)
-    line = total[18:19] + total[19:20]
+    total_out[...] = total
     after = where[2] + 1
     next_block = received[jnp.minimum(after, count - 1)].astype(F32)
     following = jnp.concatenate(
@@ -603,11 +619,6 @@
     x_grad = conv_back(ext, wx[...], 0, 256).astype(BF)
     b_grad = conv_back(ext, group_lanes(wb, where), 256, 384).astype(BF)
     c_grad = conv_back(ext, group_lanes(wc, where), 384, 512).astype(BF)
-    conv_x_out[...] = jnp.concatenate([total[0:4], total[4:8]], axis=1)
-    for e in range(HD):
-        alog_out[e] = jnp.sum(line[:, e : e + 1])
-        bias_out[e] = jnp.sum(line[:, 32 + e : 33 + e])
-        skip_out[e] = jnp.sum(line[:, 64 + e : 65 + e])
     dt_low = dt_grad[...].astype(BF)
     lane, row = iota((128, 128), 1), iota((128, 128), 0)
     apart = dot(dt_low, ((lane // ROWS == row) & (row < HD)).astype(BF), 1, 0)
@@ -625,7 +636,16 @@
         send[j, :, 768:896] = jnp.where(row == 10, joined[j : j + 1], shared).astype(BF)
 
 
-def unpack_kernel(received, x_out, b_out, c_out, dt_out, gate_out, conv_b_out, conv_c_out, gain_out):
+def unpack_kernel(
+    received, total, x_out, b_out, c_out, dt_out, gate_out, conv_x_out, conv_b_out, conv_c_out,
+    alog_out, bias_out, skip_out, gain_out,
+):
+    line = total[18:19] + total[19:20]
+    conv_x_out[...] = jnp.concatenate([total[0:4], total[4:8]], axis=1)
+    for e in range(HD):
+        alog_out[e] = jnp.sum(line[:, e : e + 1])
+        bias_out[e] = jnp.sum(line[:, 32 + e : 33 + e])
+        skip_out[e] = jnp.sum(line[:, 64 + e : 65 + e])
     ways = received.shape[0]
     shared, lines = [], []
     for j in range(ways):
@@ -677,7 +697,10 @@
         pack_kernel,
         [sds((ways, ROWS, IN_W), BF)],
         "hhhhhh",
-        scratch=[pltpu.VMEM(a.shape, a.dtype) for a in inputs] + [pltpu.SemaphoreType.DMA((6,))],
+        "h",
+        scratch=[pltpu.VMEM(a.shape, a.dtype) for a in (x_in, b_in, c_in, dt_in, gate_in, out_grad)]
+        + [pltpu.VMEM((ways, ROWS, IN_W), BF)]
+        + [pltpu.SemaphoreType.DMA((6,)), pltpu.SemaphoreType.DMA((4,))],
         limit=PACK_LIMIT,
     )(*inputs)[0]
     arrived = head_swap(sent)
@@ -746,16 +769,15 @@
         end_grad, rows, rim, head, xbc, step, cum, y_grad, middle, dots, carried, gain_grad, slopes,
     )
     received = ctx_swap(send)
-    four = sds((HD,), F32)
-    send, conv_x_grad, alog_grad, bias_grad, skip_sum = call(
+    send, total = call(
         finish_kernel,
-        [sds((ways, ROWS, OUT_W), BF), sds((KT, CW), F32), four, four, four],
+        [sds((ways, ROWS, OUT_W), BF), sds((32, 128), F32)],
         "vsvvvvvv",
-        "vvsss",
         scratch=[pltpu.VMEM((T + 8, 512), F32)],
     )(received, where, conv_x, conv_b, conv_c, pre, dt_grad, gate_grad)
     received = head_swap(send)
-    x_grad, b_grad, c_grad, dt_out, gate_out, conv_b_grad, conv_c_grad, gain_sum = call(
+    four = sds((HD,), F32)
+    *grads, gain_sum = call(
         unpack_kernel,
         [
             sds(x_in.shape, BF),
@@ -763,26 +785,18 @@
             sds(c_in.shape, BF),
             sds(dt_in.shape, BF),
             sds(gate_in.shape, BF),
+            sds(conv_x.shape, F32),
             sds(conv_b.shape, F32),
             sds(conv_c.shape, F32),
+            four,
+            four,
+            four,
             sds((1, norm_gain.shape[0]), F32),
         ],
-        "v",
-    )(received)
-    return (
-        x_grad,
-        b_grad,
-        c_grad,
-        dt_out,
-        gate_out,
-        conv_x_grad,
-        conv_b_grad,
-        conv_c_grad,
-        alog_grad,
-        bias_grad,
-        skip_sum,
-        gain_sum.reshape(-1),
-    )
+        "vv",
+        "vvvvvvvvsssv",
+    )(received, total)
+    return (*grads, gain_sum.reshape(-1))
 
 
 def solution(mesh):

time: 142 us -> 141 us (level)
  no operation moved by 1% of the time
where the time goes in v6:
time: 141 us; the launch traced here: 140 us
  blocking collectives  73.8 us (52%)
  waiting for transfers between devices  27.9 us (20%)
  starting transfers between devices  19.7 us (14%)
  Pallas kernels  17 us (12%)
    all_to_all x3, blocking collectives, ctx_swap(): return lax.all_to_all(value, 'ctx', 0, 0, tiled=True)  52.9 us
    all_to_all x2, waiting for transfers between devices, ctx_swap(): return lax.all_to_all(value, 'ctx', 0, 0, tiled=True)  18.1 us
    all_to_all x1, blocking collectives, head_swap(): return lax.all_to_all(value, 'head', 0, 0, tiled=True)  16 us
    all_to_all x1, starting transfers between devices, head_swap(): return lax.all_to_all(value, 'head', 0, 0, tiled=True)  10.3 us
    all_to_all x1, waiting for transfers between devices, head_swap(): return lax.all_to_all(value, 'head', 0, 0, tiled=True)  9.85 us
    all_to_all x2, starting transfers between devices, ctx_swap(): return lax.all_to_all(value, 'ctx', 0, 0, tiled=True)  9.47 us
    psum x1, blocking collectives, per_device(): lax.psum(sums, 'head', axis_index_groups=[[g * per + i for i in range(per...  4.79 us
  transfers between devices with their start and end apart: 3, of which 3 were waited for; matrix products, arithmetic and copies ran while one was open for 0% of the time, Pallas kernels for 3%

profile of v6, /device:TPU:1, one launch (start us, length us, event | category | flops | bytes accessed | tf_op | source)
XLA Modules:
  0.0 139.9 jit_solution(13791559786976443983)
XLA Ops:
  0.6 1.9 %shard_map.220 = bf16[16,16,1152]{2,1,0:T(8,128)(2,1)} custom-call(bf16[16,4096]{1,0:T(8,128)(2,1)} %x_at.1, bf16[16,1024]{1,0:T(8,128)(2,1)} %b_at.1, bf16[16,1024]{1,0:T(8,128)(2,1)} %c_at.1, bf16[16,64]{1,0:T(8,128)(2,1)} %dt_at.1, bf16[16,4096]{1,0:T(8,128)(2,1)} %gate_at.1, bf16[16,4096]{1,0:T(8,128)(2,1)} %grad_at.1), custom_call_target="tpu_custom_call" | custom-call | tf_op jit(solution)/shard_map/pallas_call | solution.py:696
  2.6 10.3 %all-to-all-start = ((bf16[16,16,1152]{2,1,0:T(8,128)(2,1)}), bf16[16,16,1152]{2,1,0:T(8,128)(2,1)S(1)}, u32[]{:S(2)}, u32[]{:S(2)}) async-start(bf16[16,16,1152]{2,1,0:T(8,128)(2,1)} %shard_map.220), calls=%async_computation | async-start | bytes 1179648 | tf_op jit(solution)/shard_map/all_to_all | solution.py:693
  12.9 0.1 pad_add_fusion.where
  13.0 0.5 copy-done.4
  13.6 9.8 %all-to-all-done = bf16[16,16,1152]{2,1,0:T(8,128)(2,1)S(1)} async-done(((bf16[16,16,1152]{2,1,0:T(8,128)(2,1)}), bf16[16,16,1152]{2,1,0:T(8,128)(2,1)S(1)}, u32[]{:S(2)}, u32[]{:S(2)}) %all-to-all-start) | async-done | bytes 589856 | tf_op jit(solution)/shard_map/all_to_all | solution.py:693
  23.5 1.5 %shard_map.221 = (f32[256,128]{1,0:T(8,128)S(1)}, f32[256,128]{1,0:T(8,128)S(1)}, bf16[32,24,128]{2,1,0:T(8,128)(2,1)S(1)}) custom-call(bf16[256,1152]{1,0:T(8,128)(2,1)S(1)} %bitcast.7, f32[4,256]{1,0:T(4,128)S(1)} %copy-done.2, f32[4,1024]{1,0:T(4,128)S(1)} %copy-done, f32[12]{0:T(128)S(1)} %pad_maximum_fusion.head, s32[3]{0:T(128)S(1)} %pad_add_fusion.where), custom_call_target="tpu_custom_call" | custom-call | tf_op jit(solution)/shard_map/pallas_call | solution.py:714
  25.0 23.4 %all_to_all.35.received = bf16[32,24,128]{2,1,0:T(8,128)(2,1)S(1)} all-to-all(bf16[32,24,128]{2,1,0:T(8,128)(2,1)S(1)} %get-tuple-element.49), channel_id=1, replica_groups=mesh['ctx'=32,'head'=16] {'ctx'}, dimensions={0} | all-to-all | bytes 393216 | tf_op jit(solution)/shard_map/all_to_all | solution.py:690
  48.4 1.9 %shard_map.222 = (bf16[32,24,128]{2,1,0:T(8,128)(2,1)}, f32[32,8,128]{2,1,0:T(8,128)S(1)}) custom-call(bf16[32,24,128]{2,1,0:T(8,128)(2,1)S(1)} %all_to_all.35.received, f32[4,256]{1,0:T(4,128)S(1)} %copy-done.2, f32[4,1024]{1,0:T(4,128)S(1)} %copy-done, s32[3]{0:T(128)S(1)} %pad_add_fusion.where), custom_call_target="tpu_custom_call" | custom-call | tf_op jit(solution)/shard_map/pallas_call | solution.py:721
  50.3 5.6 %all-to-all-start.2 = ((bf16[32,24,128]{2,1,0:T(8,128)(2,1)}), bf16[32,24,128]{2,1,0:T(8,128)(2,1)S(1)}, u32[]{:S(2)}, u32[]{:S(2)}) async-start(bf16[32,24,128]{2,1,0:T(8,128)(2,1)} %get-tuple-element.50), calls=%async_computation.2 | async-start | bytes 393216 | tf_op jit(solution)/shard_map/all_to_all | solution.py:690
  55.9 1.8 %shard_map.223 = (bf16[256,512]{1,0:T(8,128)(2,1)S(1)}, f32[256,256]{1,0:T(8,128)S(1)}) custom-call(bf16[256,1152]{1,0:T(8,128)(2,1)S(1)} %bitcast.8, f32[4,256]{1,0:T(4,128)S(1)} %copy-done.2, f32[4,1024]{1,0:T(4,128)S(1)} %copy-done, f32[4,1024]{1,0:T(4,128)S(1)} %copy-done.1, s32[3]{0:T(128)S(1)} %pad_add_fusion.where, ...), custom_call_target="tpu_custom_call" | custom-call | flops 100000000 | bytes 3000000 | tf_op jit(solution)/shard_map/pallas_call | solution.py:728
  57.8 9.7 %all-to-all-done.2.received = bf16[32,24,128]{2,1,0:T(8,128)(2,1)S(1)} async-done(((bf16[32,24,128]{2,1,0:T(8,128)(2,1)}), bf16[32,24,128]{2,1,0:T(8,128)(2,1)S(1)}, u32[]{:S(2)}, u32[]{:S(2)}) %all-to-all-start.2) | async-done | bytes 196640 | tf_op jit(solution)/shard_map/all_to_all | solution.py:690
  67.4 1.3 shard_map.224
  68.7 4.8 %psum.7.message = f32[8,256]{1,0:T(8,128)S(1)} all-reduce(f32[8,256]{1,0:T(8,128)S(1)} %get-tuple-element.56), channel_id=1, replica_groups={{0,1},{2,3},{4,5},{6,7},{8,9},{10,11},{12,13},{14,15},{16,17},{18,19},{..., use_global_device_ids=true, to_apply=%region_0.1 | all-reduce | flops 2048 | bytes 16384 | tf_op jit(solution)/shard_map/psum | solution.py:742
  73.5 1.4 shard_map.225
  74.9 14.8 %all_to_all.36.received = bf16[32,8,128]{2,1,0:T(8,128)(2,1)S(1)} all-to-all(bf16[32,8,128]{2,1,0:T(8,128)(2,1)S(1)} %get-tuple-element.59), channel_id=1, replica_groups=mesh['ctx'=32,'head'=16] {'ctx'}, dimensions={0} | all-to-all | bytes 131072 | tf_op jit(solution)/shard_map/all_to_all | solution.py:690
  89.6 0.7 shard_map.226
  90.3 3.9 %all-to-all-start.4 = ((bf16[32,8,128]{2,1,0:T(8,128)(2,1)}), bf16[32,8,128]{2,1,0:T(8,128)(2,1)S(1)}, u32[]{:S(2)}, u32[]{:S(2)}) async-start(bf16[32,8,128]{2,1,0:T(8,128)(2,1)} %shard_map.226), calls=%async_computation.4 | async-start | bytes 131072 | tf_op jit(solution)/shard_map/all_to_all | solution.py:690
  94.2 2.7 %shard_map.227 = (f32[256,512]{1,0:T(8,128)S(1)}, f32[264,128]{1,0:T(8,128)S(1)}, f32[256,512]{1,0:T(8,128)S(1)}) custom-call(bf16[256,1152]{1,0:T(8,128)(2,1)S(1)} %bitcast.11, f32[8,512]{1,0:T(8,128)S(1)} %get-tuple-element.60.rim, f32[4,256]{1,0:T(4,128)S(1)} %copy-done.2, f32[4,1024]{1,0:T(4,128)S(1)} %copy-done, f32[4,1024]{1,0:T(4,128)S(1)} %copy-done.1, ...), custom_call_target="tpu_custom_call" | custom-call | flops 300000000 | bytes 4000000 | tf_op jit(solution)/shard_map/pallas_call | solution.py:751
  96.9 8.4 %all-to-all-done.4 = bf16[32,8,128]{2,1,0:T(8,128)(2,1)S(1)} async-done(((bf16[32,8,128]{2,1,0:T(8,128)(2,1)}), bf16[32,8,128]{2,1,0:T(8,128)(2,1)S(1)}, u32[]{:S(2)}, u32[]{:S(2)}) %all-to-all-start.4) | async-done | bytes 65568 | tf_op jit(solution)/shard_map/all_to_all | solution.py:690
  105.3 1.6 %shard_map.228 = (f32[256,512]{1,0:T(8,128)S(1)}, f32[256,128]{1,0:T(8,128)S(1)}, bf16[32,32,128]{2,1,0:T(8,128)(2,1)S(1)}) custom-call(bf16[256,128]{1,0:T(8,128)(2,1)S(1)} %bitcast.13, bf16[256,1152]{1,0:T(8,128)(2,1)S(1)} %bitcast.12, f32[8,512]{1,0:T(8,128)S(1)} %get-tuple-element.60.rim, f32[12]{0:T(128)S(1)} %pad_maximum_fusion.head, ...), custom_call_target="tpu_custom_call" | custom-call | tf_op jit(solution)/shard_map/pallas_call | solution.py:763
  106.9 14.8 %all_to_all.37.received = bf16[32,32,128]{2,1,0:T(8,128)(2,1)S(1)} all-to-all(bf16[32,32,128]{2,1,0:T(8,128)(2,1)S(1)} %get-tuple-element.68), channel_id=1, replica_groups=mesh['ctx'=32,'head'=16] {'ctx'}, dimensions={0} | all-to-all | bytes 524288 | tf_op jit(solution)/shard_map/all_to_all | solution.py:690
  121.7 1.2 shard_map.229
  122.9 16.0 %all_to_all.38.received = bf16[16,16,896]{2,1,0:T(8,128)(2,1)S(1)} all-to-all(bf16[16,16,896]{2,1,0:T(8,128)(2,1)S(1)} %get-tuple-element.72), channel_id=1, replica_groups=mesh['ctx'=32,'head'=16] {'head'}, dimensions={0} | all-to-all | bytes 917504 | tf_op jit(solution)/shard_map/all_to_all | solution.py:693
  139.0 0.9 shard_map.230
  (14 shorter events, 0.1 us)
Async XLA Ops:
  2.6 20.9 %all-to-all-start = ((bf16[16,16,1152]{2,1,0:T(8,128)(2,1)}), bf16[16,16,1152]{2,1,0:T(8,128)(2,1)S(1)}, u32[]{:S(2)}, u32[]{:S(2)}) async-start(bf16[16,16,1152]{2,1,0:T(8,128)(2,1)} %shard_map.220), calls=%async_computation | async-start | bytes 1179648 | tf_op jit(solution)/shard_map/all_to_all | solution.py:693
  12.8 10.6 %copy-start = (f32[4,1024]{1,0:T(4,128)S(1)}, f32[4,1024]{1,0:T(4,128)}, u32[]{:S(2)}) copy-start(f32[4,1024]{1,0:T(4,128)} %wb.11) | copy-start | bytes 49156
  12.8 0.7 copy-start.4
  12.8 0.7 copy-start.5
  12.9 0.7 copy-start.6
  12.9 10.6 %copy-start.2 = (f32[4,256]{1,0:T(4,128)S(1)}, f32[4,256]{1,0:T(4,128)}, u32[]{:S(2)}) copy-start(f32[4,256]{1,0:T(4,128)} %wx.11) | copy-start | bytes 12292
  50.3 5.6 %copy-start.1 = (f32[4,1024]{1,0:T(4,128)S(1)}, f32[4,1024]{1,0:T(4,128)}, u32[]{:S(2)}) copy-start(f32[4,1024]{1,0:T(4,128)} %wc.7) | copy-start | bytes 49156
  50.3 17.1 %all-to-all-start.2 = ((bf16[32,24,128]{2,1,0:T(8,128)(2,1)}), bf16[32,24,128]{2,1,0:T(8,128)(2,1)S(1)}, u32[]{:S(2)}, u32[]{:S(2)}) async-start(bf16[32,24,128]{2,1,0:T(8,128)(2,1)} %get-tuple-element.50), calls=%async_computation.2 | async-start | bytes 393216 | tf_op jit(solution)/shard_map/all_to_all | solution.py:690
  55.9 11.5 %copy-start.3 = (f32[4096]{0:T(1024)S(1)}, f32[4096]{0:T(1024)}, u32[]{:S(2)}) copy-start(f32[4096]{0:T(1024)} %param.25) | copy-start | bytes 49156
  90.3 14.9 %all-to-all-start.4 = ((bf16[32,8,128]{2,1,0:T(8,128)(2,1)}), bf16[32,8,128]{2,1,0:T(8,128)(2,1)S(1)}, u32[]{:S(2)}, u32[]{:S(2)}) async-start(bf16[32,8,128]{2,1,0:T(8,128)(2,1)} %shard_map.226), calls=%async_computation.4 | async-start | bytes 131072 | tf_op jit(solution)/shard_map/all_to_all | solution.py:690
